TPU v7x, 32 devices: a whole 2x2x4 slice. The times are simulated.
32 devices in a mesh: blk: 2 (over x), mblk: 16 (over z, y, core).
Axes of the slice: x: 2, y: 2, z: 4, core: 2. Of those that a mesh axis runs over, the one named last changes fastest.
Arguments:
- pixels: float32 [512, 1024], P(('blk', 'mblk')), may hold values from -6 to 6
- block_ids: int32 [512], P(('blk', 'mblk')), may hold values from 0 to 511, as said below
- block_mask: int32 [512], P(('blk', 'mblk')), may hold values 0 or 1
- model_cl: float32 [4096], replicated, may hold values from 0.5 to 1.5
Outputs:
- pseudo_cl: float32 [4096], replicated
- misfit: float32 [], replicated
Inputs may be any that keep to these rules, and one draw needn't show every extreme that they name: block_ids holds every block number once. The device at blk index s and mblk index j holds, for every blk index b, exactly 8 blocks of the cycles of the device at blk index b and mblk index j, where cycle r belongs to the device at blk index r // 32 and mblk index (r % 32) // 2.
All inputs are finite; a program needn't handle non-finite values. No bound on the sum of `block_mask` on one device may be relied on, other than what follows from the above.
Results may differ from a plain program's by a relative error of at most 0.0003.
Values sent between devices are 32-bit elements; how exact they have to be, the bound alone decides.
No kernel may reach another device: no remote copies, remote signals or barrier semaphores. Data moves between devices by JAX's collectives and lax.ppermute only.
A program may use at most 64 MiB of HBM per device.

v0:
```python
import math

import jax
import jax.numpy as jnp
from jax import lax
from jax.sharding import PartitionSpec as P

NSIDE = 2048
CYCLE_PIX = 8192
LMAX = 4096
BLOCK_PIX = 1024
SEGS = 8


def log_products(degree_count):
    counter = jnp.arange(1, degree_count, dtype=jnp.int32).astype(jnp.float32)
    return jnp.concatenate([jnp.zeros((1,), jnp.float32), jnp.cumsum(jnp.log1p(-0.5 / counter))])


def seeds_for(latitude, orders_f, log_prod):
    base_log = 0.5 * (jnp.log(2.0 * orders_f + 1.0) - math.log(4.0 * math.pi)) + 0.5 * log_prod
    return jnp.exp(
        base_log[None, :]
        + 0.5 * orders_f[None, :] * jnp.log1p(-latitude[:, None] * latitude[:, None])
    )


def coefficients(degree_f, orders_f):
    alpha_term = jnp.sqrt(
        (2.0 * degree_f - 1.0)
        * (2.0 * degree_f + 1.0)
        / jnp.maximum((degree_f - orders_f) * (degree_f + orders_f), 1.0)
    )
    beta_term = alpha_term * jnp.sqrt(
        jnp.maximum((degree_f - 1.0 - orders_f) * (degree_f - 1.0 + orders_f), 0.0)
        / jnp.maximum((2.0 * degree_f - 3.0) * (2.0 * degree_f - 1.0), 1.0)
    )
    return (alpha_term, beta_term)


def advance_rows(degree, orders, latitude, prev_one, prev_two, seed_rows):
    degree_f = degree.astype(jnp.float32)
    orders_f = orders.astype(jnp.float32)
    alpha_term, beta_term = coefficients(degree_f, orders_f)
    grown = alpha_term[:, None] * latitude[None, :] * prev_one - beta_term[:, None] * prev_two
    return jnp.where(
        degree > orders[:, None], grown, jnp.where(degree == orders[:, None], seed_rows, 0.0)
    )


def cycle_spectra(cycle_rows, cycle_index):
    cycle_count, cycle_len = cycle_rows.shape
    inner_len = min(128, cycle_len)
    outer_len = cycle_len // inner_len
    kept_orders = cycle_len // 2
    upper_len = kept_orders // outer_len
    highest = lax.Precision.HIGHEST
    folded = cycle_rows.reshape(cycle_count, outer_len, inner_len)
    outer_idx = jnp.arange(outer_len, dtype=jnp.int32)
    inner_idx = jnp.arange(inner_len, dtype=jnp.int32)
    upper_idx = jnp.arange(upper_len, dtype=jnp.int32)
    angle_one = (outer_idx[:, None] * outer_idx[None, :] % outer_len).astype(jnp.float32) * (
        2.0 * math.pi / outer_len
    )
    section_re = jnp.einsum("rap,ak->rkp", folded, jnp.cos(angle_one), precision=highest)
    section_im = -jnp.einsum("rap,ak->rkp", folded, jnp.sin(angle_one), precision=highest)
    twist = (outer_idx[:, None] * inner_idx[None, :] % cycle_len).astype(jnp.float32) * (
        2.0 * math.pi / cycle_len
    )
    twist_cos = jnp.cos(twist)[None]
    twist_sin = jnp.sin(twist)[None]
    turned_re = section_re * twist_cos + section_im * twist_sin
    turned_im = section_im * twist_cos - section_re * twist_sin
    angle_two = (inner_idx[:, None] * upper_idx[None, :] % inner_len).astype(jnp.float32) * (
        2.0 * math.pi / inner_len
    )
    cos_two = jnp.cos(angle_two)
    sin_two = jnp.sin(angle_two)
    out_re = jnp.einsum("rkp,pq->rkq", turned_re, cos_two, precision=highest) + jnp.einsum(
        "rkp,pq->rkq", turned_im, sin_two, precision=highest
    )
    out_im = jnp.einsum("rkp,pq->rkq", turned_im, cos_two, precision=highest) - jnp.einsum(
        "rkp,pq->rkq", turned_re, sin_two, precision=highest
    )
    out_re = jnp.transpose(out_re, (0, 2, 1)).reshape(cycle_count, kept_orders)
    out_im = jnp.transpose(out_im, (0, 2, 1)).reshape(cycle_count, kept_orders)
    orders_f = jnp.arange(kept_orders, dtype=jnp.int32).astype(jnp.float32)
    half_shift = jnp.where(cycle_index % 2 == 0, 0.5, 0.0).astype(jnp.float32)
    phase_angle = half_shift[:, None] * orders_f[None, :] * (2.0 * math.pi / cycle_len)
    phase_cos = jnp.cos(phase_angle)
    phase_sin = jnp.sin(phase_angle)
    spec_re = out_re * phase_cos + out_im * phase_sin
    spec_im = out_im * phase_cos - out_re * phase_sin
    return jnp.stack([spec_re, spec_im])


def recurrence(spectra, latitude, chosen, log_prod, block_len, norm_scale):
    degree_count = log_prod.shape[0]
    group_size = chosen.shape[0]
    spec_rows = jnp.transpose(spectra, (0, 2, 1))
    seed_rows = jnp.transpose(seeds_for(latitude, chosen.astype(jnp.float32), log_prod[chosen]))
    first_block = jnp.min(chosen) // block_len
    zero_state = jnp.zeros((group_size, latitude.shape[0]), jnp.float32)

    def one_block(block_idx, carried):
        prev_one, prev_two, result = carried
        base_degree = block_idx * block_len

        def sixteen_rows(part_idx, inner_state):
            state_one, state_two, buffer = inner_state
            row_list = []
            for offset in range(16):
                degree = base_degree + part_idx * 16 + offset
                fresh_row = advance_rows(degree, chosen, latitude, state_one, state_two, seed_rows)
                state_two = state_one
                state_one = fresh_row
                row_list.append(
                    jnp.stack(
                        [
                            jnp.sum(fresh_row * spec_rows[0], axis=1),
                            jnp.sum(fresh_row * spec_rows[1], axis=1),
                        ]
                    )
                )
            stacked = jnp.stack(row_list, axis=1)
            return (
                state_one,
                state_two,
                lax.dynamic_update_slice_in_dim(buffer, stacked, part_idx * 16, 1),
            )

        empty_buffer = jnp.zeros((2, block_len, group_size), jnp.float32)
        prev_one, prev_two, buffer = lax.fori_loop(
            0, block_len // 16, sixteen_rows, (prev_one, prev_two, empty_buffer)
        )
        placed = jnp.transpose(buffer * norm_scale, (2, 0, 1))
        return (prev_one, prev_two, lax.dynamic_update_slice_in_dim(result, placed, base_degree, 2))

    empty_result = jnp.zeros((group_size, 2, degree_count), jnp.float32)
    return lax.fori_loop(
        first_block, degree_count // block_len, one_block, (zero_state, zero_state, empty_result)
    )[2]


def legendre(band_rows, latitude, orders, log_prod, start_row, row_total, group_size, norm_scale):
    degree_count = log_prod.shape[0]
    block_len = min(256, degree_count)

    def one_group(group_idx, result):
        offset = start_row + group_idx * group_size
        spectra = lax.dynamic_slice_in_dim(band_rows, offset, group_size, 2)
        chosen = lax.dynamic_slice_in_dim(orders, offset, group_size, 0)
        group_rows = recurrence(spectra, latitude, chosen, log_prod, block_len, norm_scale)
        return lax.dynamic_update_slice_in_dim(result, group_rows, group_idx * group_size, 0)

    return lax.fori_loop(
        0, row_total // group_size, one_group, jnp.zeros((row_total, 2, degree_count), jnp.float32)
    )


def arrange(spectra, groups):
    spec_pair, cycle_count, order_count = spectra.shape
    return spectra.reshape(spec_pair, cycle_count, groups, order_count // groups)


def owned_orders(group_idx, groups, order_count):
    per_group = order_count // groups
    return group_idx * per_group + jnp.arange(per_group, dtype=jnp.int32)


def power_part(alm_rows, chosen):
    weights = jnp.where(chosen == 0, 1.0, 2.0).astype(jnp.float32)
    return jnp.sum(
        weights[:, None] * (alm_rows[:, 0] * alm_rows[:, 0] + alm_rows[:, 1] * alm_rows[:, 1]),
        axis=0,
    )


def latitudes(cycle_idx, cycles_all):
    return (cycles_all // 2 - cycle_idx).astype(jnp.float32) * (2.0 / (3.0 * NSIDE))


def on_device(pixels, block_ids, block_mask, model_cl):
    n_blk = lax.axis_size("blk")
    n_mblk = lax.axis_size("mblk")
    blk_idx = lax.axis_index("blk")
    mblk_idx = lax.axis_index("mblk")
    slots = pixels.shape[0]
    cap_band = slots // n_blk
    cycle_dev = slots // SEGS
    r_band = cycle_dev * n_mblk
    cycles_all = r_band * n_blk
    norm_scale = math.sqrt(4.0 * math.pi / (cycles_all * CYCLE_PIX))
    kept_pixels = pixels * block_mask[:, None].astype(jnp.float32)
    band_of = block_ids // SEGS // r_band
    sorting = jnp.argsort(band_of * slots + jnp.arange(slots, dtype=jnp.int32))
    outgoing = kept_pixels[sorting].reshape(n_blk, cap_band, BLOCK_PIX)
    outgoing_ids = block_ids[sorting].reshape(n_blk, cap_band)
    got_blocks, got_ids = (
        lax.all_to_all(outgoing, "blk", split_axis=0, concat_axis=0, tiled=True),
        lax.all_to_all(outgoing_ids, "blk", split_axis=0, concat_axis=0, tiled=True),
    )
    owner = blk_idx * n_mblk + mblk_idx
    slot_pos = got_ids.reshape(-1) - owner * slots
    cycle_rows = (
        jnp.zeros((slots, BLOCK_PIX), jnp.float32)
        .at[slot_pos]
        .set(got_blocks.reshape(slots, BLOCK_PIX))
    )
    cycle_rows = cycle_rows.reshape(cycle_dev, CYCLE_PIX)
    cycle_index = owner * cycle_dev + jnp.arange(cycle_dev, dtype=jnp.int32)
    spectra = cycle_spectra(cycle_rows, cycle_index)
    log_prod = log_products(LMAX)
    sent = arrange(spectra, n_mblk)
    got_rows = lax.all_to_all(sent, "mblk", split_axis=2, concat_axis=1, tiled=True)
    band_rows = got_rows.reshape(2, r_band, -1)
    latitude = latitudes(blk_idx * r_band + jnp.arange(r_band, dtype=jnp.int32), cycles_all)
    orders = owned_orders(mblk_idx, n_mblk, LMAX)
    per_dev = orders.shape[0]
    row_count = per_dev // n_blk
    group_size = math.gcd(row_count, per_dev // 2)
    partial_alm = legendre(
        band_rows, latitude, orders, log_prod, 0, per_dev, group_size, norm_scale
    )
    alm_rows = lax.psum(partial_alm, "blk")
    power_sum = lax.psum(power_part(alm_rows, orders), "mblk")
    degrees_f = jnp.arange(LMAX, dtype=jnp.int32).astype(jnp.float32)
    pseudo_cl = power_sum / (2.0 * degrees_f + 1.0)
    rel_error = (pseudo_cl - model_cl) / model_cl
    misfit = jnp.mean(rel_error * rel_error)
    return (pseudo_cl, misfit)


def solution(mesh):
    in_specs = (P(("blk", "mblk"), None), P(("blk", "mblk")), P(("blk", "mblk")), P())
    out_specs = (P(), P())
    return jax.shard_map(
        on_device, mesh=mesh, in_specs=in_specs, out_specs=out_specs, check_vma=False
    )
```

profile of v0, /device:TPU:0, one launch (start us, length us, event | category | flops | bytes accessed | tf_op | source)
XLA Modules:
  0.0 1875.1 jit_solution(16293405366613098013)
XLA Ops:
  11.1 4.2 all-to-all-start
  19.0 3.3 all-to-all-start.1
  22.4 4.0 all-to-all-done.1
  30.4 6.4 all-to-all-start.2
  36.9 6.8 all-to-all-done.2
  43.7 5.5 broadcast_in_dim.916
  49.2 1550.9 %while.94 = (s32[]{:T(128)}, f32[256,2,4096]{0,1,2:T(2,128)}, s32[256]{0:T(256)S(1)}, f32[4096]{0:T(1024)S(1)}, f32[2,32,256]{2,0,1:T(2,128)S(1)}, /*index=5*/s3...) while((s32[]{:T(128)}, f32[256,2,4096]{0,1,2:T(2,128)}, ...), condition=%wide.region_42.43_spmd.clone.clone, body=%wide.region_4.42_spmd.clone.clone.sunk | while | flops 758783 | bytes 14412863 | solution.py:156
  54.1 2.9 broadcast.2978
  57.0 762.9 %while.95 = (s32[]{:T(128)}, f32[128,32]{1,0:T(8,128)S(1)}, f32[128,32]{1,0:T(8,128)S(1)}, f32[128,2,4096]{0,1,2:T(2,128)}, s32[128]{0:T(128)S(1)}, /*index=5*/f...) while((s32[]{:T(128)}, f32[128,32]{1,0:T(8,128)S(1)}, ...), condition=%wide.region_41.41_spmd.clone, body=%wide.region_6.40_spmd.clone.sunk | while | flops 755883 | bytes 1654218 | solution.py:140
  57.2 46.6 %while.96 = (s32[]{:T(128)}, f32[128,32]{1,0:T(8,128)S(1)}, f32[128,32]{1,0:T(8,128)S(1)}, f32[2,256,128]{2,0,1:T(2,128)S(1)}, s32[]{:T(128)}, /*index=5*/s32[12...) while((s32[]{:T(128)}, f32[128,32]{1,0:T(8,128)S(1)}, ...), condition=%wide.region_40.39_spmd, body=%wide.region_7.38_spmd.sunk | while | flops 682149 | bytes 849607 | solution.py:133
  104.9 46.6 %while.96 = (s32[]{:T(128)}, f32[128,32]{1,0:T(8,128)S(1)}, f32[128,32]{1,0:T(8,128)S(1)}, f32[2,256,128]{2,0,1:T(2,128)S(1)}, s32[]{:T(128)}, /*index=5*/s32[12...) while((s32[]{:T(128)}, f32[128,32]{1,0:T(8,128)S(1)}, ...), condition=%wide.region_40.39_spmd, body=%wide.region_7.38_spmd.sunk | while | flops 682149 | bytes 849607 | solution.py:133
  152.6 46.6 %while.96 = (s32[]{:T(128)}, f32[128,32]{1,0:T(8,128)S(1)}, f32[128,32]{1,0:T(8,128)S(1)}, f32[2,256,128]{2,0,1:T(2,128)S(1)}, s32[]{:T(128)}, /*index=5*/s32[12...) while((s32[]{:T(128)}, f32[128,32]{1,0:T(8,128)S(1)}, ...), condition=%wide.region_40.39_spmd, body=%wide.region_7.38_spmd.sunk | while | flops 682149 | bytes 849607 | solution.py:133
  200.2 46.6 %while.96 = (s32[]{:T(128)}, f32[128,32]{1,0:T(8,128)S(1)}, f32[128,32]{1,0:T(8,128)S(1)}, f32[2,256,128]{2,0,1:T(2,128)S(1)}, s32[]{:T(128)}, /*index=5*/s32[12...) while((s32[]{:T(128)}, f32[128,32]{1,0:T(8,128)S(1)}, ...), condition=%wide.region_40.39_spmd, body=%wide.region_7.38_spmd.sunk | while | flops 682149 | bytes 849607 | solution.py:133
  247.9 46.6 %while.96 = (s32[]{:T(128)}, f32[128,32]{1,0:T(8,128)S(1)}, f32[128,32]{1,0:T(8,128)S(1)}, f32[2,256,128]{2,0,1:T(2,128)S(1)}, s32[]{:T(128)}, /*index=5*/s32[12...) while((s32[]{:T(128)}, f32[128,32]{1,0:T(8,128)S(1)}, ...), condition=%wide.region_40.39_spmd, body=%wide.region_7.38_spmd.sunk | while | flops 682149 | bytes 849607 | solution.py:133
  295.6 46.6 %while.96 = (s32[]{:T(128)}, f32[128,32]{1,0:T(8,128)S(1)}, f32[128,32]{1,0:T(8,128)S(1)}, f32[2,256,128]{2,0,1:T(2,128)S(1)}, s32[]{:T(128)}, /*index=5*/s32[12...) while((s32[]{:T(128)}, f32[128,32]{1,0:T(8,128)S(1)}, ...), condition=%wide.region_40.39_spmd, body=%wide.region_7.38_spmd.sunk | while | flops 682149 | bytes 849607 | solution.py:133
  343.3 46.6 %while.96 = (s32[]{:T(128)}, f32[128,32]{1,0:T(8,128)S(1)}, f32[128,32]{1,0:T(8,128)S(1)}, f32[2,256,128]{2,0,1:T(2,128)S(1)}, s32[]{:T(128)}, /*index=5*/s32[12...) while((s32[]{:T(128)}, f32[128,32]{1,0:T(8,128)S(1)}, ...), condition=%wide.region_40.39_spmd, body=%wide.region_7.38_spmd.sunk | while | flops 682149 | bytes 849607 | solution.py:133
  390.9 46.6 %while.96 = (s32[]{:T(128)}, f32[128,32]{1,0:T(8,128)S(1)}, f32[128,32]{1,0:T(8,128)S(1)}, f32[2,256,128]{2,0,1:T(2,128)S(1)}, s32[]{:T(128)}, /*index=5*/s32[12...) while((s32[]{:T(128)}, f32[128,32]{1,0:T(8,128)S(1)}, ...), condition=%wide.region_40.39_spmd, body=%wide.region_7.38_spmd.sunk | while | flops 682149 | bytes 849607 | solution.py:133
  438.6 46.6 %while.96 = (s32[]{:T(128)}, f32[128,32]{1,0:T(8,128)S(1)}, f32[128,32]{1,0:T(8,128)S(1)}, f32[2,256,128]{2,0,1:T(2,128)S(1)}, s32[]{:T(128)}, /*index=5*/s32[12...) while((s32[]{:T(128)}, f32[128,32]{1,0:T(8,128)S(1)}, ...), condition=%wide.region_40.39_spmd, body=%wide.region_7.38_spmd.sunk | while | flops 682149 | bytes 849607 | solution.py:133
  486.3 46.6 %while.96 = (s32[]{:T(128)}, f32[128,32]{1,0:T(8,128)S(1)}, f32[128,32]{1,0:T(8,128)S(1)}, f32[2,256,128]{2,0,1:T(2,128)S(1)}, s32[]{:T(128)}, /*index=5*/s32[12...) while((s32[]{:T(128)}, f32[128,32]{1,0:T(8,128)S(1)}, ...), condition=%wide.region_40.39_spmd, body=%wide.region_7.38_spmd.sunk | while | flops 682149 | bytes 849607 | solution.py:133
  534.0 46.6 %while.96 = (s32[]{:T(128)}, f32[128,32]{1,0:T(8,128)S(1)}, f32[128,32]{1,0:T(8,128)S(1)}, f32[2,256,128]{2,0,1:T(2,128)S(1)}, s32[]{:T(128)}, /*index=5*/s32[12...) while((s32[]{:T(128)}, f32[128,32]{1,0:T(8,128)S(1)}, ...), condition=%wide.region_40.39_spmd, body=%wide.region_7.38_spmd.sunk | while | flops 682149 | bytes 849607 | solution.py:133
  581.7 46.6 %while.96 = (s32[]{:T(128)}, f32[128,32]{1,0:T(8,128)S(1)}, f32[128,32]{1,0:T(8,128)S(1)}, f32[2,256,128]{2,0,1:T(2,128)S(1)}, s32[]{:T(128)}, /*index=5*/s32[12...) while((s32[]{:T(128)}, f32[128,32]{1,0:T(8,128)S(1)}, ...), condition=%wide.region_40.39_spmd, body=%wide.region_7.38_spmd.sunk | while | flops 682149 | bytes 849607 | solution.py:133
  629.4 46.6 %while.96 = (s32[]{:T(128)}, f32[128,32]{1,0:T(8,128)S(1)}, f32[128,32]{1,0:T(8,128)S(1)}, f32[2,256,128]{2,0,1:T(2,128)S(1)}, s32[]{:T(128)}, /*index=5*/s32[12...) while((s32[]{:T(128)}, f32[128,32]{1,0:T(8,128)S(1)}, ...), condition=%wide.region_40.39_spmd, body=%wide.region_7.38_spmd.sunk | while | flops 682149 | bytes 849607 | solution.py:133
  677.0 46.6 %while.96 = (s32[]{:T(128)}, f32[128,32]{1,0:T(8,128)S(1)}, f32[128,32]{1,0:T(8,128)S(1)}, f32[2,256,128]{2,0,1:T(2,128)S(1)}, s32[]{:T(128)}, /*index=5*/s32[12...) while((s32[]{:T(128)}, f32[128,32]{1,0:T(8,128)S(1)}, ...), condition=%wide.region_40.39_spmd, body=%wide.region_7.38_spmd.sunk | while | flops 682149 | bytes 849607 | solution.py:133
  724.7 46.6 %while.96 = (s32[]{:T(128)}, f32[128,32]{1,0:T(8,128)S(1)}, f32[128,32]{1,0:T(8,128)S(1)}, f32[2,256,128]{2,0,1:T(2,128)S(1)}, s32[]{:T(128)}, /*index=5*/s32[12...) while((s32[]{:T(128)}, f32[128,32]{1,0:T(8,128)S(1)}, ...), condition=%wide.region_40.39_spmd, body=%wide.region_7.38_spmd.sunk | while | flops 682149 | bytes 849607 | solution.py:133
  772.4 46.6 %while.96 = (s32[]{:T(128)}, f32[128,32]{1,0:T(8,128)S(1)}, f32[128,32]{1,0:T(8,128)S(1)}, f32[2,256,128]{2,0,1:T(2,128)S(1)}, s32[]{:T(128)}, /*index=5*/s32[12...) while((s32[]{:T(128)}, f32[128,32]{1,0:T(8,128)S(1)}, ...), condition=%wide.region_40.39_spmd, body=%wide.region_7.38_spmd.sunk | while | flops 682149 | bytes 849607 | solution.py:133
  819.9 4.8 constant_dynamic-update-slice_fusion.36
  829.6 2.9 broadcast.2978
  832.5 762.9 %while.95 = (s32[]{:T(128)}, f32[128,32]{1,0:T(8,128)S(1)}, f32[128,32]{1,0:T(8,128)S(1)}, f32[128,2,4096]{0,1,2:T(2,128)}, s32[128]{0:T(128)S(1)}, /*index=5*/f...) while((s32[]{:T(128)}, f32[128,32]{1,0:T(8,128)S(1)}, ...), condition=%wide.region_41.41_spmd.clone, body=%wide.region_6.40_spmd.clone.sunk | while | flops 755883 | bytes 1654218 | solution.py:140
  832.7 46.6 %while.96 = (s32[]{:T(128)}, f32[128,32]{1,0:T(8,128)S(1)}, f32[128,32]{1,0:T(8,128)S(1)}, f32[2,256,128]{2,0,1:T(2,128)S(1)}, s32[]{:T(128)}, /*index=5*/s32[12...) while((s32[]{:T(128)}, f32[128,32]{1,0:T(8,128)S(1)}, ...), condition=%wide.region_40.39_spmd, body=%wide.region_7.38_spmd.sunk | while | flops 682149 | bytes 849607 | solution.py:133
  880.3 46.6 %while.96 = (s32[]{:T(128)}, f32[128,32]{1,0:T(8,128)S(1)}, f32[128,32]{1,0:T(8,128)S(1)}, f32[2,256,128]{2,0,1:T(2,128)S(1)}, s32[]{:T(128)}, /*index=5*/s32[12...) while((s32[]{:T(128)}, f32[128,32]{1,0:T(8,128)S(1)}, ...), condition=%wide.region_40.39_spmd, body=%wide.region_7.38_spmd.sunk | while | flops 682149 | bytes 849607 | solution.py:133
  928.0 46.6 %while.96 = (s32[]{:T(128)}, f32[128,32]{1,0:T(8,128)S(1)}, f32[128,32]{1,0:T(8,128)S(1)}, f32[2,256,128]{2,0,1:T(2,128)S(1)}, s32[]{:T(128)}, /*index=5*/s32[12...) while((s32[]{:T(128)}, f32[128,32]{1,0:T(8,128)S(1)}, ...), condition=%wide.region_40.39_spmd, body=%wide.region_7.38_spmd.sunk | while | flops 682149 | bytes 849607 | solution.py:133
  975.7 46.6 %while.96 = (s32[]{:T(128)}, f32[128,32]{1,0:T(8,128)S(1)}, f32[128,32]{1,0:T(8,128)S(1)}, f32[2,256,128]{2,0,1:T(2,128)S(1)}, s32[]{:T(128)}, /*index=5*/s32[12...) while((s32[]{:T(128)}, f32[128,32]{1,0:T(8,128)S(1)}, ...), condition=%wide.region_40.39_spmd, body=%wide.region_7.38_spmd.sunk | while | flops 682149 | bytes 849607 | solution.py:133
  1023.4 46.6 %while.96 = (s32[]{:T(128)}, f32[128,32]{1,0:T(8,128)S(1)}, f32[128,32]{1,0:T(8,128)S(1)}, f32[2,256,128]{2,0,1:T(2,128)S(1)}, s32[]{:T(128)}, /*index=5*/s32[12...) while((s32[]{:T(128)}, f32[128,32]{1,0:T(8,128)S(1)}, ...), condition=%wide.region_40.39_spmd, body=%wide.region_7.38_spmd.sunk | while | flops 682149 | bytes 849607 | solution.py:133
  1071.0 46.6 %while.96 = (s32[]{:T(128)}, f32[128,32]{1,0:T(8,128)S(1)}, f32[128,32]{1,0:T(8,128)S(1)}, f32[2,256,128]{2,0,1:T(2,128)S(1)}, s32[]{:T(128)}, /*index=5*/s32[12...) while((s32[]{:T(128)}, f32[128,32]{1,0:T(8,128)S(1)}, ...), condition=%wide.region_40.39_spmd, body=%wide.region_7.38_spmd.sunk | while | flops 682149 | bytes 849607 | solution.py:133
  1118.7 46.6 %while.96 = (s32[]{:T(128)}, f32[128,32]{1,0:T(8,128)S(1)}, f32[128,32]{1,0:T(8,128)S(1)}, f32[2,256,128]{2,0,1:T(2,128)S(1)}, s32[]{:T(128)}, /*index=5*/s32[12...) while((s32[]{:T(128)}, f32[128,32]{1,0:T(8,128)S(1)}, ...), condition=%wide.region_40.39_spmd, body=%wide.region_7.38_spmd.sunk | while | flops 682149 | bytes 849607 | solution.py:133
  1166.4 46.6 %while.96 = (s32[]{:T(128)}, f32[128,32]{1,0:T(8,128)S(1)}, f32[128,32]{1,0:T(8,128)S(1)}, f32[2,256,128]{2,0,1:T(2,128)S(1)}, s32[]{:T(128)}, /*index=5*/s32[12...) while((s32[]{:T(128)}, f32[128,32]{1,0:T(8,128)S(1)}, ...), condition=%wide.region_40.39_spmd, body=%wide.region_7.38_spmd.sunk | while | flops 682149 | bytes 849607 | solution.py:133
  1214.1 46.6 %while.96 = (s32[]{:T(128)}, f32[128,32]{1,0:T(8,128)S(1)}, f32[128,32]{1,0:T(8,128)S(1)}, f32[2,256,128]{2,0,1:T(2,128)S(1)}, s32[]{:T(128)}, /*index=5*/s32[12...) while((s32[]{:T(128)}, f32[128,32]{1,0:T(8,128)S(1)}, ...), condition=%wide.region_40.39_spmd, body=%wide.region_7.38_spmd.sunk | while | flops 682149 | bytes 849607 | solution.py:133
  1261.8 46.6 %while.96 = (s32[]{:T(128)}, f32[128,32]{1,0:T(8,128)S(1)}, f32[128,32]{1,0:T(8,128)S(1)}, f32[2,256,128]{2,0,1:T(2,128)S(1)}, s32[]{:T(128)}, /*index=5*/s32[12...) while((s32[]{:T(128)}, f32[128,32]{1,0:T(8,128)S(1)}, ...), condition=%wide.region_40.39_spmd, body=%wide.region_7.38_spmd.sunk | while | flops 682149 | bytes 849607 | solution.py:133
  1309.4 46.6 %while.96 = (s32[]{:T(128)}, f32[128,32]{1,0:T(8,128)S(1)}, f32[128,32]{1,0:T(8,128)S(1)}, f32[2,256,128]{2,0,1:T(2,128)S(1)}, s32[]{:T(128)}, /*index=5*/s32[12...) while((s32[]{:T(128)}, f32[128,32]{1,0:T(8,128)S(1)}, ...), condition=%wide.region_40.39_spmd, body=%wide.region_7.38_spmd.sunk | while | flops 682149 | bytes 849607 | solution.py:133
  1357.1 46.6 %while.96 = (s32[]{:T(128)}, f32[128,32]{1,0:T(8,128)S(1)}, f32[128,32]{1,0:T(8,128)S(1)}, f32[2,256,128]{2,0,1:T(2,128)S(1)}, s32[]{:T(128)}, /*index=5*/s32[12...) while((s32[]{:T(128)}, f32[128,32]{1,0:T(8,128)S(1)}, ...), condition=%wide.region_40.39_spmd, body=%wide.region_7.38_spmd.sunk | while | flops 682149 | bytes 849607 | solution.py:133
  1404.8 46.6 %while.96 = (s32[]{:T(128)}, f32[128,32]{1,0:T(8,128)S(1)}, f32[128,32]{1,0:T(8,128)S(1)}, f32[2,256,128]{2,0,1:T(2,128)S(1)}, s32[]{:T(128)}, /*index=5*/s32[12...) while((s32[]{:T(128)}, f32[128,32]{1,0:T(8,128)S(1)}, ...), condition=%wide.region_40.39_spmd, body=%wide.region_7.38_spmd.sunk | while | flops 682149 | bytes 849607 | solution.py:133
  1452.5 46.6 %while.96 = (s32[]{:T(128)}, f32[128,32]{1,0:T(8,128)S(1)}, f32[128,32]{1,0:T(8,128)S(1)}, f32[2,256,128]{2,0,1:T(2,128)S(1)}, s32[]{:T(128)}, /*index=5*/s32[12...) while((s32[]{:T(128)}, f32[128,32]{1,0:T(8,128)S(1)}, ...), condition=%wide.region_40.39_spmd, body=%wide.region_7.38_spmd.sunk | while | flops 682149 | bytes 849607 | solution.py:133
  1500.2 46.6 %while.96 = (s32[]{:T(128)}, f32[128,32]{1,0:T(8,128)S(1)}, f32[128,32]{1,0:T(8,128)S(1)}, f32[2,256,128]{2,0,1:T(2,128)S(1)}, s32[]{:T(128)}, /*index=5*/s32[12...) while((s32[]{:T(128)}, f32[128,32]{1,0:T(8,128)S(1)}, ...), condition=%wide.region_40.39_spmd, body=%wide.region_7.38_spmd.sunk | while | flops 682149 | bytes 849607 | solution.py:133
  1547.8 46.6 %while.96 = (s32[]{:T(128)}, f32[128,32]{1,0:T(8,128)S(1)}, f32[128,32]{1,0:T(8,128)S(1)}, f32[2,256,128]{2,0,1:T(2,128)S(1)}, s32[]{:T(128)}, /*index=5*/s32[12...) while((s32[]{:T(128)}, f32[128,32]{1,0:T(8,128)S(1)}, ...), condition=%wide.region_40.39_spmd, body=%wide.region_7.38_spmd.sunk | while | flops 682149 | bytes 849607 | solution.py:133
  1595.3 4.8 constant_dynamic-update-slice_fusion.36
  1600.2 194.0 %all-reduce.3.cloned.1.call-done = f32[256,2,4096]{0,1,2:T(2,128)} async-done(((f32[256,2,4096]{0,1,2:T(2,128)}), f32[256,2,4096]{0,1,2:T(2,128)}) %all-reduce.3.cloned.1.call-update) | async-done | bytes 8388624 | tf_op jit(solution)/shard_map/psum | solution.py:225
  1794.2 9.3 fusion.40
  1804.1 61.2 %psum.15 = f32[4096]{0:T(1024)S(1)} all-reduce(f32[4096]{0:T(1024)S(1)} %fusion.41), channel_id=1, replica_groups=mesh['blk'=2,'mblk'=16] {'mblk'}, use_global_device_ids=true, to_apply=%region_45.46 | all-reduce | flops 4096 | bytes 32768 | tf_op jit(solution)/shard_map/psum | solution.py:226
  (14503 shorter events, 1402.5 us)
Async XLA Ops:
  11.1 7.9 all-to-all-start
  19.0 7.4 all-to-all-start.1
  30.4 13.3 all-to-all-start.2
  36.7 1757.4 %all-reduce.3.cloned.1.call-start = ((), (), s32[]{:S(2)}) async-start(), calls=%async_computation.3 | async-start | bytes 16777216 | tf_op jit(solution)/shard_map/psum | solution.py:225
  1803.5 61.8 %copy-start = (f32[4096]{0:T(1024)S(1)}, f32[4096]{0:T(1024)}, u32[]{:S(2)}) copy-start(f32[4096]{0:T(1024)} %param.13) | copy-start | bytes 49156
Sparse Core Ops, SparseCore 0:
  1600.3 193.8 all-reduce.2
where the time goes:
time: 1880 us
  other arithmetic  1390 us (74%)
  waiting for transfers between devices  205 us (11%)
  loops' own time  147 us (8%)
  blocking collectives  61.2 us (3%)
  local copies, waits for them, and re-layouts  36.7 us (2%)
    reduce_sum x1536, other arithmetic, sixteen_rows(): jnp.sum(fresh_row * spec_rows[0], axis=1)  677 us
    select_n x1536, other arithmetic, advance_rows(): jnp.where(degree > orders[:, None], grown, jnp.where(degree == orders[:,...  454 us
    psum x1, waiting for transfers between devices, on_device(): alm_rows = lax.psum(partial_alm, 'blk')  194 us
    another operation x32, loops' own time, one_block(): lax.fori_loop(0, block_len // 16, sixteen_rows, (prev_one, prev_two, empt...  140 us
    while x7680, other arithmetic  112 us
    mul x2048, other arithmetic, coefficients(): alpha_term * jnp.sqrt(jnp.maximum((degree_f - 1.0 - orders_f) * (degree_f...  64.1 us
    psum x1, blocking collectives, on_device(): power_sum = lax.psum(power_part(alm_rows, orders), 'mblk')  61.2 us

commit v1 on v0

v1 whole, which is shorter than its diff:
```python
import functools
import math

import jax
import jax.numpy as jnp
import numpy as np
from jax import lax
from jax.experimental import pallas as pl
from jax.experimental.pallas import tpu as pltpu
from jax.sharding import PartitionSpec as P

NSIDE = 2048
CYCLE_PIX = 8192
LMAX = 4096
BLOCK_PIX = 1024
SEGS = 8
LANES = 128
HIGHEST = lax.Precision.HIGHEST


def dft_tables(n_dev):
    width = CYCLE_PIX // n_dev
    pairs = LMAX // (2 * n_dev)
    a = np.arange(n_dev)
    p2 = np.arange(n_dev)
    p1 = np.arange(width)
    one = 2.0 * np.pi * (a[:, None] * p2[None, :] % n_dev) / n_dev
    first = np.concatenate([np.cos(one), -np.sin(one), np.cos(one)[::-1], -np.sin(one)[::-1]])
    two = 2.0 * np.pi * a[:, None] * p1[None, :] / CYCLE_PIX
    turn = np.stack([np.cos(two), np.sin(two), np.cos(two)[::-1], np.sin(two)[::-1]])
    q = np.arange(pairs)
    second = []
    for i in (q, 2 * pairs - 1 - q):
        angle = 2.0 * np.pi * (p1[:, None] * i[None, :] % width) / width
        cos, sin = np.cos(angle), np.sin(angle)
        second.append(np.block([[cos, -sin], [sin, cos]]))
    low = a[:, None] + n_dev * q[None, :]
    half = []
    for m in (low, LMAX - 1 - low):
        angle = np.pi * m / CYCLE_PIX
        cos, sin = np.cos(angle), np.sin(angle)
        half.append(np.concatenate([cos, cos], 1))
        half.append(np.concatenate([sin, -sin], 1))
    f32 = np.float32
    return first.astype(f32), turn.astype(f32), np.stack(second).astype(f32), np.stack(half).astype(f32)


def dft_kernel(
    n_dev, pairs, place_ref, mask_ref, pix_ref, first_ref, turn_ref, second_ref, half_ref, out_ref, x_ref
):
    slots = pix_ref.shape[0]
    cycles = x_ref.shape[0]
    width = CYCLE_PIX // n_dev
    rows = BLOCK_PIX // width
    x_ref[...] = jnp.zeros_like(x_ref)
    for i in range(slots):
        place = place_ref[i]
        cycle, seg = place // SEGS, lax.rem(place, SEGS)
        keep = mask_ref[i].astype(jnp.float32)
        for h in range(rows):
            x_ref[cycle, pl.ds(seg * rows + h, 1), :] = pix_ref[i : i + 1, h * width : (h + 1) * width] * keep
    for phase in range(2):
        for c in range(cycles):
            y = jnp.dot(
                first_ref[2 * phase * n_dev : 2 * (phase + 1) * n_dev, :],
                x_ref[c],
                precision=HIGHEST,
                preferred_element_type=jnp.float32,
            )
            y_re, y_im = y[:n_dev], y[n_dev:]
            cos, sin = turn_ref[2 * phase], turn_ref[2 * phase + 1]
            z = jnp.concatenate([y_re * cos + y_im * sin, y_im * cos - y_re * sin], axis=1)
            spec = jnp.dot(z, second_ref[phase], precision=HIGHEST, preferred_element_type=jnp.float32)
            if c % 2 == 0:
                if 2 * pairs == LANES:
                    swapped = pltpu.roll(spec, pairs, 1)
                else:
                    swapped = jnp.concatenate([spec[:, pairs:], spec[:, :pairs]], axis=1)
                spec = spec * half_ref[2 * phase] + swapped * half_ref[2 * phase + 1]
            out_ref[pl.ds(2 * c + phase, n_dev, stride=2 * cycles), :] = spec


def cycle_spectra(pixels, place, mask, n_dev, cycles):
    pairs = LMAX // (2 * n_dev)
    tables = [jnp.asarray(t) for t in dft_tables(n_dev)]
    smem = pl.BlockSpec(memory_space=pltpu.SMEM)
    vmem = pl.BlockSpec(memory_space=pltpu.VMEM)
    return pl.pallas_call(
        functools.partial(dft_kernel, n_dev, pairs),
        out_shape=jax.ShapeDtypeStruct((n_dev * 2 * cycles, 2 * pairs), jnp.float32),
        in_specs=[smem, smem] + [vmem] * 5,
        out_specs=vmem,
        scratch_shapes=[pltpu.VMEM((cycles, n_dev, CYCLE_PIX // n_dev), jnp.float32)],
        compiler_params=pltpu.CompilerParams(vmem_limit_bytes=32 * 1024 * 1024),
        name="cycle_dft",
    )(place, mask, pixels, *tables)


def wallis(count):
    value = np.zeros(count)
    k = np.arange(0, count - 2, 2)
    value[0::2] = np.concatenate([[1.0], np.cumprod((k + 1.0) / (k + 2.0))])[: len(value[0::2])]
    value[1::2] = 2.0 / np.pi * np.concatenate([[1.0], np.cumprod((k + 2.0) / (k + 3.0))])[: len(value[1::2])]
    return value


def legendre_tables(n_dev, n_blk, cycles_all, slots):
    pairs = LMAX // (2 * n_dev)
    blocks = 2 * pairs + 1
    total = blocks * n_dev
    value = wallis(2 * LMAX + 4 * n_dev + total)
    tau = np.arange(total)[:, None]
    q = (np.arange(LANES) % pairs)[None, :]
    rise = np.where(q < tau // n_dev, tau - n_dev * (q + 1), tau)
    t_rise = value[rise]
    wide = np.arange(total + 2 * n_dev)[:, None]
    t_low = value[np.maximum(wide - n_dev + n_dev * q, 0)]
    t_high = value[wide + 2 * LMAX - 2 - 2 * n_dev * q - 2 * (n_dev - 1)]

    lats = cycles_all // 2
    x = (lats - np.arange(lats)) * (2.0 / (3.0 * NSIDE))
    reps = LANES // pairs
    vregs = lats // (8 * reps)
    order = np.arange(lats).reshape(vregs, reps, 8)
    x_lanes = np.repeat(x[order].transpose(0, 2, 1), pairs, axis=2).reshape(vregs * 8, LANES)
    x_tabs = np.stack([x_lanes, x_lanes * x_lanes, 0.5 * np.log1p(-x_lanes * x_lanes)])

    n_mblk = n_dev // n_blk
    cycle_dev = slots // SEGS
    r_band = cycle_dev * n_mblk
    col = 2 * n_blk * cycle_dev
    pick = np.zeros((4 * lats + 8, n_dev * col))

    def put(row, cycle, phase, weight):
        band, inner = divmod(cycle, r_band)
        j, k = divmod(inner, cycle_dev)
        for s in range(n_blk):
            pick[row, (s * n_mblk + j) * col + (band * cycle_dev + k) * 2 + phase] += weight

    for phase in range(2):
        for n in range(lats):
            for odd in range(2):
                row = (2 * phase + odd) * lats + n
                put(row, n, phase, 1.0)
                if n:
                    put(row, cycles_all - n, phase, -1.0 if odd else 1.0)
        put(4 * lats + phase, lats, phase, 1.0)

    lane = np.arange(LANES)
    band_of = (3 * pairs - 2 - lane) % LANES
    copies = LANES // n_dev
    spread = (band_of[None, :] % copies == (lane // n_dev)[:, None]) & (band_of[None, :] < 2 * pairs)
    gather = band_of[None, :] // copies == np.arange(LMAX // LANES)[:, None]
    f32 = np.float32
    return [t.astype(f32) for t in (t_rise, t_low, t_high, x_tabs, pick, spread, gather)]


def legendre_kernel(
    n_dev,
    pairs,
    lats,
    pixel_total,
    dev_ref,
    got_ref,
    rise_ref,
    low_ref,
    high_ref,
    x_ref,
    pick_ref,
    spread_ref,
    gather_ref,
    out_ref,
    f_ref,
    coef_ref,
    prod_ref,
    accl_ref,
    acch_ref,
):
    d = dev_ref[0]
    reps = LANES // pairs
    vregs = lats // (8 * reps)
    blocks = 2 * pairs + 1
    tiles = n_dev // 8
    group = min(4, tiles)
    span = 2 * pairs

    lane = lax.broadcasted_iota(jnp.int32, (8, LANES), 1)
    sub = lax.broadcasted_iota(jnp.int32, (8, LANES), 0)
    q = lane % pairs
    m_low = (d + n_dev * q).astype(jnp.float32)
    m_high = (LMAX - 1.0) - m_low

    f_all = jnp.dot(pick_ref[...], got_ref[...], precision=HIGHEST, preferred_element_type=jnp.float32)

    def lanes_of(start, v, part):
        pieces = []
        for h in range(reps):
            row = start + (v * reps + h) * 8
            pieces.append(f_all[row : row + 8, part * pairs : (part + 1) * pairs])
        return jnp.concatenate(pieces, axis=1)

    for phase in range(2):
        for odd in range(2):
            for v in range(vregs):
                for part in range(2):
                    val = lanes_of((2 * phase + odd) * lats, v, part)
                    if odd:
                        val = val * x_ref[0, 8 * v : 8 * v + 8, :]
                    slot = ((phase * 2 + odd) * vregs + v) * 2 + part
                    f_ref[8 * slot : 8 * slot + 8, :] = val
    base = 8 * vregs
    for phase in range(2):
        for part in range(2):
            row = f_all[4 * lats + phase : 4 * lats + phase + 1, part * pairs : (part + 1) * pairs]
            row = jnp.concatenate([row] * reps, axis=1)
            slot = base + phase * 2 + part
            f_ref[8 * slot : 8 * slot + 8, :] = jnp.broadcast_to(row, (8, LANES))

    accl_ref[...] = jnp.zeros_like(accl_ref)
    acch_ref[...] = jnp.zeros_like(acch_ref)
    x2 = [x_ref[1, 8 * v : 8 * v + 8, :] for v in range(vregs)]
    logs = [x_ref[2, 8 * v : 8 * v + 8, :] for v in range(vregs)]
    seed_low = [jnp.exp(m_low * g) for g in logs]
    seed_high = [jnp.exp(m_high * g) for g in logs]
    sign = jnp.where(sub % 4 == 0, 1.0, jnp.where(sub % 4 == 2, -1.0, 0.0)).astype(jnp.float32)
    q_f = q.astype(jnp.float32)
    sub_f = sub.astype(jnp.float32)
    d_f = d.astype(jnp.float32)
    weight_low = jnp.where(m_low == 0.0, 1.0, 2.0) / pixel_total
    weight_high = jnp.full((8, LANES), 2.0 / pixel_total, jnp.float32)
    head = lane < pairs

    def one_block(b, state):
        even, odd = list(state[:vregs]), list(state[vregs:])
        is_low = q < b
        turned = q == b - 1
        even = [jnp.where(turned, s, e) for s, e in zip(seed_low, even)]
        odd = [jnp.where(turned, 0.0, o) for o in odd]

        def pick_phase(slot_low, slot_high):
            return jnp.where(is_low, f_ref[8 * slot_low : 8 * slot_low + 8, :], f_ref[8 * slot_high : 8 * slot_high + 8, :])

        def spectra(parity, v, part):
            return pick_phase((parity * vregs + v) * 2 + part, ((2 + parity) * vregs + v) * 2 + part)

        f_now = [[[spectra(o, v, part) for part in range(2)] for v in range(vregs)] for o in range(2)]
        flat = [pick_phase(base + part, base + 2 + part) * sign for part in range(2)]
        weight = jnp.where(is_low, weight_low, weight_high)
        start = (b * n_dev).astype(jnp.float32)
        l_first = jnp.where(is_low, start - n_dev + d_f, start + (LMAX - 1.0) - d_f - n_dev * q_f) + sub_f
        low_lane = jnp.logical_and(head, is_low)
        high_lane = jnp.logical_and(head, jnp.logical_not(is_low))
        target = lax.rem(3 * pairs - 2 - (b - 1) + 2 * LANES, LANES)

        def one_group(g, state):
            even, odd = list(state[:vregs]), list(state[vregs:])
            weights = []
            for i in range(group):
                row = g * (8 * group) + 8 * i
                tau = b * n_dev + row
                vv = rise_ref[pl.ds(pl.multiple_of(tau, 8), 8), :] * jnp.where(
                    is_low, low_ref[pl.ds(tau + 2 * d, 8), :], high_ref[pl.ds(tau + 2 * (n_dev - 1 - d), 8), :]
                )
                degree = l_first + lax.convert_element_type(row, jnp.float32)
                coef_ref[8 * i : 8 * i + 8, :] = vv * (degree * math.pi + 0.5 * math.pi)
                weights.append(jnp.where(degree < LMAX, vv * weight, 0.0))
            for i in range(group):
                for j in range(0, 8, 2):
                    for parity in range(2):
                        step = 8 * i + j + parity
                        now = odd if parity else even
                        for part in range(2):
                            total = now[0] * f_now[parity][0][part]
                            for v in range(1, vregs):
                                total = total + now[v] * f_now[parity][v][part]
                            prod_ref[part, 8 * step : 8 * step + 8, :] = total
                        coef = coef_ref[step : step + 1, :]
                        if parity:
                            even = [(coef * x2[v]) * odd[v] - even[v] for v in range(vregs)]
                        else:
                            odd = [coef * even[v] - odd[v] for v in range(vregs)]
                sums = []
                for part in range(2):
                    total = prod_ref[part, pl.ds(64 * i, 8, stride=8), :]
                    for s in range(1, 8):
                        total = total + prod_ref[part, pl.ds(64 * i + s, 8, stride=8), :]
                    width = pairs
                    while width < LANES:
                        total = total + pltpu.roll(total, width, 1)
                        width *= 2
                    sums.append(total + flat[part])
                power = (sums[0] * sums[0] + sums[1] * sums[1]) * weights[i]
                row = pl.multiple_of(g * (8 * group) + 8 * i, 8)
                low_sum = jnp.sum(jnp.where(low_lane, power, 0.0), axis=1, keepdims=True)
                accl_ref[pl.ds(row, 8), :] = jnp.where(lane == target, low_sum, accl_ref[pl.ds(row, 8), :])

                @pl.when(b < pairs)
                def _():
                    acch_ref[pl.ds(row, 8), :] = pltpu.roll(acch_ref[pl.ds(row, 8), :], 1, 1) + jnp.where(
                        high_lane, power, 0.0
                    )

            return (*even, *odd)

        if tiles == group:
            return one_group(0, (*even, *odd))
        return lax.fori_loop(0, tiles // group, one_group, (*even, *odd))

    zero = jnp.zeros((8, LANES), jnp.float32)
    lax.fori_loop(0, blocks, one_block, (*seed_high, *([zero] * vregs)))

    rows = lax.broadcasted_iota(jnp.int32, (n_dev, LANES), 0)

    def shifted(acc, shift):
        rolled = pltpu.roll(acc, shift, 0)
        return jnp.where(rows < shift, pltpu.roll(rolled, LANES - 1, 1), rolled)

    power = shifted(accl_ref[...], d) + shifted(acch_ref[...], n_dev - 1 - d)
    copies = LANES // n_dev
    tall = jnp.concatenate([power] * copies, axis=0) * spread_ref[...]
    out_ref[...] = lax.dot_general(
        gather_ref[...], tall, (((1,), (1,)), ((), ())), precision=HIGHEST, preferred_element_type=jnp.float32
    )


def legendre_power(got, dev, n_dev, n_blk, cycles_all, slots):
    pairs = LMAX // (2 * n_dev)
    lats = cycles_all // 2
    vregs = lats * pairs // (8 * LANES)
    tables = [jnp.asarray(t) for t in legendre_tables(n_dev, n_blk, cycles_all, slots)]
    smem = pl.BlockSpec(memory_space=pltpu.SMEM)
    vmem = pl.BlockSpec(memory_space=pltpu.VMEM)
    return pl.pallas_call(
        functools.partial(legendre_kernel, n_dev, pairs, lats, float(cycles_all * CYCLE_PIX)),
        out_shape=jax.ShapeDtypeStruct((LMAX // LANES, LANES), jnp.float32),
        in_specs=[smem] + [vmem] * 8,
        out_specs=vmem,
        scratch_shapes=[
            pltpu.VMEM((8 * (8 * vregs + 4), LANES), jnp.float32),
            pltpu.VMEM((32, LANES), jnp.float32),
            pltpu.VMEM((2, 256, LANES), jnp.float32),
            pltpu.VMEM((n_dev, LANES), jnp.float32),
            pltpu.VMEM((n_dev, LANES), jnp.float32),
        ],
        compiler_params=pltpu.CompilerParams(vmem_limit_bytes=48 * 1024 * 1024),
        name="legendre_power",
    )(dev, got, *tables)


def on_device(pixels, block_ids, block_mask, model_cl):
    n_blk = lax.axis_size("blk")
    n_mblk = lax.axis_size("mblk")
    n_dev = n_blk * n_mblk
    both = ("blk", "mblk")
    dev = lax.axis_index("blk") * n_mblk + lax.axis_index("mblk")
    slots = pixels.shape[0]
    cycle_dev = slots // SEGS
    cycles = n_blk * cycle_dev
    r_band = cycle_dev * n_mblk
    cycles_all = r_band * n_blk
    pairs = LMAX // (2 * n_dev)

    cycle = block_ids // SEGS
    band = cycle // r_band
    local = cycle - band * r_band - lax.axis_index("mblk") * cycle_dev
    place = (band * cycle_dev + local) * SEGS + block_ids % SEGS
    sent = cycle_spectra(pixels, place, block_mask, n_dev, cycles)
    got = lax.all_to_all(sent.reshape(n_dev, 2 * cycles, 2 * pairs), both, 0, 0, tiled=True)
    got = got.reshape(n_dev * 2 * cycles, 2 * pairs)
    power = legendre_power(got, dev[None], n_dev, n_blk, cycles_all, slots)

    bit = 1
    while bit < n_mblk:
        power = power + lax.ppermute(power, "mblk", [(i, i ^ bit) for i in range(n_mblk)])
        bit *= 2
    bit = 1
    while bit < n_blk:
        power = power + lax.ppermute(power, "blk", [(i, i ^ bit) for i in range(n_blk)])
        bit *= 2
    pseudo_cl = power.reshape(LMAX)
    rel_error = (pseudo_cl - model_cl) / model_cl
    misfit = jnp.mean(rel_error * rel_error)
    return (pseudo_cl, misfit)


def solution(mesh):
    in_specs = (P(("blk", "mblk"), None), P(("blk", "mblk")), P(("blk", "mblk")), P())
    out_specs = (P(), P())
    return jax.shard_map(
        on_device, mesh=mesh, in_specs=in_specs, out_specs=out_specs, check_vma=False
    )
```

time: 1880 us -> 153 us (0.08)
  other arithmetic: 1390 us -> 1.9 us
  waiting for transfers between devices: 205 us -> 22.8 us
  loops' own time: 147 us -> 0 us
  Pallas kernels: 0 us -> 104 us
  blocking collectives: 61.2 us -> 0 us
  local copies, waits for them, and re-layouts: 36.7 us -> 11.5 us
    reduce_sum x1537 -> x0, other arithmetic: 678 us -> none  [the longest x1536 677 us: sixteen_rows(): jnp.sum(fresh_row * spec_rows[0], axis=1)]
    select_n x1542 -> x0, other arithmetic: 454 us -> none  [the longest x1536 454 us: advance_rows(): jnp.where(degree > orders[:, None], grown, jnp.where(degree == orders[:,...]
    psum x1 -> x0, waiting for transfers between devices: 194 us -> none  [on_device(): alm_rows = lax.psum(partial_alm, 'blk')]
    another operation x35 -> x0, loops' own time: 147 us -> none  [the longest x32 140 us: one_block(): lax.fori_loop(0, block_len // 16, sixteen_rows, (prev_one, prev_two, empt...]
    while x7680 -> x0, other arithmetic: 112 us -> none
    pallas_call x0 -> x2, Pallas kernels: none -> 104 us  [the longest x1 99.9 us: legendre_power(): pl.pallas_call(functools.partial(legendre_kernel, n_dev, pairs, lats, flo...]
    mul x2053 -> x0, other arithmetic: 65.1 us -> none  [the longest x2048 64.1 us: coefficients(): alpha_term * jnp.sqrt(jnp.maximum((degree_f - 1.0 - orders_f) * (degree_f...]
    psum x1 -> x0, blocking collectives: 61.2 us -> none  [on_device(): power_sum = lax.psum(power_part(alm_rows, orders), 'mblk')]
where the time goes in v1:
time: 153 us
  Pallas kernels  104 us (68%)
  waiting for transfers between devices  22.8 us (15%)
  local copies, waits for them, and re-layouts  11.5 us (8%)
  starting transfers between devices  9.74 us (6%)
  between operations  2.46 us (2%)
  other arithmetic  1.9 us (1%)
    pallas_call x1, Pallas kernels, legendre_power(): pl.pallas_call(functools.partial(legendre_kernel, n_dev, pairs, lats, flo...  99.9 us
    ppermute x4, waiting for transfers between devices, on_device(): lax.ppermute(power, 'mblk', [(i, i ^ bit) for i in range(n_mblk)])  11.7 us
    unnamed x26, local copies, waits for them, and re-layouts  11.5 us
    all_to_all x1, waiting for transfers between devices, on_device(): lax.all_to_all(sent.reshape(n_dev, 2 * cycles, 2 * pairs), both, 0, 0, ti...  8.22 us
    all_to_all x1, starting transfers between devices, on_device(): lax.all_to_all(sent.reshape(n_dev, 2 * cycles, 2 * pairs), both, 0, 0, ti...  7.3 us
    pallas_call x1, Pallas kernels, cycle_spectra(): pl.pallas_call(functools.partial(dft_kernel, n_dev, pairs), out_shape=jax...  4.24 us
  transfers between devices with their start and end apart: 6, of which 6 were waited for; matrix products, arithmetic and copies ran while one was open for 0% of the time, Pallas kernels for 0%

profile of v1, /device:TPU:0, one launch (start us, length us, event | category | flops | bytes accessed | tf_op | source)
XLA Modules:
  0.0 152.6 jit_solution(1983972894217506454)
XLA Ops:
  0.6 0.7 fusion.2.place_ref
  1.3 0.0 copy-start.2
  1.3 1.0 copy-done.2
  2.4 0.0 copy-start.4
  2.4 0.9 copy-done.4
  3.3 0.0 copy-start.6
  3.3 0.8 copy-done.6
  4.1 0.0 copy-start.7
  4.1 0.8 copy-done.7
  4.9 0.0 copy-start.8
  4.9 0.8 copy-done.8
  5.8 0.0 copy-start.11
  5.8 0.7 copy-done.11
  6.4 4.2 %cycle_dft.1 = f32[256,128]{1,0:T(8,128)} custom-call(s32[16]{0:T(128)S(1)} %fusion.2.place_ref, s32[16]{0:T(128)S(1)} %copy-done.11, f32[16,1024]{1,0:T(8,128)S(1)} %copy-done.6, f32[128,32]{1,0:T(8,128)S(1)} %copy-done.8, f32[4,32,256]{2,1,0:T(8,128)S(1)} %copy-done.4, f32[2,512,128]{2,1,0:T(8,128)S(1)} %copy-done.2, f32[4,32,128]{2,1,0:T(8,128)S(1)} %copy-done.7), custom_call_target="tpu_custom_call" | custom-call | tf_op jit(solution)/shard_map/cycle_dft/pallas_call | solution.py:88
  10.7 7.3 %all-to-all-start = ((f32[32,8,128]{2,1,0:T(8,128)}), f32[32,8,128]{2,1,0:T(8,128)S(1)}, u32[]{:S(2)}, u32[]{:S(2)}) async-start(f32[32,8,128]{2,1,0:T(8,128)} %bitcast.1), calls=%async_computation | async-start | bytes 262144 | tf_op jit(solution)/shard_map/all_to_all | solution.py:368
  18.0 8.2 %all-to-all-done = f32[32,8,128]{2,1,0:T(8,128)S(1)} async-done(((f32[32,8,128]{2,1,0:T(8,128)}), f32[32,8,128]{2,1,0:T(8,128)S(1)}, u32[]{:S(2)}, u32[]{:S(2)}) %all-to-all-start) | async-done | bytes 131104 | tf_op jit(solution)/shard_map/all_to_all | solution.py:368
  26.2 0.0 copy-start
  26.2 1.6 %copy-done = f32[4192,128]{1,0:T(8,128)S(1)} copy-done((f32[4192,128]{1,0:T(8,128)S(1)}, f32[4192,128]{1,0:T(8,128)}, u32[]{:S(2)}) %copy-start) | copy-done | bytes 2146328
  27.8 0.0 copy-start.1
  27.8 1.6 %copy-done.1 = f32[4128,128]{1,0:T(8,128)S(1)} copy-done((f32[4128,128]{1,0:T(8,128)S(1)}, f32[4128,128]{1,0:T(8,128)}, u32[]{:S(2)}) %copy-start.1) | copy-done | bytes 2113560
  29.4 0.0 copy-start.3
  29.4 0.9 copy-done.3
  30.3 0.0 copy-start.5
  30.3 0.8 copy-done.5
  31.2 0.0 copy-start.9
  31.2 0.7 copy-done.9
  31.9 0.0 copy-start.10
  31.9 0.7 copy-done.10
  32.6 0.0 copy-start.12
  32.6 99.9 %legendre_power.1 = f32[32,128]{1,0:T(8,128)S(1)} custom-call(s32[1]{0:T(128)} %bitcast.dev_ref, f32[256,128]{1,0:T(8,128)S(1)} %bitcast.6, f32[4128,128]{1,0:T(8,128)S(1)} %copy-done.1, f32[4192,128]{1,0:T(8,128)S(1)} %copy-done, f32[4192,128]{1,0:T(8,128)} %constant.89.clone.high_ref, f32[3,16,128]{2,1,0:T(8,128)S(1)} %copy-done.9, ...), custom_call_target="tpu_custom_call" | custom-call | tf_op jit(solution)/shard_map/legendre_power/pallas_call | solution.py:333
  132.5 0.4 collective-permute-start
  132.9 0.9 collective-permute-done
  133.7 0.6 collective-permute-start.1
  134.3 3.1 %collective-permute-done.1 = f32[32,128]{1,0:T(8,128)S(1)} collective-permute-done((f32[32,128]{1,0:T(8,128)S(1)}, f32[32,128]{1,0:T(8,128)S(1)}, u32[]{:S(2)}, u32[]{:S(2)}) %collective-permute-start.1) | collective-permute-done | bytes 16416 | tf_op jit(solution)/shard_map/ppermute | solution.py:374
  137.5 0.1 collective-permute-start.2
  137.6 3.7 %collective-permute-done.2 = f32[32,128]{1,0:T(8,128)S(1)} collective-permute-done((f32[32,128]{1,0:T(8,128)S(1)}, f32[32,128]{1,0:T(8,128)S(1)}, u32[]{:S(2)}, u32[]{:S(2)}) %collective-permute-start.2) | collective-permute-done | bytes 16416 | tf_op jit(solution)/shard_map/ppermute | solution.py:374
  141.2 0.6 collective-permute-start.3
  141.8 4.0 %collective-permute-done.3 = f32[32,128]{1,0:T(8,128)S(1)} collective-permute-done((f32[32,128]{1,0:T(8,128)S(1)}, f32[32,128]{1,0:T(8,128)S(1)}, u32[]{:S(2)}, u32[]{:S(2)}) %collective-permute-start.3) | collective-permute-done | bytes 16416 | tf_op jit(solution)/shard_map/ppermute | solution.py:374
  145.9 0.8 collective-permute-start.4
  146.7 3.0 %collective-permute-done.4 = f32[32,128]{1,0:T(8,128)S(1)} collective-permute-done((f32[32,128]{1,0:T(8,128)S(1)}, f32[32,128]{1,0:T(8,128)S(1)}, u32[]{:S(2)}, u32[]{:S(2)}) %collective-permute-start.4) | collective-permute-done | bytes 16416 | tf_op jit(solution)/shard_map/ppermute | solution.py:378
  149.6 0.0 copy-done.12
  149.6 1.2 fusion.1
  (4 shorter events, 0.0 us)
Async XLA Ops:
  1.3 1.0 copy-start.2
  2.4 0.9 copy-start.4
  3.3 0.8 copy-start.6
  4.1 0.8 copy-start.7
  4.9 0.8 copy-start.8
  5.8 0.7 copy-start.11
  10.7 15.5 %all-to-all-start = ((f32[32,8,128]{2,1,0:T(8,128)}), f32[32,8,128]{2,1,0:T(8,128)S(1)}, u32[]{:S(2)}, u32[]{:S(2)}) async-start(f32[32,8,128]{2,1,0:T(8,128)} %bitcast.1), calls=%async_computation | async-start | bytes 262144 | tf_op jit(solution)/shard_map/all_to_all | solution.py:368
  26.2 1.6 %copy-start = (f32[4192,128]{1,0:T(8,128)S(1)}, f32[4192,128]{1,0:T(8,128)}, u32[]{:S(2)}) copy-start(f32[4192,128]{1,0:T(8,128)} %constant.88.clone.low_ref) | copy-start | bytes 6438916
  27.8 1.6 %copy-start.1 = (f32[4128,128]{1,0:T(8,128)S(1)}, f32[4128,128]{1,0:T(8,128)}, u32[]{:S(2)}) copy-start(f32[4128,128]{1,0:T(8,128)} %constant.87.clone.rise_ref) | copy-start | bytes 6340612
  29.4 0.9 copy-start.3
  30.3 0.8 copy-start.5
  31.2 0.7 copy-start.9
  31.9 0.7 copy-start.10
  32.6 117.0 %copy-start.12 = (f32[4096]{0:T(1024)S(1)}, f32[4096]{0:T(1024)}, u32[]{:S(2)}) copy-start(f32[4096]{0:T(1024)} %param.18) | copy-start | bytes 49156
  132.5 1.2 collective-permute-start
  133.7 3.7 %collective-permute-start.1 = (f32[32,128]{1,0:T(8,128)S(1)}, f32[32,128]{1,0:T(8,128)S(1)}, u32[]{:S(2)}, u32[]{:S(2)}) collective-permute-start(f32[32,128]{1,0:T(8,128)S(1)} %add.36), channel_id=1, source_target_pairs={{0,2},{1,3},{2,0},{3,1},{4,6},{5,7},{6,4},{7,5},{8,10},{9,11},{10,... | collective-permute-start | bytes 49160 | tf_op jit(solution)/shard_map/ppermute | solution.py:374
  137.5 3.7 %collective-permute-start.2 = (f32[32,128]{1,0:T(8,128)S(1)}, f32[32,128]{1,0:T(8,128)S(1)}, u32[]{:S(2)}, u32[]{:S(2)}) collective-permute-start(f32[32,128]{1,0:T(8,128)S(1)} %add.37), channel_id=1, source_target_pairs={{0,4},{1,5},{2,6},{3,7},{4,0},{5,1},{6,2},{7,3},{8,12},{9,13},{10,... | collective-permute-start | bytes 49160 | tf_op jit(solution)/shard_map/ppermute | solution.py:374
  141.2 4.6 %collective-permute-start.3 = (f32[32,128]{1,0:T(8,128)S(1)}, f32[32,128]{1,0:T(8,128)S(1)}, u32[]{:S(2)}, u32[]{:S(2)}) collective-permute-start(f32[32,128]{1,0:T(8,128)S(1)} %add.38), channel_id=1, source_target_pairs={{0,8},{1,9},{2,10},{3,11},{4,12},{5,13},{6,14},{7,15},{8,0},{9,1},... | collective-permute-start | bytes 49160 | tf_op jit(solution)/shard_map/ppermute | solution.py:374
  145.9 3.7 %collective-permute-start.4 = (f32[32,128]{1,0:T(8,128)S(1)}, f32[32,128]{1,0:T(8,128)S(1)}, u32[]{:S(2)}, u32[]{:S(2)}) collective-permute-start(f32[32,128]{1,0:T(8,128)S(1)} %add.39), channel_id=1, source_target_pairs={{0,16},{16,0},{1,17},{17,1},{2,18},{18,2},{3,19},{19,3},{4,20},{20... | collective-permute-start | bytes 49160 | tf_op jit(solution)/shard_map/ppermute | solution.py:378

commit v2 on v1

v2 whole, which is shorter than its diff:
```python
import functools
import math

import jax
import jax.numpy as jnp
import numpy as np
from jax import lax
from jax.experimental import pallas as pl
from jax.experimental.pallas import tpu as pltpu
from jax.sharding import PartitionSpec as P

NSIDE = 2048
CYCLE_PIX = 8192
LMAX = 4096
BLOCK_PIX = 1024
SEGS = 8
LANES = 128
CHUNK = 32
PITCH = 12
STREAMED = 80
PIECES = 5
VMEM_LIMIT = 56 * 1024 * 1024
F32 = jnp.float32
BF16 = jnp.bfloat16
ANY = pl.BlockSpec(memory_space=pl.ANY)
SMEM = pl.BlockSpec(memory_space=pltpu.SMEM)
VMEM = pl.BlockSpec(memory_space=pltpu.VMEM)


def device_index():
    return lax.axis_index("blk") * lax.axis_size("mblk") + lax.axis_index("mblk")


def split_table(table):
    high = table.astype(jnp.bfloat16)
    low = (table - high.astype(np.float64)).astype(jnp.bfloat16)
    return high, low


def split(x):
    high = x.astype(BF16)
    return high, (x - high.astype(F32)).astype(BF16)


def dot(a, b):
    return jnp.dot(a, b, preferred_element_type=F32)


def fetch(pairs, sems):
    copies = [pltpu.make_async_copy(src, dst, sems.at[i]) for i, (src, dst) in enumerate(pairs)]
    for copy in copies:
        copy.start()
    return copies


def dft_tables(n_dev):
    width = CYCLE_PIX // n_dev
    pairs = LMAX // (2 * n_dev)
    a = np.arange(n_dev)
    p2 = np.arange(n_dev)
    p1 = np.arange(width)
    one = 2.0 * np.pi * (a[:, None] * p2[None, :] % n_dev) / n_dev
    first = np.concatenate([np.cos(one), -np.sin(one), np.cos(one)[::-1], -np.sin(one)[::-1]])
    high, low = split_table(first)
    first = np.concatenate([high, low, high], axis=1)
    two = 2.0 * np.pi * a[:, None] * p1[None, :] / CYCLE_PIX
    turn = np.stack([np.cos(two), np.sin(two), np.cos(two)[::-1], np.sin(two)[::-1]])
    q = np.arange(pairs)
    second = []
    for i in (q, 2 * pairs - 1 - q):
        angle = 2.0 * np.pi * (p1[:, None] * i[None, :] % width) / width
        cos, sin = np.cos(angle), np.sin(angle)
        second.append(np.concatenate(split_table(np.block([[cos, -sin], [sin, cos]])), axis=1))
    below = a[:, None] + n_dev * q[None, :]
    half = []
    for m in (below, LMAX - 1 - below):
        angle = np.pi * m / CYCLE_PIX
        cos, sin = np.cos(angle), np.sin(angle)
        half.append(np.concatenate([cos, cos], 1))
        half.append(np.concatenate([sin, -sin], 1))
    return first, turn.astype(np.float32), np.stack(second), np.stack(half).astype(np.float32)


def dft_kernel(
    n_dev,
    n_blk,
    ids_ref,
    mask_ref,
    pix_hbm,
    first_hbm,
    turn_hbm,
    second_hbm,
    half_hbm,
    out_ref,
    x_ref,
    pix_ref,
    first_ref,
    turn_ref,
    second_ref,
    half_ref,
    sems,
):
    copies = fetch(
        [
            (pix_hbm, pix_ref),
            (first_hbm, first_ref),
            (turn_hbm, turn_ref),
            (second_hbm, second_ref),
            (half_hbm, half_ref),
        ],
        sems,
    )
    slots = pix_ref.shape[0]
    cycle_dev = slots // SEGS
    cycles = n_blk * cycle_dev
    r_band = cycle_dev * (n_dev // n_blk)
    own = lax.axis_index("mblk") * cycle_dev
    width = CYCLE_PIX // n_dev
    rows = BLOCK_PIX // width
    pairs = LMAX // (2 * n_dev)
    x_ref[...] = jnp.zeros_like(x_ref)
    copies[0].wait()
    for i in range(slots):
        number = ids_ref[i]
        cycle, seg = lax.div(number, SEGS), lax.rem(number, SEGS)
        band = lax.div(cycle, r_band)
        place = band * cycle_dev + cycle - band * r_band - own
        keep = mask_ref[i].astype(F32)
        for h in range(rows):
            x_ref[place, pl.ds(seg * rows + h, 1), :] = pix_ref[i : i + 1, h * width : (h + 1) * width] * keep
    x = jnp.concatenate([x_ref[c] for c in range(cycles)], axis=1)
    x_high, x_low = split(x)
    copies[1].wait()
    y = dot(first_ref[...], jnp.concatenate([x_high, x_high, x_low], axis=0))
    copies[2].wait()
    copies[3].wait()
    copies[4].wait()
    for phase in range(2):
        y_re = y[2 * phase * n_dev : (2 * phase + 1) * n_dev]
        y_im = y[(2 * phase + 1) * n_dev : (2 * phase + 2) * n_dev]
        cos, sin = turn_ref[2 * phase], turn_ref[2 * phase + 1]
        z = []
        for c in range(cycles):
            re, im = y_re[:, c * width : (c + 1) * width], y_im[:, c * width : (c + 1) * width]
            z.append(jnp.concatenate([re * cos + im * sin, im * cos - re * sin], axis=1))
        z_high, z_low = split(jnp.concatenate(z, axis=0))
        table = second_ref[phase]
        both = dot(z_high, table)
        spec_all = both[:, : 2 * pairs] + both[:, 2 * pairs :] + dot(z_low, table[:, : 2 * pairs])
        for c in range(cycles):
            spec = spec_all[c * n_dev : (c + 1) * n_dev]
            if c % 2 == 0:
                if 2 * pairs == LANES:
                    swapped = pltpu.roll(spec, pairs, 1)
                else:
                    swapped = jnp.concatenate([spec[:, pairs:], spec[:, :pairs]], axis=1)
                spec = spec * half_ref[2 * phase] + swapped * half_ref[2 * phase + 1]
            out_ref[pl.ds(2 * c + phase, n_dev, stride=2 * cycles), :] = spec


def cycle_spectra(pixels, block_ids, mask, n_dev, n_blk):
    pairs = LMAX // (2 * n_dev)
    cycles = n_blk * pixels.shape[0] // SEGS
    tables = [jnp.asarray(t) for t in dft_tables(n_dev)]
    return pl.pallas_call(
        functools.partial(dft_kernel, n_dev, n_blk),
        out_shape=jax.ShapeDtypeStruct((n_dev * 2 * cycles, 2 * pairs), F32),
        in_specs=[SMEM, SMEM] + [ANY] * 5,
        out_specs=VMEM,
        scratch_shapes=[pltpu.VMEM((cycles, n_dev, CYCLE_PIX // n_dev), F32), pltpu.VMEM(pixels.shape, F32)]
        + [pltpu.VMEM(t.shape, t.dtype) for t in tables]
        + [pltpu.SemaphoreType.DMA((5,))],
        compiler_params=pltpu.CompilerParams(vmem_limit_bytes=VMEM_LIMIT),
        name="cycle_dft",
    )(block_ids, mask, pixels, *tables)


def wallis(count):
    value = np.zeros(count)
    k = np.arange(0, count - 2, 2)
    value[0::2] = np.concatenate([[1.0], np.cumprod((k + 1.0) / (k + 2.0))])[: len(value[0::2])]
    value[1::2] = 2.0 / np.pi * np.concatenate([[1.0], np.cumprod((k + 2.0) / (k + 3.0))])[: len(value[1::2])]
    return value


def step_blocks(n_dev):
    blocks = LMAX // n_dev + 1
    return blocks + blocks * (n_dev // CHUNK) % 2


def latitude_lanes(n_dev, lats):
    pairs = LMAX // (2 * n_dev)
    x = (lats - np.arange(lats)) * (2.0 / (3.0 * NSIDE))
    reps = LANES // pairs
    order = np.arange(lats).reshape(-1, reps, 8)
    return np.repeat(x[order].transpose(0, 2, 1), pairs, axis=2).reshape(-1, LANES)


def recurrence_tables(n_dev, lats):
    pairs = LMAX // (2 * n_dev)
    total = step_blocks(n_dev) * n_dev
    value = wallis(2 * LMAX + 6 * n_dev + total)
    tau = np.arange(total)[:, None]
    q = np.arange(pairs)[None, :]
    rise = np.where(q < tau // n_dev, tau - n_dev * (q + 1), tau)
    wide = np.arange(total + 2 * n_dev)[:, None]
    t_low = value[np.maximum(wide - n_dev + n_dev * q, 0)]
    t_high = value[wide + 2 * LMAX - 2 - 2 * n_dev * q - 2 * (n_dev - 1)]
    x = latitude_lanes(n_dev, lats)
    x_tabs = np.stack([x, x * x, 0.5 * np.log1p(-x * x)])
    tables = [np.tile(t, (1, LANES // pairs)) for t in (value[rise], t_low, t_high)]
    return [t.astype(np.float32) for t in tables + [x_tabs]]


def advance(coef_ref, row, even, odd, x2):
    one, two = coef_ref[pl.ds(row, 1), :], coef_ref[pl.ds(row + 1, 1), :]
    fresh_odd = [one * e - o for e, o in zip(even, odd)]
    gains = [two * x for x in x2]
    fresh_even = [(g * one - 1.0) * e - g * o for g, e, o in zip(gains, even, odd)]
    return fresh_even, fresh_odd


def turn_lanes(chunk, per_block, q, seeds, even, odd):
    turned = q == lax.div(chunk, per_block) - 1
    if per_block > 1:
        turned = jnp.logical_and(turned, lax.rem(chunk, per_block) == 0)
    return [jnp.where(turned, s, e) for s, e in zip(seeds, even)], [jnp.where(turned, 0.0, o) for o in odd]


def recurrence_kernel(
    n_dev,
    vregs,
    pixel_total,
    rise_hbm,
    low_hbm,
    high_hbm,
    x_hbm,
    rows_hbm,
    u_hbm,
    rise_ref,
    low_ref,
    high_ref,
    x_ref,
    rows_ref,
    u_ref,
    sems,
):
    copies = fetch([(rise_hbm, rise_ref), (low_hbm, low_ref), (high_hbm, high_ref), (x_hbm, x_ref)], sems)
    d = device_index()
    pairs = LMAX // (2 * n_dev)
    per_block = n_dev // CHUNK
    chunks = step_blocks(n_dev) * per_block
    inline = chunks - STREAMED
    total = chunks * CHUNK
    many = max(n for n in range(1, 13) if chunks % n == 0)
    lane = lax.broadcasted_iota(jnp.int32, (8, LANES), 1)
    sub = lax.broadcasted_iota(jnp.int32, (8, LANES), 0)
    q = lax.rem(lane, pairs)
    m_low = (d + n_dev * q).astype(F32)
    m_high = (LMAX - 1.0) - m_low
    weight_low = jnp.where(m_low == 0.0, 1.0, 2.0) / pixel_total
    weight_high = jnp.full((8, LANES), 2.0 / pixel_total, F32)
    l_low = sub.astype(F32) + (d.astype(F32) - n_dev)
    l_high = sub.astype(F32) + m_high
    for copy in copies:
        copy.wait()
    x2 = [x_ref[1, 8 * v : 8 * v + 8, :] for v in range(vregs)]
    logs = [x_ref[2, 8 * v : 8 * v + 8, :] for v in range(vregs)]
    seed_low = [jnp.exp(m_low * g) for g in logs]
    seed_high = [jnp.exp(m_high * g) for g in logs]

    def coefficients(first, carry):
        fresh = []
        for step in range(many):
            chunk = first * many + step
            is_low = q < lax.div(chunk, per_block)
            weight = jnp.where(is_low, weight_low, weight_high)
            start = jnp.where(is_low, l_low, l_high) + (chunk * CHUNK).astype(F32)
            for i in range(CHUNK // 8):
                tau = pl.multiple_of(chunk * CHUNK, CHUNK) + 8 * i
                low = low_ref[pl.ds(tau + 2 * d, 8), :]
                high = high_ref[pl.ds(tau + 2 * (n_dev - 1 - d), 8), :]
                product = rise_ref[pl.ds(tau, 8), :] * jnp.where(is_low, low, high)
                degree = start + 8.0 * i
                coef = product * (degree * math.pi + 0.5 * math.pi)
                fresh.append((tau, coef, jnp.where(degree < LMAX, product * weight, 0.0)))
        for tau, coef, weight in fresh:
            rows_ref[pl.ds(tau, 8), :] = coef
            rows_ref[pl.ds(total + tau, 8), :] = weight
        return carry

    def steps(chunk, state):
        even, odd = turn_lanes(chunk, per_block, q, seed_low, list(state[:vregs]), list(state[vregs:]))
        first = pl.multiple_of(chunk * CHUNK, CHUNK)
        start = pl.multiple_of((chunk - inline) * (CHUNK * 8 * vregs), CHUNK * 8 * vregs)
        for s in range(0, CHUNK, 2):
            fresh_even, fresh_odd = advance(rows_ref, first + s, even, odd, x2)
            for v in range(vregs):
                u_ref[pl.ds(start + 8 * (s * vregs + v), 8), :] = even[v]
                u_ref[pl.ds(start + 8 * ((s + 1) * vregs + v), 8), :] = fresh_odd[v]
            even, odd = fresh_even, fresh_odd
        return (*even, *odd)

    def plain_steps(chunk, state):
        even, odd = turn_lanes(chunk, per_block, q, seed_low, list(state[:vregs]), list(state[vregs:]))
        first = pl.multiple_of(chunk * CHUNK, CHUNK)
        for s in range(0, CHUNK, 2):
            even, odd = advance(rows_ref, first + s, even, odd, x2)
        return (*even, *odd)

    lax.fori_loop(0, chunks // many, coefficients, 0)
    out = [pltpu.make_async_copy(rows_ref, rows_hbm, sems.at[4])]
    out[0].start()
    zero = jnp.zeros((8, LANES), F32)
    state = (*seed_high, *([zero] * vregs))
    state = lax.fori_loop(0, inline // 2, lambda h, s: plain_steps(2 * h + 1, plain_steps(2 * h, s)), state)
    piece = STREAMED // PIECES
    for p in range(PIECES):
        first = inline + p * piece
        state = lax.fori_loop(first // 2, (first + piece) // 2, lambda h, s: steps(2 * h + 1, steps(2 * h, s)), state)
        size = piece * CHUNK * 8 * vregs
        out.append(pltpu.make_async_copy(u_ref.at[pl.ds(p * size, size)], u_hbm.at[pl.ds(p * size, size)], sems.at[5 + p]))
        out[-1].start()
    for copy in out:
        copy.wait()


def legendre_rows(n_dev, lats):
    pairs = LMAX // (2 * n_dev)
    vregs = lats * pairs // (8 * LANES)
    total = step_blocks(n_dev) * n_dev
    tables = [jnp.asarray(t) for t in recurrence_tables(n_dev, lats)]
    rows = jax.ShapeDtypeStruct((2 * total, LANES), F32)
    u = jax.ShapeDtypeStruct((STREAMED * CHUNK * 8 * vregs, LANES), F32)
    return pl.pallas_call(
        functools.partial(recurrence_kernel, n_dev, vregs, float(2 * lats * CYCLE_PIX)),
        out_shape=(rows, u),
        in_specs=[ANY] * 4,
        out_specs=(ANY, ANY),
        scratch_shapes=[pltpu.VMEM(t.shape, t.dtype) for t in [*tables, rows, u]]
        + [pltpu.SemaphoreType.DMA((5 + PIECES,))],
        compiler_params=pltpu.CompilerParams(vmem_limit_bytes=VMEM_LIMIT),
        cost_estimate=pl.CostEstimate(flops=total * 8 * LANES * vregs * 8, bytes_accessed=30000000, transcendentals=0),
        name="legendre_rows",
    )(*tables)


def power_tables(n_dev, n_blk, lats, slots):
    pairs = LMAX // (2 * n_dev)
    cycles_all = 2 * lats
    n_mblk = n_dev // n_blk
    cycle_dev = slots // SEGS
    r_band = cycle_dev * n_mblk
    col = 2 * n_blk * cycle_dev
    pick = np.zeros((4 * lats + 16, n_dev * col))

    def put(row, cycle, phase, weight):
        band, inner = divmod(cycle, r_band)
        j, k = divmod(inner, cycle_dev)
        for s in range(n_blk):
            pick[row, (s * n_mblk + j) * col + (band * cycle_dev + k) * 2 + phase] += weight

    for phase in range(2):
        for n in range(lats):
            for odd in range(2):
                row = (2 * phase + odd) * lats + n
                put(row, n, phase, 1.0)
                if n:
                    put(row, cycles_all - n, phase, -1.0 if odd else 1.0)
        put(4 * lats + phase, lats, phase, 1.0)

    lane = np.arange(LANES)
    band_of = (3 * pairs - 2 - lane) % LANES
    copies = LANES // n_dev
    spread = (band_of[None, :] % copies == (lane // n_dev)[:, None]) & (band_of[None, :] < 2 * pairs)
    gather = band_of[None, :] // copies == np.arange(LMAX // LANES)[:, None]
    return (
        pick.astype(jnp.bfloat16),
        recurrence_tables(n_dev, lats)[3],
        spread.astype(np.float32),
        gather.astype(jnp.bfloat16),
    )


def exact_dot(zero_one, x, dims):
    total = None
    for _ in range(3):
        part = x.astype(BF16)
        x = x - part.astype(F32)
        term = lax.dot_general(zero_one, part, (dims, ((), ())), preferred_element_type=F32)
        total = term if total is None else total + term
    return total


def power_kernel(
    n_dev,
    vregs,
    rows_hbm,
    u_hbm,
    got_hbm,
    pick_hbm,
    x_hbm,
    spread_hbm,
    gather_hbm,
    out_ref,
    rows_ref,
    u_ref,
    got_ref,
    pick_ref,
    x_ref,
    spread_ref,
    gather_ref,
    f_ref,
    prod_a,
    prod_b,
    sum_ref,
    accl_ref,
    acch_ref,
    sems,
):
    small = [
        (got_hbm, got_ref),
        (pick_hbm, pick_ref),
        (x_hbm, x_ref),
        (rows_hbm, rows_ref),
        (spread_hbm, spread_ref),
        (gather_hbm, gather_ref),
    ]
    size = u_ref.shape[0] // PIECES
    large = [(u_hbm.at[pl.ds(p * size, size)], u_ref.at[pl.ds(p * size, size)]) for p in range(PIECES)]
    copies = fetch(small + large, sems)
    d = device_index()
    pairs = LMAX // (2 * n_dev)
    reps = LANES // pairs
    lats = vregs * 8 * reps
    per_block = n_dev // CHUNK
    blocks = step_blocks(n_dev)
    chunks = blocks * per_block
    inline = chunks - STREAMED
    weights = chunks * CHUNK
    lane = lax.broadcasted_iota(jnp.int32, (8, LANES), 1)
    sub = lax.broadcasted_iota(jnp.int32, (8, LANES), 0)
    q = lax.rem(lane, pairs)
    head = lane < pairs
    sign = jnp.where(sub % 4 == 0, 1.0, jnp.where(sub % 4 == 2, -1.0, 0.0)).astype(F32)
    accl_ref[...] = jnp.zeros_like(accl_ref)
    acch_ref[...] = jnp.zeros_like(acch_ref)
    prod_b[...] = jnp.zeros_like(prod_b)

    for copy in copies[:3]:
        copy.wait()
    f_all = exact_dot(pick_ref[...], got_ref[...], ((1,), (0,)))

    def store(slot, value):
        f_ref[8 * slot : 8 * slot + 8, :] = value

    def load(slot):
        return f_ref[8 * slot : 8 * slot + 8, :]

    for phase in range(2):
        for odd in range(2):
            for v in range(vregs):
                for part in range(2):
                    pieces = []
                    for h in range(reps):
                        row = (2 * phase + odd) * lats + (v * reps + h) * 8
                        pieces.append(f_all[row : row + 8, part * pairs : (part + 1) * pairs])
                    value = jnp.concatenate(pieces, axis=1)
                    if odd:
                        value = value * x_ref[0, 8 * v : 8 * v + 8, :]
                    store(((phase * 2 + odd) * vregs + v) * 2 + part, value)
    base = 8 * vregs
    for phase in range(2):
        row = f_all[4 * lats + phase : 4 * lats + phase + 1, :]
        if 2 * pairs < LANES:
            row = jnp.concatenate([row, jnp.zeros((1, LANES - 2 * pairs), F32)], axis=1)
        store(base + phase, jnp.broadcast_to(row, (8, LANES)) * sign)

    def spectra_now(chunk):
        is_low = q < lax.div(chunk, per_block)

        def now(o, v, p):
            return jnp.where(is_low, load((o * vregs + v) * 2 + p), load(((2 + o) * vregs + v) * 2 + p))

        return [[[now(o, v, p) for p in range(2)] for v in range(vregs)] for o in range(2)]

    def product(s, u, now, prod_ref):
        for part in range(2):
            value = u[0] * now[s % 2][0][part]
            for v in range(1, vregs):
                value = value + u[v] * now[s % 2][v][part]
            prod_ref[part, pl.ds((s // 8) * 8 * PITCH + s % 8, 8, stride=PITCH), :] = value

    def products(chunk, prod_ref):
        now = spectra_now(chunk)
        start = pl.multiple_of((chunk - inline) * (CHUNK * 8 * vregs), CHUNK * 8 * vregs)
        for s in range(CHUNK):
            product(s, [u_ref[pl.ds(start + 8 * (s * vregs + v), 8), :] for v in range(vregs)], now, prod_ref)

    def steps(chunk, prod_ref, state):
        now = spectra_now(chunk)
        even, odd = turn_lanes(chunk, per_block, q, seed_low, list(state[:vregs]), list(state[vregs:]))
        first = pl.multiple_of(chunk * CHUNK, CHUNK)
        for s in range(0, CHUNK, 2):
            fresh_even, fresh_odd = advance(rows_ref, first + s, even, odd, x2)
            product(s, even, now, prod_ref)
            product(s + 1, fresh_odd, now, prod_ref)
            even, odd = fresh_even, fresh_odd
        return (*even, *odd)

    def reduce(chunk, prod_ref):
        for i in range(CHUNK // 8):
            for part in range(2):
                rows = [prod_ref[part, pl.ds((8 * i + s) * PITCH, 8), :] for s in range(8)]
                while len(rows) > 1:
                    rows = [a + b for a, b in zip(rows[::2], rows[1::2])]
                sum_ref[part, pl.ds(pl.multiple_of(chunk * CHUNK, CHUNK) + 8 * i, 8), :] = rows[0]

    def two_inline(h, state):
        state = steps(2 * h, prod_a, state)
        reduce(jnp.maximum(2 * h - 1, 0), prod_b)
        state = steps(2 * h + 1, prod_b, state)
        reduce(2 * h, prod_a)
        return state

    def two_streamed(h, carry):
        products(2 * h, prod_a)
        reduce(2 * h - 1, prod_b)
        products(2 * h + 1, prod_b)
        reduce(2 * h, prod_a)
        return carry

    m_low = (d + n_dev * q).astype(F32)
    x2 = [x_ref[1, 8 * v : 8 * v + 8, :] for v in range(vregs)]
    logs = [x_ref[2, 8 * v : 8 * v + 8, :] for v in range(vregs)]
    seed_low = [jnp.exp(m_low * g) for g in logs]
    seed_high = [jnp.exp(((LMAX - 1.0) - m_low) * g) for g in logs]
    for copy in copies[3:6]:
        copy.wait()
    lax.fori_loop(0, inline // 2, two_inline, (*seed_high, *([jnp.zeros((8, LANES), F32)] * vregs)))
    piece = STREAMED // PIECES
    for p in range(PIECES):
        copies[6 + p].wait()
        first = inline + p * piece
        lax.fori_loop(first // 2, (first + piece) // 2, two_streamed, 0)
    reduce(chunks - 1, prod_b)

    def packed(tau):
        re, im = sum_ref[0, pl.ds(tau, 8), :], sum_ref[1, pl.ds(tau, 8), :]
        if 2 * pairs == LANES:
            return jnp.where(head, re, im) + pltpu.roll(jnp.where(head, im, re), pairs, 1)
        step = pairs
        while step < LANES:
            re, im = re + pltpu.roll(re, step, 1), im + pltpu.roll(im, step, 1)
            step *= 2
        return jnp.where(head, re, jnp.where(lane < 2 * pairs, im, 0.0))

    def powers(first, count, with_high):
        tiles = n_dev // 8
        places = [(i, j) for j in range(count) for i in range(tiles)]
        taus = [pl.multiple_of((first + j) * n_dev, n_dev) + 8 * i for i, j in places]
        lows = [q < first + j for j in range(count)]
        flats = [load(base)] * count
        if with_high:
            flats = [jnp.where(low, load(base), load(base + 1)) for low in lows]
        values = [packed(tau) for tau in taus]
        values = [v + flats[j] for v, (_, j) in zip(values, places)]
        values = [v * v * rows_ref[pl.ds(weights + tau, 8), :] for v, tau in zip(values, taus)]
        low_parts = values
        if with_high:
            low_parts = [jnp.where(lows[j], v, 0.0) for v, (_, j) in zip(values, places)]
            high_parts = [v - low for v, low in zip(values, low_parts)]
        sums = [jnp.sum(v, axis=1, keepdims=True) for v in low_parts]
        if with_high:
            shifts = [count - 1 - j for _, j in places]
            high_parts = [pltpu.roll(v, shift, 1) if shift else v for v, shift in zip(high_parts, shifts)]
        for i in range(tiles):
            total = accl_ref[8 * i : 8 * i + 8, :]
            for j in range(count):
                target = lax.rem(3 * pairs - 1 - (first + j) + 2 * LANES, LANES)
                total = total + jnp.where(lane == target, sums[j * tiles + i], 0.0)
            accl_ref[8 * i : 8 * i + 8, :] = total
            if with_high:
                total = pltpu.roll(acch_ref[8 * i : 8 * i + 8, :], count, 1)
                for j in range(count):
                    total = total + high_parts[j * tiles + i]
                acch_ref[8 * i : 8 * i + 8, :] = total

    many = 512 // n_dev
    half = pairs // many

    def both_halves(g, carry):
        powers(g * many, many, True)
        return carry

    def low_half(g, carry):
        powers(g * many, many, False)
        return carry

    lax.fori_loop(0, half, both_halves, 0)
    lax.fori_loop(half, blocks // many, low_half, 0)
    if blocks % many:
        powers(jnp.int32(blocks - blocks % many), blocks % many, False)

    rows = lax.broadcasted_iota(jnp.int32, (n_dev, LANES), 0)

    def shifted(acc, shift):
        rolled = pltpu.roll(acc, shift, 0)
        return jnp.where(rows < shift, pltpu.roll(rolled, LANES - 1, 1), rolled)

    lanes = lax.broadcasted_iota(jnp.int32, (n_dev, LANES), 1)
    high = acch_ref[...] + pltpu.roll(acch_ref[...], LANES - pairs, 1)
    high = jnp.where(jnp.logical_and(lanes >= pairs - 1, lanes < 2 * pairs - 1), high, 0.0)
    power = shifted(accl_ref[...], d) + shifted(high, n_dev - 1 - d)
    tall = jnp.concatenate([power] * (LANES // n_dev), axis=0) * spread_ref[...]
    out_ref[...] = exact_dot(gather_ref[...], tall, ((1,), (1,)))


def power_of_orders(rows, u, got, n_dev, n_blk, lats, slots):
    pairs = LMAX // (2 * n_dev)
    vregs = lats * pairs // (8 * LANES)
    tables = [jnp.asarray(t) for t in power_tables(n_dev, n_blk, lats, slots)]
    prod = pltpu.VMEM((2, CHUNK * PITCH, LANES), F32)
    return pl.pallas_call(
        functools.partial(power_kernel, n_dev, vregs),
        out_shape=jax.ShapeDtypeStruct((LMAX // LANES, LANES), F32),
        in_specs=[ANY] * 7,
        out_specs=VMEM,
        scratch_shapes=[pltpu.VMEM(t.shape, t.dtype) for t in [rows, u, got, *tables]]
        + [
            pltpu.VMEM((8 * (8 * vregs + 2), LANES), F32),
            prod,
            prod,
            pltpu.VMEM((2, step_blocks(n_dev) * n_dev, LANES), F32),
            pltpu.VMEM((n_dev, LANES), F32),
            pltpu.VMEM((n_dev, LANES), F32),
            pltpu.SemaphoreType.DMA((6 + PIECES,)),
        ],
        compiler_params=pltpu.CompilerParams(vmem_limit_bytes=VMEM_LIMIT),
        cost_estimate=pl.CostEstimate(flops=u.size * 4, bytes_accessed=1000000, transcendentals=0),
        name="order_power",
    )(rows, u, got, *tables)


def on_device(pixels, block_ids, block_mask, model_cl):
    n_blk = lax.axis_size("blk")
    n_mblk = lax.axis_size("mblk")
    n_dev = n_blk * n_mblk
    slots = pixels.shape[0]
    cycles = n_blk * slots // SEGS
    lats = slots * n_dev // SEGS // 2
    pairs = LMAX // (2 * n_dev)

    rows, u = legendre_rows(n_dev, lats)
    sent = cycle_spectra(pixels, block_ids, block_mask, n_dev, n_blk)
    got = lax.all_to_all(sent.reshape(n_dev, 2 * cycles, 2 * pairs), ("blk", "mblk"), 0, 0, tiled=True)
    got = got.reshape(n_dev * 2 * cycles, 2 * pairs)
    power = power_of_orders(rows, u, got, n_dev, n_blk, lats, slots)

    for axis, size in (("mblk", n_mblk), ("blk", n_blk)):
        bit = 1
        while bit < size:
            power = power + lax.ppermute(power, axis, [(i, i ^ bit) for i in range(size)])
            bit *= 2
    pseudo_cl = power.reshape(LMAX)
    rel_error = (pseudo_cl - model_cl) / model_cl
    misfit = jnp.mean(rel_error * rel_error)
    return (pseudo_cl, misfit)


def solution(mesh):
    in_specs = (P(("blk", "mblk"), None), P(("blk", "mblk")), P(("blk", "mblk")), P())
    out_specs = (P(), P())
    return jax.shard_map(
        on_device, mesh=mesh, in_specs=in_specs, out_specs=out_specs, check_vma=False
    )
```

time: 153 us -> 58.7 us (0.38)
  Pallas kernels: 104 us -> 28.7 us
  waiting for transfers between devices: 22.8 us -> 8.99 us
  local copies, waits for them, and re-layouts: 11.5 us -> 0.65 us
  starting transfers between devices: 9.74 us -> 15.6 us
    pallas_call x2 -> x3, Pallas kernels: 104 us -> 28.7 us  [the longest x1 13.4 us: legendre_rows(): pl.pallas_call(functools.partial(recurrence_kernel, n_dev, vregs, float(2...]
    unnamed x26 -> x4, local copies, waits for them, and re-layouts: 11.5 us -> 0.65 us
    all_to_all x1, waiting for transfers between devices: 8.22 us -> 0.01 us  [on_device(): lax.all_to_all(sent.reshape(n_dev, 2 * cycles, 2 * pairs), ('blk', 'mblk'...]
    ppermute x5, starting transfers between devices: 2.44 us -> 8.32 us  [on_device(): lax.ppermute(power, axis, [(i, i ^ bit) for i in range(size)])]
    ppermute x5, waiting for transfers between devices: 14.6 us -> 8.99 us  [on_device(): lax.ppermute(power, axis, [(i, i ^ bit) for i in range(size)])]
  transfers between devices with their start and end apart: 6 -> 6, of which waited for: 6 -> 5; matrix products, arithmetic and copies ran while one was open for 0% -> 0% of each run, Pallas kernels for 0% -> 23%
where the time goes in v2:
time: 58.7 us; the launch traced here: 58.4 us
  Pallas kernels  28.7 us (49%)
  starting transfers between devices  15.6 us (27%)
  waiting for transfers between devices  8.99 us (15%)
  between operations  2.46 us (4%)
  other arithmetic  1.94 us (3%)
  local copies, waits for them, and re-layouts  0.65 us (1%)
    pallas_call x1, Pallas kernels, legendre_rows(): pl.pallas_call(functools.partial(recurrence_kernel, n_dev, vregs, float(2...  13.4 us
    pallas_call x1, Pallas kernels, power_of_orders(): pl.pallas_call(functools.partial(power_kernel, n_dev, vregs), out_shape=j...  12.3 us
    ppermute x5, waiting for transfers between devices, on_device(): lax.ppermute(power, axis, [(i, i ^ bit) for i in range(size)])  8.99 us
    ppermute x5, starting transfers between devices, on_device(): lax.ppermute(power, axis, [(i, i ^ bit) for i in range(size)])  8.32 us
    all_to_all x1, starting transfers between devices, on_device(): lax.all_to_all(sent.reshape(n_dev, 2 * cycles, 2 * pairs), ('blk', 'mblk'...  7.3 us
    pallas_call x1, Pallas kernels, cycle_spectra(): pl.pallas_call(functools.partial(dft_kernel, n_dev, n_blk), out_shape=jax...  3.02 us
    reduce_sum x1, other arithmetic, on_device(): misfit = jnp.mean(rel_error * rel_error)  1.21 us
  transfers between devices with their start and end apart: 6, of which 5 were waited for; matrix products, arithmetic and copies ran while one was open for 0% of the time, Pallas kernels for 23%

profile of v2, /device:TPU:0, one launch (start us, length us, event | category | flops | bytes accessed | tf_op | source)
XLA Modules:
  0.0 58.4 jit_solution(2385567916088569651)
XLA Ops:
  0.6 3.0 %cycle_dft.1 = f32[256,128]{1,0:T(8,128)} custom-call(s32[16]{0:T(128)} %ids_ref.1, s32[16]{0:T(128)} %mask_ref.1, f32[16,1024]{1,0:T(8,128)} %pix_hbm.1, bf16[128,96]{1,0:T(8,128)(2,1)} %constant.31.clone.first_hbm, f32[4,32,256]{2,1,0:T(8,128)} %constant.32.clone.turn_hbm, bf16[2,512,256]{2,1,0:T(8,128)(2,1)} %constant.33.clone.second_hbm, ...), custom_call_target="tpu_custom_call" | custom-call | tf_op jit(solution)/shard_map/cycle_dft/pallas_call | solution.py:165
  3.7 7.3 %all-to-all-start = ((f32[32,8,128]{2,1,0:T(8,128)}), f32[32,8,128]{2,1,0:T(8,128)S(1)}, u32[]{:S(2)}, u32[]{:S(2)}) async-start(f32[32,8,128]{2,1,0:T(8,128)} %bitcast.6), calls=%async_computation | async-start | bytes 262144 | tf_op jit(solution)/shard_map/all_to_all | solution.py:656
  11.0 13.4 %legendre_rows.1 = (f32[8320,128]{1,0:T(8,128)}, f32[40960,128]{1,0:T(8,128)}) custom-call(f32[4160,128]{1,0:T(8,128)} %constant.27.clone.rise_hbm, f32[4224,128]{1,0:T(8,128)} %constant.28.clone.low_hbm, f32[4224,128]{1,0:T(8,128)} %constant.29.clone.high_hbm, f32[3,16,128]{2,1,0:T(8,128)} %constant.30.clone.x_hbm), custom_call_target="tpu_custom_call" | custom-call | flops 68157440 | bytes 30000000 | tf_op jit(solution)/shard_map/legendre_rows/pallas_call | solution.py:335
  24.4 0.0 all-to-all-done
  24.4 0.0 copy-start
  24.4 0.6 %copy-done = f32[32,8,128]{2,1,0:T(8,128)} copy-done((f32[32,8,128]{2,1,0:T(8,128)}, f32[32,8,128]{2,1,0:T(8,128)S(1)}, u32[]{:S(2)}) %copy-start) | copy-done | bytes 131096
  25.0 0.0 copy-start.1
  25.0 12.3 %order_power.1 = f32[32,128]{1,0:T(8,128)} custom-call(f32[8320,128]{1,0:T(8,128)} %get-tuple-element.4.rows_hbm, f32[40960,128]{1,0:T(8,128)} %get-tuple-element.5.u_hbm, f32[256,128]{1,0:T(8,128)} %bitcast.5, bf16[144,256]{1,0:T(8,128)(2,1)} %constant.35.clone.pick_hbm, f32[3,16,128]{2,1,0:T(8,128)} %constant.30.clone.x_hbm, ...), custom_call_target="tpu_custom_call" | custom-call | flops 20971520 | bytes 1000000 | tf_op jit(solution)/shard_map/order_power/pallas_call | solution.py:624
  37.3 0.3 collective-permute-start
  37.7 1.1 %collective-permute-done = f32[32,128]{1,0:T(8,128)S(1)} collective-permute-done((f32[32,128]{1,0:T(8,128)}, f32[32,128]{1,0:T(8,128)S(1)}, u32[]{:S(2)}, u32[]{:S(2)}) %collective-permute-start) | collective-permute-done | bytes 16416 | tf_op jit(solution)/shard_map/ppermute | solution.py:663
  38.8 0.7 %add.15 = f32[32,128]{1,0:T(8,128)S(1)} add(f32[32,128]{1,0:T(8,128)} %order_power.1, f32[32,128]{1,0:T(8,128)S(1)} %collective-permute-done) | non-fusion elementwise | flops 4096 | bytes 49152 | tf_op jit(solution)/shard_map/add | solution.py:663
  39.5 1.8 %collective-permute-start.1 = (f32[32,128]{1,0:T(8,128)S(1)}, f32[32,128]{1,0:T(8,128)S(1)}, u32[]{:S(2)}, u32[]{:S(2)}) collective-permute-start(f32[32,128]{1,0:T(8,128)S(1)} %add.15), channel_id=1, source_target_pairs={{0,2},{1,3},{2,0},{3,1},{4,6},{5,7},{6,4},{7,5},{8,10},{9,11},{10,... | collective-permute-start | bytes 49160 | tf_op jit(solution)/shard_map/ppermute | solution.py:663
  41.3 2.0 %collective-permute-done.1 = f32[32,128]{1,0:T(8,128)S(1)} collective-permute-done((f32[32,128]{1,0:T(8,128)S(1)}, f32[32,128]{1,0:T(8,128)S(1)}, u32[]{:S(2)}, u32[]{:S(2)}) %collective-permute-start.1) | collective-permute-done | bytes 16416 | tf_op jit(solution)/shard_map/ppermute | solution.py:663
  43.3 1.8 %collective-permute-start.2 = (f32[32,128]{1,0:T(8,128)S(1)}, f32[32,128]{1,0:T(8,128)S(1)}, u32[]{:S(2)}, u32[]{:S(2)}) collective-permute-start(f32[32,128]{1,0:T(8,128)S(1)} %add.16), channel_id=1, source_target_pairs={{0,4},{1,5},{2,6},{3,7},{4,0},{5,1},{6,2},{7,3},{8,12},{9,13},{10,... | collective-permute-start | bytes 49160 | tf_op jit(solution)/shard_map/ppermute | solution.py:663
  45.0 1.9 %collective-permute-done.2 = f32[32,128]{1,0:T(8,128)S(1)} collective-permute-done((f32[32,128]{1,0:T(8,128)S(1)}, f32[32,128]{1,0:T(8,128)S(1)}, u32[]{:S(2)}, u32[]{:S(2)}) %collective-permute-start.2) | collective-permute-done | bytes 16416 | tf_op jit(solution)/shard_map/ppermute | solution.py:663
  47.0 2.7 %collective-permute-start.3 = (f32[32,128]{1,0:T(8,128)S(1)}, f32[32,128]{1,0:T(8,128)S(1)}, u32[]{:S(2)}, u32[]{:S(2)}) collective-permute-start(f32[32,128]{1,0:T(8,128)S(1)} %add.17), channel_id=1, source_target_pairs={{0,8},{1,9},{2,10},{3,11},{4,12},{5,13},{6,14},{7,15},{8,0},{9,1},... | collective-permute-start | bytes 49160 | tf_op jit(solution)/shard_map/ppermute | solution.py:663
  49.7 2.0 %collective-permute-done.3 = f32[32,128]{1,0:T(8,128)S(1)} collective-permute-done((f32[32,128]{1,0:T(8,128)S(1)}, f32[32,128]{1,0:T(8,128)S(1)}, u32[]{:S(2)}, u32[]{:S(2)}) %collective-permute-start.3) | collective-permute-done | bytes 16416 | tf_op jit(solution)/shard_map/ppermute | solution.py:663
  51.6 1.8 %collective-permute-start.4 = (f32[32,128]{1,0:T(8,128)S(1)}, f32[32,128]{1,0:T(8,128)S(1)}, u32[]{:S(2)}, u32[]{:S(2)}) collective-permute-start(f32[32,128]{1,0:T(8,128)S(1)} %add.18), channel_id=1, source_target_pairs={{0,16},{16,0},{1,17},{17,1},{2,18},{18,2},{3,19},{19,3},{4,20},{20... | collective-permute-start | bytes 49160 | tf_op jit(solution)/shard_map/ppermute | solution.py:663
  53.4 2.0 %collective-permute-done.4 = f32[32,128]{1,0:T(8,128)S(1)} collective-permute-done((f32[32,128]{1,0:T(8,128)S(1)}, f32[32,128]{1,0:T(8,128)S(1)}, u32[]{:S(2)}, u32[]{:S(2)}) %collective-permute-start.4) | collective-permute-done | bytes 16416 | tf_op jit(solution)/shard_map/ppermute | solution.py:663
  55.4 0.0 copy-done.1
  55.4 1.2 %fusion.1 = (f32[]{:T(128)}, f32[4096]{0:T(1024)}) fusion(f32[4096]{0:T(1024)S(1)} %copy-done.1, f32[32,128]{1,0:T(8,128)S(1)} %add.18, f32[32,128]{1,0:T(8,128)S(1)} %collective-permute-done.4), kind=kLoop, calls=%fused_computation.3 | loop fusion | flops 20479 | bytes 65540 | tf_op jit(solution)/shard_map/reduce_sum | solution.py:667
  (3 shorter events, 0.0 us)
Async XLA Ops:
  3.7 20.7 %all-to-all-start = ((f32[32,8,128]{2,1,0:T(8,128)}), f32[32,8,128]{2,1,0:T(8,128)S(1)}, u32[]{:S(2)}, u32[]{:S(2)}) async-start(f32[32,8,128]{2,1,0:T(8,128)} %bitcast.6), calls=%async_computation | async-start | bytes 262144 | tf_op jit(solution)/shard_map/all_to_all | solution.py:656
  24.4 0.6 %copy-start = (f32[32,8,128]{2,1,0:T(8,128)}, f32[32,8,128]{2,1,0:T(8,128)S(1)}, u32[]{:S(2)}) copy-start(f32[32,8,128]{2,1,0:T(8,128)S(1)} %all-to-all-done) | copy-start | bytes 393220
  25.0 30.4 %copy-start.1 = (f32[4096]{0:T(1024)S(1)}, f32[4096]{0:T(1024)}, u32[]{:S(2)}) copy-start(f32[4096]{0:T(1024)} %param.19) | copy-start | bytes 49156
  37.3 1.5 %collective-permute-start = (f32[32,128]{1,0:T(8,128)}, f32[32,128]{1,0:T(8,128)S(1)}, u32[]{:S(2)}, u32[]{:S(2)}) collective-permute-start(f32[32,128]{1,0:T(8,128)} %order_power.1), channel_id=1, source_target_pairs={{0,1},{1,0},{2,3},{3,2},{4,5},{5,4},{6,7},{7,6},{8,9},{9,8},{10,11... | collective-permute-start | bytes 49160 | tf_op jit(solution)/shard_map/ppermute | solution.py:663
  39.5 3.7 %collective-permute-start.1 = (f32[32,128]{1,0:T(8,128)S(1)}, f32[32,128]{1,0:T(8,128)S(1)}, u32[]{:S(2)}, u32[]{:S(2)}) collective-permute-start(f32[32,128]{1,0:T(8,128)S(1)} %add.15), channel_id=1, source_target_pairs={{0,2},{1,3},{2,0},{3,1},{4,6},{5,7},{6,4},{7,5},{8,10},{9,11},{10,... | collective-permute-start | bytes 49160 | tf_op jit(solution)/shard_map/ppermute | solution.py:663
  43.3 3.7 %collective-permute-start.2 = (f32[32,128]{1,0:T(8,128)S(1)}, f32[32,128]{1,0:T(8,128)S(1)}, u32[]{:S(2)}, u32[]{:S(2)}) collective-permute-start(f32[32,128]{1,0:T(8,128)S(1)} %add.16), channel_id=1, source_target_pairs={{0,4},{1,5},{2,6},{3,7},{4,0},{5,1},{6,2},{7,3},{8,12},{9,13},{10,... | collective-permute-start | bytes 49160 | tf_op jit(solution)/shard_map/ppermute | solution.py:663
  47.0 4.6 %collective-permute-start.3 = (f32[32,128]{1,0:T(8,128)S(1)}, f32[32,128]{1,0:T(8,128)S(1)}, u32[]{:S(2)}, u32[]{:S(2)}) collective-permute-start(f32[32,128]{1,0:T(8,128)S(1)} %add.17), channel_id=1, source_target_pairs={{0,8},{1,9},{2,10},{3,11},{4,12},{5,13},{6,14},{7,15},{8,0},{9,1},... | collective-permute-start | bytes 49160 | tf_op jit(solution)/shard_map/ppermute | solution.py:663
  51.6 3.7 %collective-permute-start.4 = (f32[32,128]{1,0:T(8,128)S(1)}, f32[32,128]{1,0:T(8,128)S(1)}, u32[]{:S(2)}, u32[]{:S(2)}) collective-permute-start(f32[32,128]{1,0:T(8,128)S(1)} %add.18), channel_id=1, source_target_pairs={{0,16},{16,0},{1,17},{17,1},{2,18},{18,2},{3,19},{19,3},{4,20},{20... | collective-permute-start | bytes 49160 | tf_op jit(solution)/shard_map/ppermute | solution.py:663

commit v3 on v2

--- a/solution.py
+++ b/solution.py
@@ -17,9 +17,10 @@
 LANES = 128
 CHUNK = 32
 PITCH = 12
-STREAMED = 80
-PIECES = 5
+STREAMED = 48
+PIECES = 4
 VMEM_LIMIT = 56 * 1024 * 1024
+POWER_VMEM = 51 * 1024 * 1024
 F32 = jnp.float32
 BF16 = jnp.bfloat16
 ANY = pl.BlockSpec(memory_space=pl.ANY)
@@ -245,14 +246,20 @@
     u_ref,
     sems,
 ):
-    copies = fetch([(rise_hbm, rise_ref), (low_hbm, low_ref), (high_hbm, high_ref), (x_hbm, x_ref)], sems)
-    d = device_index()
     pairs = LMAX // (2 * n_dev)
     per_block = n_dev // CHUNK
     chunks = step_blocks(n_dev) * per_block
-    inline = chunks - STREAMED
     total = chunks * CHUNK
-    many = max(n for n in range(1, 13) if chunks % n == 0)
+    cut = STREAMED * CHUNK
+    parts = [(x_hbm, x_ref)]
+    for start, stop in ((0, cut), (cut, total)):
+        for src, dst in ((rise_hbm, rise_ref), (low_hbm, low_ref), (high_hbm, high_ref)):
+            reach = 0 if src is rise_hbm else 2 * n_dev
+            first = start + reach if start else 0
+            span = pl.ds(first, stop + reach - first)
+            parts.append((src.at[span], dst.at[span]))
+    copies = fetch(parts, sems)
+    d = device_index()
     lane = lax.broadcasted_iota(jnp.int32, (8, LANES), 1)
     sub = lax.broadcasted_iota(jnp.int32, (8, LANES), 0)
     q = lax.rem(lane, pairs)
@@ -262,37 +269,42 @@
     weight_high = jnp.full((8, LANES), 2.0 / pixel_total, F32)
     l_low = sub.astype(F32) + (d.astype(F32) - n_dev)
     l_high = sub.astype(F32) + m_high
-    for copy in copies:
+    for copy in copies[:4]:
         copy.wait()
     x2 = [x_ref[1, 8 * v : 8 * v + 8, :] for v in range(vregs)]
     logs = [x_ref[2, 8 * v : 8 * v + 8, :] for v in range(vregs)]
     seed_low = [jnp.exp(m_low * g) for g in logs]
     seed_high = [jnp.exp(m_high * g) for g in logs]
 
-    def coefficients(first, carry):
-        fresh = []
-        for step in range(many):
-            chunk = first * many + step
-            is_low = q < lax.div(chunk, per_block)
-            weight = jnp.where(is_low, weight_low, weight_high)
-            start = jnp.where(is_low, l_low, l_high) + (chunk * CHUNK).astype(F32)
-            for i in range(CHUNK // 8):
-                tau = pl.multiple_of(chunk * CHUNK, CHUNK) + 8 * i
-                low = low_ref[pl.ds(tau + 2 * d, 8), :]
-                high = high_ref[pl.ds(tau + 2 * (n_dev - 1 - d), 8), :]
-                product = rise_ref[pl.ds(tau, 8), :] * jnp.where(is_low, low, high)
-                degree = start + 8.0 * i
-                coef = product * (degree * math.pi + 0.5 * math.pi)
-                fresh.append((tau, coef, jnp.where(degree < LMAX, product * weight, 0.0)))
-        for tau, coef, weight in fresh:
-            rows_ref[pl.ds(tau, 8), :] = coef
-            rows_ref[pl.ds(total + tau, 8), :] = weight
-        return carry
+    def coefficients(start, stop):
+        many = max(n for n in range(1, 13) if (stop - start) % n == 0)
+
+        def some(group, carry):
+            fresh = []
+            for step in range(many):
+                chunk = start + group * many + step
+                is_low = q < lax.div(chunk, per_block)
+                weight = jnp.where(is_low, weight_low, weight_high)
+                first = jnp.where(is_low, l_low, l_high) + (chunk * CHUNK).astype(F32)
+                for i in range(CHUNK // 8):
+                    tau = pl.multiple_of(chunk * CHUNK, CHUNK) + 8 * i
+                    low = low_ref[pl.ds(tau + 2 * d, 8), :]
+                    high = high_ref[pl.ds(tau + 2 * (n_dev - 1 - d), 8), :]
+                    product = rise_ref[pl.ds(tau, 8), :] * jnp.where(is_low, low, high)
+                    degree = first + 8.0 * i
+                    coef = product * (degree * math.pi + 0.5 * math.pi)
+                    fresh.append((tau, coef, jnp.where(degree < LMAX, product * weight, 0.0)))
+            for tau, coef, weight in fresh:
+                rows_ref[pl.ds(tau, 8), :] = coef
+                rows_ref[pl.ds(total + tau, 8), :] = weight
+            return carry
+
+        lax.fori_loop(0, (stop - start) // many, some, 0)
 
     def steps(chunk, state):
         even, odd = turn_lanes(chunk, per_block, q, seed_low, list(state[:vregs]), list(state[vregs:]))
         first = pl.multiple_of(chunk * CHUNK, CHUNK)
-        start = pl.multiple_of((chunk - inline) * (CHUNK * 8 * vregs), CHUNK * 8 * vregs)
+        start = pl.multiple_of(chunk * (CHUNK * 8 * vregs), CHUNK * 8 * vregs)
         for s in range(0, CHUNK, 2):
             fresh_even, fresh_odd = advance(rows_ref, first + s, even, odd, x2)
             for v in range(vregs):
@@ -301,26 +313,31 @@
             even, odd = fresh_even, fresh_odd
         return (*even, *odd)
 
-    def plain_steps(chunk, state):
-        even, odd = turn_lanes(chunk, per_block, q, seed_low, list(state[:vregs]), list(state[vregs:]))
-        first = pl.multiple_of(chunk * CHUNK, CHUNK)
-        for s in range(0, CHUNK, 2):
-            even, odd = advance(rows_ref, first + s, even, odd, x2)
-        return (*even, *odd)
-
-    lax.fori_loop(0, chunks // many, coefficients, 0)
-    out = [pltpu.make_async_copy(rows_ref, rows_hbm, sems.at[4])]
-    out[0].start()
+    coefficients(0, STREAMED)
     zero = jnp.zeros((8, LANES), F32)
     state = (*seed_high, *([zero] * vregs))
-    state = lax.fori_loop(0, inline // 2, lambda h, s: plain_steps(2 * h + 1, plain_steps(2 * h, s)), state)
     piece = STREAMED // PIECES
+    size = piece * CHUNK * 8 * vregs
+    out = []
+
+    def send(src, dst, sem):
+        out.append(pltpu.make_async_copy(src, dst, sems.at[sem]))
+        out[-1].start()
+
     for p in range(PIECES):
-        first = inline + p * piece
+        first = p * piece
         state = lax.fori_loop(first // 2, (first + piece) // 2, lambda h, s: steps(2 * h + 1, steps(2 * h, s)), state)
-        size = piece * CHUNK * 8 * vregs
-        out.append(pltpu.make_async_copy(u_ref.at[pl.ds(p * size, size)], u_hbm.at[pl.ds(p * size, size)], sems.at[5 + p]))
-        out[-1].start()
+        extra = 0
+        if p == PIECES - 1:
+            extra = 16 * vregs
+            for v in range(2 * vregs):
+                u_ref[PIECES * size + 8 * v : PIECES * size + 8 * v + 8, :] = state[v]
+        span = pl.ds(p * size, size + extra)
+        send(u_ref.at[span], u_hbm.at[span], 7 + p)
+    for copy in copies[4:]:
+        copy.wait()
+    coefficients(STREAMED, chunks)
+    send(rows_ref.at[pl.ds(cut, 2 * total - cut)], rows_hbm, 7 + PIECES)
     for copy in out:
         copy.wait()
 
@@ -329,18 +346,20 @@
     pairs = LMAX // (2 * n_dev)
     vregs = lats * pairs // (8 * LANES)
     total = step_blocks(n_dev) * n_dev
+    cut = STREAMED * CHUNK
     tables = [jnp.asarray(t) for t in recurrence_tables(n_dev, lats)]
     rows = jax.ShapeDtypeStruct((2 * total, LANES), F32)
-    u = jax.ShapeDtypeStruct((STREAMED * CHUNK * 8 * vregs, LANES), F32)
+    rest = jax.ShapeDtypeStruct((2 * total - cut, LANES), F32)
+    u = jax.ShapeDtypeStruct((cut * 8 * vregs + 16 * vregs, LANES), F32)
     return pl.pallas_call(
         functools.partial(recurrence_kernel, n_dev, vregs, float(2 * lats * CYCLE_PIX)),
-        out_shape=(rows, u),
+        out_shape=(rest, u),
         in_specs=[ANY] * 4,
         out_specs=(ANY, ANY),
         scratch_shapes=[pltpu.VMEM(t.shape, t.dtype) for t in [*tables, rows, u]]
-        + [pltpu.SemaphoreType.DMA((5 + PIECES,))],
+        + [pltpu.SemaphoreType.DMA((8 + PIECES,))],
         compiler_params=pltpu.CompilerParams(vmem_limit_bytes=VMEM_LIMIT),
-        cost_estimate=pl.CostEstimate(flops=total * 8 * LANES * vregs * 8, bytes_accessed=30000000, transcendentals=0),
+        cost_estimate=pl.CostEstimate(flops=total * 8 * LANES * vregs * 8, bytes_accessed=25000000, transcendentals=0),
         name="legendre_rows",
     )(*tables)
 
@@ -397,19 +416,14 @@
     vregs,
     rows_hbm,
     u_hbm,
-    got_hbm,
-    pick_hbm,
-    x_hbm,
-    spread_hbm,
-    gather_hbm,
-    out_ref,
-    rows_ref,
-    u_ref,
     got_ref,
     pick_ref,
     x_ref,
     spread_ref,
     gather_ref,
+    out_ref,
+    rows_ref,
+    u_ref,
     f_ref,
     prod_a,
     prod_b,
@@ -418,26 +432,25 @@
     acch_ref,
     sems,
 ):
-    small = [
-        (got_hbm, got_ref),
-        (pick_hbm, pick_ref),
-        (x_hbm, x_ref),
-        (rows_hbm, rows_ref),
-        (spread_hbm, spread_ref),
-        (gather_hbm, gather_ref),
-    ]
-    size = u_ref.shape[0] // PIECES
-    large = [(u_hbm.at[pl.ds(p * size, size)], u_ref.at[pl.ds(p * size, size)]) for p in range(PIECES)]
-    copies = fetch(small + large, sems)
+    pairs = LMAX // (2 * n_dev)
+    all_steps = step_blocks(n_dev) * n_dev
+    cut = STREAMED * CHUNK
+    size = cut // PIECES * 8 * vregs
+    spans = [pl.ds(p * size, size) for p in range(PIECES)]
+    states, coefs, weights = pl.ds(PIECES * size, 16 * vregs), pl.ds(0, all_steps - cut), pl.ds(all_steps - cut, all_steps)
+    copies = fetch(
+        [
+            (u_hbm.at[states], u_ref.at[states]),
+            (rows_hbm.at[coefs], rows_ref.at[coefs]),
+        ],
+        sems,
+    )
     d = device_index()
-    pairs = LMAX // (2 * n_dev)
     reps = LANES // pairs
     lats = vregs * 8 * reps
     per_block = n_dev // CHUNK
     blocks = step_blocks(n_dev)
     chunks = blocks * per_block
-    inline = chunks - STREAMED
-    weights = chunks * CHUNK
     lane = lax.broadcasted_iota(jnp.int32, (8, LANES), 1)
     sub = lax.broadcasted_iota(jnp.int32, (8, LANES), 0)
     q = lax.rem(lane, pairs)
@@ -447,8 +460,6 @@
     acch_ref[...] = jnp.zeros_like(acch_ref)
     prod_b[...] = jnp.zeros_like(prod_b)
 
-    for copy in copies[:3]:
-        copy.wait()
     f_all = exact_dot(pick_ref[...], got_ref[...], ((1,), (0,)))
 
     def store(slot, value):
@@ -493,14 +504,14 @@
 
     def products(chunk, prod_ref):
         now = spectra_now(chunk)
-        start = pl.multiple_of((chunk - inline) * (CHUNK * 8 * vregs), CHUNK * 8 * vregs)
+        start = pl.multiple_of(chunk * (CHUNK * 8 * vregs), CHUNK * 8 * vregs)
         for s in range(CHUNK):
             product(s, [u_ref[pl.ds(start + 8 * (s * vregs + v), 8), :] for v in range(vregs)], now, prod_ref)
 
     def steps(chunk, prod_ref, state):
         now = spectra_now(chunk)
         even, odd = turn_lanes(chunk, per_block, q, seed_low, list(state[:vregs]), list(state[vregs:]))
-        first = pl.multiple_of(chunk * CHUNK, CHUNK)
+        first = pl.multiple_of((chunk - STREAMED) * CHUNK, CHUNK)
         for s in range(0, CHUNK, 2):
             fresh_even, fresh_odd = advance(rows_ref, first + s, even, odd, x2)
             product(s, even, now, prod_ref)
@@ -518,32 +529,39 @@
 
     def two_inline(h, state):
         state = steps(2 * h, prod_a, state)
-        reduce(jnp.maximum(2 * h - 1, 0), prod_b)
+        reduce(jnp.maximum(2 * h - 1, STREAMED), prod_b)
         state = steps(2 * h + 1, prod_b, state)
         reduce(2 * h, prod_a)
         return state
 
     def two_streamed(h, carry):
         products(2 * h, prod_a)
-        reduce(2 * h - 1, prod_b)
+        reduce(jnp.maximum(2 * h - 1, 0), prod_b)
         products(2 * h + 1, prod_b)
         reduce(2 * h, prod_a)
         return carry
 
     m_low = (d + n_dev * q).astype(F32)
     x2 = [x_ref[1, 8 * v : 8 * v + 8, :] for v in range(vregs)]
-    logs = [x_ref[2, 8 * v : 8 * v + 8, :] for v in range(vregs)]
-    seed_low = [jnp.exp(m_low * g) for g in logs]
-    seed_high = [jnp.exp(((LMAX - 1.0) - m_low) * g) for g in logs]
-    for copy in copies[3:6]:
+    seed_low = [jnp.exp(m_low * x_ref[2, 8 * v : 8 * v + 8, :]) for v in range(vregs)]
+    for copy in copies:
         copy.wait()
-    lax.fori_loop(0, inline // 2, two_inline, (*seed_high, *([jnp.zeros((8, LANES), F32)] * vregs)))
+    moved = [(u_hbm.at[span], u_ref.at[span]) for span in spans] + [
+        (rows_hbm.at[weights], rows_ref.at[weights]),
+    ]
+    copies = [pltpu.make_async_copy(src, dst, sems.at[2 + i]) for i, (src, dst) in enumerate(moved)]
+    for copy in copies:
+        copy.start()
+    state = [u_ref[PIECES * size + 8 * v : PIECES * size + 8 * v + 8, :] for v in range(2 * vregs)]
+    lax.fori_loop(STREAMED // 2, chunks // 2, two_inline, tuple(state))
+    reduce(chunks - 1, prod_b)
     piece = STREAMED // PIECES
     for p in range(PIECES):
-        copies[6 + p].wait()
-        first = inline + p * piece
-        lax.fori_loop(first // 2, (first + piece) // 2, two_streamed, 0)
-    reduce(chunks - 1, prod_b)
+        copies[p].wait()
+        lax.fori_loop(p * piece // 2, (p + 1) * piece // 2, two_streamed, 0)
+    reduce(STREAMED - 1, prod_b)
+    for copy in copies[PIECES:]:
+        copy.wait()
 
     def packed(tau):
         re, im = sum_ref[0, pl.ds(tau, 8), :], sum_ref[1, pl.ds(tau, 8), :]
@@ -565,7 +583,7 @@
             flats = [jnp.where(low, load(base), load(base + 1)) for low in lows]
         values = [packed(tau) for tau in taus]
         values = [v + flats[j] for v, (_, j) in zip(values, places)]
-        values = [v * v * rows_ref[pl.ds(weights + tau, 8), :] for v, tau in zip(values, taus)]
+        values = [v * v * rows_ref[pl.ds(all_steps - cut + tau, 8), :] for v, tau in zip(values, taus)]
         low_parts = values
         if with_high:
             low_parts = [jnp.where(lows[j], v, 0.0) for v, (_, j) in zip(values, places)]
@@ -624,9 +642,9 @@
     return pl.pallas_call(
         functools.partial(power_kernel, n_dev, vregs),
         out_shape=jax.ShapeDtypeStruct((LMAX // LANES, LANES), F32),
-        in_specs=[ANY] * 7,
+        in_specs=[ANY] * 2 + [VMEM] * 5,
         out_specs=VMEM,
-        scratch_shapes=[pltpu.VMEM(t.shape, t.dtype) for t in [rows, u, got, *tables]]
+        scratch_shapes=[pltpu.VMEM(t.shape, t.dtype) for t in [rows, u]]
         + [
             pltpu.VMEM((8 * (8 * vregs + 2), LANES), F32),
             prod,
@@ -634,9 +652,9 @@
             pltpu.VMEM((2, step_blocks(n_dev) * n_dev, LANES), F32),
             pltpu.VMEM((n_dev, LANES), F32),
             pltpu.VMEM((n_dev, LANES), F32),
-            pltpu.SemaphoreType.DMA((6 + PIECES,)),
+            pltpu.SemaphoreType.DMA((3 + PIECES,)),
         ],
-        compiler_params=pltpu.CompilerParams(vmem_limit_bytes=VMEM_LIMIT),
+        compiler_params=pltpu.CompilerParams(vmem_limit_bytes=POWER_VMEM),
         cost_estimate=pl.CostEstimate(flops=u.size * 4, bytes_accessed=1000000, transcendentals=0),
         name="order_power",
     )(rows, u, got, *tables)

time: 58.7 us -> 51.3 us (0.87)
  Pallas kernels: 28.7 us -> 22.9 us
  other arithmetic: 1.94 us -> 1.23 us
  local copies, waits for them, and re-layouts: 0.65 us -> 0.03 us
    pallas_call x1, Pallas kernels: 13.4 us -> 8.13 us  [legendre_rows(): pl.pallas_call(functools.partial(recurrence_kernel, n_dev, vregs, float(2...]
    add x4, other arithmetic: 0.73 us -> 0.02 us  [on_device(): power + lax.ppermute(power, axis, [(i, i ^ bit) for i in range(size)])]
    unnamed x4 -> x10, local copies, waits for them, and re-layouts: 0.65 us -> 0.03 us
  transfers between devices with their start and end apart: 6 -> 6, of which waited for: 5 -> 5; matrix products, arithmetic and copies ran while one was open for 0% -> 0% of each run, Pallas kernels for 23% -> 16%
where the time goes in v3:
time: 51.3 us; the launch traced here: 51.1 us
  Pallas kernels  22.9 us (45%)
  starting transfers between devices  15.6 us (30%)
  waiting for transfers between devices  8.83 us (17%)
  between operations  2.5 us (5%)
  other arithmetic  1.23 us (2%)
    pallas_call x1, Pallas kernels, power_of_orders(): pl.pallas_call(functools.partial(power_kernel, n_dev, vregs), out_shape=j...  11.8 us
    ppermute x5, waiting for transfers between devices, on_device(): lax.ppermute(power, axis, [(i, i ^ bit) for i in range(size)])  8.8 us
    ppermute x5, starting transfers between devices, on_device(): lax.ppermute(power, axis, [(i, i ^ bit) for i in range(size)])  8.31 us
    pallas_call x1, Pallas kernels, legendre_rows(): pl.pallas_call(functools.partial(recurrence_kernel, n_dev, vregs, float(2...  8.13 us
    all_to_all x1, starting transfers between devices, on_device(): lax.all_to_all(sent.reshape(n_dev, 2 * cycles, 2 * pairs), ('blk', 'mblk'...  7.31 us
    pallas_call x1, Pallas kernels, cycle_spectra(): pl.pallas_call(functools.partial(dft_kernel, n_dev, n_blk), out_shape=jax...  3.01 us
    reduce_sum x1, other arithmetic, on_device(): misfit = jnp.mean(rel_error * rel_error)  1.21 us
  transfers between devices with their start and end apart: 6, of which 5 were waited for; matrix products, arithmetic and copies ran while one was open for 0% of the time, Pallas kernels for 16%

profile of v3, /device:TPU:0, one launch (start us, length us, event | category | flops | bytes accessed | tf_op | source)
XLA Modules:
  0.0 51.1 jit_solution(8036392065401173995)
XLA Ops:
  0.6 3.0 %cycle_dft.1 = f32[256,128]{1,0:T(8,128)} custom-call(s32[16]{0:T(128)} %ids_ref.1, s32[16]{0:T(128)} %mask_ref.1, f32[16,1024]{1,0:T(8,128)} %pix_hbm.1, bf16[128,96]{1,0:T(8,128)(2,1)} %constant.31.clone.first_hbm, f32[4,32,256]{2,1,0:T(8,128)} %constant.32.clone.turn_hbm, bf16[2,512,256]{2,1,0:T(8,128)(2,1)} %constant.33.clone.second_hbm, ...), custom_call_target="tpu_custom_call" | custom-call | tf_op jit(solution)/shard_map/cycle_dft/pallas_call | solution.py:166
  3.6 7.3 %all-to-all-start = ((f32[32,8,128]{2,1,0:T(8,128)}), f32[32,8,128]{2,1,0:T(8,128)S(1)}, u32[]{:S(2)}, u32[]{:S(2)}) async-start(f32[32,8,128]{2,1,0:T(8,128)} %bitcast.6), calls=%async_computation | async-start | bytes 262144 | tf_op jit(solution)/shard_map/all_to_all | solution.py:674
  11.0 0.0 copy-start
  11.0 0.0 copy-start.1
  11.0 0.0 copy-start.2
  11.0 0.0 copy-start.3
  11.0 8.1 %legendre_rows.1 = (f32[6784,128]{1,0:T(8,128)}, f32[24608,128]{1,0:T(8,128)}) custom-call(f32[4160,128]{1,0:T(8,128)} %constant.27.clone.rise_hbm, f32[4224,128]{1,0:T(8,128)} %constant.28.clone.low_hbm, f32[4224,128]{1,0:T(8,128)} %constant.29.clone.high_hbm, f32[3,16,128]{2,1,0:T(8,128)} %constant.30.clone.x_hbm.x_ref), custom_call_target="tpu_custom_call" | custom-call | flops 68157440 | bytes 25000000 | tf_op jit(solution)/shard_map/legendre_rows/pallas_call | solution.py:354
  19.2 0.0 all-to-all-done
  19.2 0.0 copy-done
  19.2 0.0 copy-done.1
  19.2 0.0 copy-done.2
  19.2 0.0 copy-done.3
  19.2 0.0 copy-start.4
  19.2 11.8 %order_power.1 = f32[32,128]{1,0:T(8,128)S(1)} custom-call(f32[6784,128]{1,0:T(8,128)} %get-tuple-element.4.rows_hbm, f32[24608,128]{1,0:T(8,128)} %get-tuple-element.5.u_hbm, f32[256,128]{1,0:T(8,128)S(1)} %bitcast.5, bf16[144,256]{1,0:T(8,128)(2,1)S(1)} %copy-done.1, f32[3,16,128]{2,1,0:T(8,128)S(1)} %copy-done, f32[128,128]{1,0:T(8,128)S(1)} %copy-done.2, ...), custom_call_target="tpu_custom_call" | custom-call | flops 12599296 | bytes 1000000 | tf_op jit(solution)/shard_map/order_power/pallas_call | solution.py:642
  31.0 0.3 collective-permute-start
  31.3 0.9 %collective-permute-done = f32[32,128]{1,0:T(8,128)S(1)} collective-permute-done((f32[32,128]{1,0:T(8,128)S(1)}, f32[32,128]{1,0:T(8,128)S(1)}, u32[]{:S(2)}, u32[]{:S(2)}) %collective-permute-start) | collective-permute-done | bytes 16416 | tf_op jit(solution)/shard_map/ppermute | solution.py:681
  32.2 1.8 %collective-permute-start.1 = (f32[32,128]{1,0:T(8,128)S(1)}, f32[32,128]{1,0:T(8,128)S(1)}, u32[]{:S(2)}, u32[]{:S(2)}) collective-permute-start(f32[32,128]{1,0:T(8,128)S(1)} %add.15), channel_id=1, source_target_pairs={{0,2},{1,3},{2,0},{3,1},{4,6},{5,7},{6,4},{7,5},{8,10},{9,11},{10,... | collective-permute-start | bytes 49160 | tf_op jit(solution)/shard_map/ppermute | solution.py:681
  34.0 2.0 %collective-permute-done.1 = f32[32,128]{1,0:T(8,128)S(1)} collective-permute-done((f32[32,128]{1,0:T(8,128)S(1)}, f32[32,128]{1,0:T(8,128)S(1)}, u32[]{:S(2)}, u32[]{:S(2)}) %collective-permute-start.1) | collective-permute-done | bytes 16416 | tf_op jit(solution)/shard_map/ppermute | solution.py:681
  36.0 1.8 %collective-permute-start.2 = (f32[32,128]{1,0:T(8,128)S(1)}, f32[32,128]{1,0:T(8,128)S(1)}, u32[]{:S(2)}, u32[]{:S(2)}) collective-permute-start(f32[32,128]{1,0:T(8,128)S(1)} %add.16), channel_id=1, source_target_pairs={{0,4},{1,5},{2,6},{3,7},{4,0},{5,1},{6,2},{7,3},{8,12},{9,13},{10,... | collective-permute-start | bytes 49160 | tf_op jit(solution)/shard_map/ppermute | solution.py:681
  37.8 2.0 %collective-permute-done.2 = f32[32,128]{1,0:T(8,128)S(1)} collective-permute-done((f32[32,128]{1,0:T(8,128)S(1)}, f32[32,128]{1,0:T(8,128)S(1)}, u32[]{:S(2)}, u32[]{:S(2)}) %collective-permute-start.2) | collective-permute-done | bytes 16416 | tf_op jit(solution)/shard_map/ppermute | solution.py:681
  39.7 2.7 %collective-permute-start.3 = (f32[32,128]{1,0:T(8,128)S(1)}, f32[32,128]{1,0:T(8,128)S(1)}, u32[]{:S(2)}, u32[]{:S(2)}) collective-permute-start(f32[32,128]{1,0:T(8,128)S(1)} %add.17), channel_id=1, source_target_pairs={{0,8},{1,9},{2,10},{3,11},{4,12},{5,13},{6,14},{7,15},{8,0},{9,1},... | collective-permute-start | bytes 49160 | tf_op jit(solution)/shard_map/ppermute | solution.py:681
  42.4 2.0 %collective-permute-done.3 = f32[32,128]{1,0:T(8,128)S(1)} collective-permute-done((f32[32,128]{1,0:T(8,128)S(1)}, f32[32,128]{1,0:T(8,128)S(1)}, u32[]{:S(2)}, u32[]{:S(2)}) %collective-permute-start.3) | collective-permute-done | bytes 16416 | tf_op jit(solution)/shard_map/ppermute | solution.py:681
  44.4 1.8 %collective-permute-start.4 = (f32[32,128]{1,0:T(8,128)S(1)}, f32[32,128]{1,0:T(8,128)S(1)}, u32[]{:S(2)}, u32[]{:S(2)}) collective-permute-start(f32[32,128]{1,0:T(8,128)S(1)} %add.18), channel_id=1, source_target_pairs={{0,16},{16,0},{1,17},{17,1},{2,18},{18,2},{3,19},{19,3},{4,20},{20... | collective-permute-start | bytes 49160 | tf_op jit(solution)/shard_map/ppermute | solution.py:681
  46.1 2.0 %collective-permute-done.4 = f32[32,128]{1,0:T(8,128)S(1)} collective-permute-done((f32[32,128]{1,0:T(8,128)S(1)}, f32[32,128]{1,0:T(8,128)S(1)}, u32[]{:S(2)}, u32[]{:S(2)}) %collective-permute-start.4) | collective-permute-done | bytes 16416 | tf_op jit(solution)/shard_map/ppermute | solution.py:681
  48.1 0.0 copy-done.4
  48.1 1.2 %fusion.1 = (f32[]{:T(128)}, f32[4096]{0:T(1024)}) fusion(f32[4096]{0:T(1024)S(1)} %copy-done.4, f32[32,128]{1,0:T(8,128)S(1)} %add.18, f32[32,128]{1,0:T(8,128)S(1)} %collective-permute-done.4), kind=kLoop, calls=%fused_computation.3 | loop fusion | flops 20479 | bytes 65540 | tf_op jit(solution)/shard_map/reduce_sum | solution.py:685
  (4 shorter events, 0.0 us)
Async XLA Ops:
  3.6 15.5 %all-to-all-start = ((f32[32,8,128]{2,1,0:T(8,128)}), f32[32,8,128]{2,1,0:T(8,128)S(1)}, u32[]{:S(2)}, u32[]{:S(2)}) async-start(f32[32,8,128]{2,1,0:T(8,128)} %bitcast.6), calls=%async_computation | async-start | bytes 262144 | tf_op jit(solution)/shard_map/all_to_all | solution.py:674
  11.0 8.2 %copy-start = (f32[3,16,128]{2,1,0:T(8,128)S(1)}, f32[3,16,128]{2,1,0:T(8,128)}, u32[]{:S(2)}) copy-start(f32[3,16,128]{2,1,0:T(8,128)} %constant.30.clone.x_hbm.x_ref) | copy-start | bytes 73732
  11.0 8.2 %copy-start.1 = (bf16[144,256]{1,0:T(8,128)(2,1)S(1)}, bf16[144,256]{1,0:T(8,128)(2,1)}, u32[]{:S(2)}) copy-start(bf16[144,256]{1,0:T(8,128)(2,1)} %constant.35.clone.pick_ref) | copy-start | bytes 221188
  11.0 8.2 %copy-start.2 = (f32[128,128]{1,0:T(8,128)S(1)}, f32[128,128]{1,0:T(8,128)}, u32[]{:S(2)}) copy-start(f32[128,128]{1,0:T(8,128)} %constant.36.clone.spread_ref) | copy-start | bytes 196612
  11.0 8.2 %copy-start.3 = (bf16[32,128]{1,0:T(8,128)(2,1)S(1)}, bf16[32,128]{1,0:T(8,128)(2,1)}, u32[]{:S(2)}) copy-start(bf16[32,128]{1,0:T(8,128)(2,1)} %constant.37.clone.gather_ref) | copy-start | bytes 24580
  19.2 28.9 %copy-start.4 = (f32[4096]{0:T(1024)S(1)}, f32[4096]{0:T(1024)}, u32[]{:S(2)}) copy-start(f32[4096]{0:T(1024)} %param.19) | copy-start | bytes 49156
  31.0 1.2 %collective-permute-start = (f32[32,128]{1,0:T(8,128)S(1)}, f32[32,128]{1,0:T(8,128)S(1)}, u32[]{:S(2)}, u32[]{:S(2)}) collective-permute-start(f32[32,128]{1,0:T(8,128)S(1)} %order_power.1), channel_id=1, source_target_pairs={{0,1},{1,0},{2,3},{3,2},{4,5},{5,4},{6,7},{7,6},{8,9},{9,8},{10,11... | collective-permute-start | bytes 49160 | tf_op jit(solution)/shard_map/ppermute | solution.py:681
  32.2 3.7 %collective-permute-start.1 = (f32[32,128]{1,0:T(8,128)S(1)}, f32[32,128]{1,0:T(8,128)S(1)}, u32[]{:S(2)}, u32[]{:S(2)}) collective-permute-start(f32[32,128]{1,0:T(8,128)S(1)} %add.15), channel_id=1, source_target_pairs={{0,2},{1,3},{2,0},{3,1},{4,6},{5,7},{6,4},{7,5},{8,10},{9,11},{10,... | collective-permute-start | bytes 49160 | tf_op jit(solution)/shard_map/ppermute | solution.py:681
  36.0 3.7 %collective-permute-start.2 = (f32[32,128]{1,0:T(8,128)S(1)}, f32[32,128]{1,0:T(8,128)S(1)}, u32[]{:S(2)}, u32[]{:S(2)}) collective-permute-start(f32[32,128]{1,0:T(8,128)S(1)} %add.16), channel_id=1, source_target_pairs={{0,4},{1,5},{2,6},{3,7},{4,0},{5,1},{6,2},{7,3},{8,12},{9,13},{10,... | collective-permute-start | bytes 49160 | tf_op jit(solution)/shard_map/ppermute | solution.py:681
  39.7 4.6 %collective-permute-start.3 = (f32[32,128]{1,0:T(8,128)S(1)}, f32[32,128]{1,0:T(8,128)S(1)}, u32[]{:S(2)}, u32[]{:S(2)}) collective-permute-start(f32[32,128]{1,0:T(8,128)S(1)} %add.17), channel_id=1, source_target_pairs={{0,8},{1,9},{2,10},{3,11},{4,12},{5,13},{6,14},{7,15},{8,0},{9,1},... | collective-permute-start | bytes 49160 | tf_op jit(solution)/shard_map/ppermute | solution.py:681
  44.4 3.7 %collective-permute-start.4 = (f32[32,128]{1,0:T(8,128)S(1)}, f32[32,128]{1,0:T(8,128)S(1)}, u32[]{:S(2)}, u32[]{:S(2)}) collective-permute-start(f32[32,128]{1,0:T(8,128)S(1)} %add.18), channel_id=1, source_target_pairs={{0,16},{16,0},{1,17},{17,1},{2,18},{18,2},{3,19},{19,3},{4,20},{20... | collective-permute-start | bytes 49160 | tf_op jit(solution)/shard_map/ppermute | solution.py:681

commit v4 on v3

--- a/solution.py
+++ b/solution.py
@@ -17,14 +17,13 @@
 LANES = 128
 CHUNK = 32
 PITCH = 12
-STREAMED = 48
-PIECES = 4
+STREAMED = 96
+PIECES = 6
 VMEM_LIMIT = 56 * 1024 * 1024
 POWER_VMEM = 51 * 1024 * 1024
 F32 = jnp.float32
 BF16 = jnp.bfloat16
 ANY = pl.BlockSpec(memory_space=pl.ANY)
-SMEM = pl.BlockSpec(memory_space=pltpu.SMEM)
 VMEM = pl.BlockSpec(memory_space=pltpu.VMEM)
 
 
@@ -85,15 +84,18 @@
 def dft_kernel(
     n_dev,
     n_blk,
-    ids_ref,
-    mask_ref,
+    ids_hbm,
+    mask_hbm,
     pix_hbm,
     first_hbm,
     turn_hbm,
     second_hbm,
     half_hbm,
+    out_hbm,
     out_ref,
     x_ref,
+    ids_ref,
+    mask_ref,
     pix_ref,
     first_ref,
     turn_ref,
@@ -103,6 +105,8 @@
 ):
     copies = fetch(
         [
+            (ids_hbm, ids_ref),
+            (mask_hbm, mask_ref),
             (pix_hbm, pix_ref),
             (first_hbm, first_ref),
             (turn_hbm, turn_ref),
@@ -120,7 +124,8 @@
     rows = BLOCK_PIX // width
     pairs = LMAX // (2 * n_dev)
     x_ref[...] = jnp.zeros_like(x_ref)
-    copies[0].wait()
+    for copy in copies[:3]:
+        copy.wait()
     for i in range(slots):
         number = ids_ref[i]
         cycle, seg = lax.div(number, SEGS), lax.rem(number, SEGS)
@@ -131,11 +136,10 @@
             x_ref[place, pl.ds(seg * rows + h, 1), :] = pix_ref[i : i + 1, h * width : (h + 1) * width] * keep
     x = jnp.concatenate([x_ref[c] for c in range(cycles)], axis=1)
     x_high, x_low = split(x)
-    copies[1].wait()
+    copies[3].wait()
     y = dot(first_ref[...], jnp.concatenate([x_high, x_high, x_low], axis=0))
-    copies[2].wait()
-    copies[3].wait()
-    copies[4].wait()
+    for copy in copies[4:]:
+        copy.wait()
     for phase in range(2):
         y_re = y[2 * phase * n_dev : (2 * phase + 1) * n_dev]
         y_im = y[(2 * phase + 1) * n_dev : (2 * phase + 2) * n_dev]
@@ -157,20 +161,25 @@
                     swapped = jnp.concatenate([spec[:, pairs:], spec[:, :pairs]], axis=1)
                 spec = spec * half_ref[2 * phase] + swapped * half_ref[2 * phase + 1]
             out_ref[pl.ds(2 * c + phase, n_dev, stride=2 * cycles), :] = spec
+    send = pltpu.make_async_copy(out_ref, out_hbm, sems.at[7])
+    send.start()
+    send.wait()
 
 
 def cycle_spectra(pixels, block_ids, mask, n_dev, n_blk):
     pairs = LMAX // (2 * n_dev)
     cycles = n_blk * pixels.shape[0] // SEGS
     tables = [jnp.asarray(t) for t in dft_tables(n_dev)]
+    out = jax.ShapeDtypeStruct((n_dev * 2 * cycles, 2 * pairs), F32)
     return pl.pallas_call(
         functools.partial(dft_kernel, n_dev, n_blk),
-        out_shape=jax.ShapeDtypeStruct((n_dev * 2 * cycles, 2 * pairs), F32),
-        in_specs=[SMEM, SMEM] + [ANY] * 5,
-        out_specs=VMEM,
-        scratch_shapes=[pltpu.VMEM((cycles, n_dev, CYCLE_PIX // n_dev), F32), pltpu.VMEM(pixels.shape, F32)]
-        + [pltpu.VMEM(t.shape, t.dtype) for t in tables]
-        + [pltpu.SemaphoreType.DMA((5,))],
+        out_shape=out,
+        in_specs=[ANY] * 7,
+        out_specs=ANY,
+        scratch_shapes=[pltpu.VMEM(out.shape, F32), pltpu.VMEM((cycles, n_dev, CYCLE_PIX // n_dev), F32)]
+        + [pltpu.SMEM(block_ids.shape, jnp.int32), pltpu.SMEM(mask.shape, jnp.int32)]
+        + [pltpu.VMEM(t.shape, t.dtype) for t in [pixels, *tables]]
+        + [pltpu.SemaphoreType.DMA((8,))],
         compiler_params=pltpu.CompilerParams(vmem_limit_bytes=VMEM_LIMIT),
         name="cycle_dft",
     )(block_ids, mask, pixels, *tables)
@@ -250,9 +259,10 @@
     per_block = n_dev // CHUNK
     chunks = step_blocks(n_dev) * per_block
     total = chunks * CHUNK
-    cut = STREAMED * CHUNK
+    piece = STREAMED // PIECES
+    ends = [0, 2 * piece * CHUNK, STREAMED * CHUNK, total]
     parts = [(x_hbm, x_ref)]
-    for start, stop in ((0, cut), (cut, total)):
+    for start, stop in zip(ends, ends[1:]):
         for src, dst in ((rise_hbm, rise_ref), (low_hbm, low_ref), (high_hbm, high_ref)):
             reach = 0 if src is rise_hbm else 2 * n_dev
             first = start + reach if start else 0
@@ -304,20 +314,17 @@
     def steps(chunk, state):
         even, odd = turn_lanes(chunk, per_block, q, seed_low, list(state[:vregs]), list(state[vregs:]))
         first = pl.multiple_of(chunk * CHUNK, CHUNK)
-        start = pl.multiple_of(chunk * (CHUNK * 8 * vregs), CHUNK * 8 * vregs)
+        start = pl.multiple_of(chunk * (CHUNK * 4 * vregs), CHUNK * 4 * vregs)
         for s in range(0, CHUNK, 2):
             fresh_even, fresh_odd = advance(rows_ref, first + s, even, odd, x2)
             for v in range(vregs):
-                u_ref[pl.ds(start + 8 * (s * vregs + v), 8), :] = even[v]
-                u_ref[pl.ds(start + 8 * ((s + 1) * vregs + v), 8), :] = fresh_odd[v]
+                u_ref[pl.ds(start + 8 * (s // 2 * vregs + v), 8), :] = even[v]
             even, odd = fresh_even, fresh_odd
         return (*even, *odd)
 
-    coefficients(0, STREAMED)
     zero = jnp.zeros((8, LANES), F32)
     state = (*seed_high, *([zero] * vregs))
-    piece = STREAMED // PIECES
-    size = piece * CHUNK * 8 * vregs
+    size = piece * CHUNK * 4 * vregs
     out = []
 
     def send(src, dst, sem):
@@ -326,6 +333,12 @@
 
     for p in range(PIECES):
         first = p * piece
+        if p == 0:
+            coefficients(0, 2 * piece)
+        if p == 2:
+            for copy in copies[4:7]:
+                copy.wait()
+            coefficients(2 * piece, STREAMED)
         state = lax.fori_loop(first // 2, (first + piece) // 2, lambda h, s: steps(2 * h + 1, steps(2 * h, s)), state)
         extra = 0
         if p == PIECES - 1:
@@ -333,11 +346,11 @@
             for v in range(2 * vregs):
                 u_ref[PIECES * size + 8 * v : PIECES * size + 8 * v + 8, :] = state[v]
         span = pl.ds(p * size, size + extra)
-        send(u_ref.at[span], u_hbm.at[span], 7 + p)
-    for copy in copies[4:]:
+        send(u_ref.at[span], u_hbm.at[span], 10 + p)
+    for copy in copies[7:]:
         copy.wait()
     coefficients(STREAMED, chunks)
-    send(rows_ref.at[pl.ds(cut, 2 * total - cut)], rows_hbm, 7 + PIECES)
+    send(rows_ref, rows_hbm, 10 + PIECES)
     for copy in out:
         copy.wait()
 
@@ -349,15 +362,14 @@
     cut = STREAMED * CHUNK
     tables = [jnp.asarray(t) for t in recurrence_tables(n_dev, lats)]
     rows = jax.ShapeDtypeStruct((2 * total, LANES), F32)
-    rest = jax.ShapeDtypeStruct((2 * total - cut, LANES), F32)
-    u = jax.ShapeDtypeStruct((cut * 8 * vregs + 16 * vregs, LANES), F32)
+    u = jax.ShapeDtypeStruct((cut * 4 * vregs + 16 * vregs, LANES), F32)
     return pl.pallas_call(
         functools.partial(recurrence_kernel, n_dev, vregs, float(2 * lats * CYCLE_PIX)),
-        out_shape=(rest, u),
+        out_shape=(rows, u),
         in_specs=[ANY] * 4,
         out_specs=(ANY, ANY),
         scratch_shapes=[pltpu.VMEM(t.shape, t.dtype) for t in [*tables, rows, u]]
-        + [pltpu.SemaphoreType.DMA((8 + PIECES,))],
+        + [pltpu.SemaphoreType.DMA((11 + PIECES,))],
         compiler_params=pltpu.CompilerParams(vmem_limit_bytes=VMEM_LIMIT),
         cost_estimate=pl.CostEstimate(flops=total * 8 * LANES * vregs * 8, bytes_accessed=25000000, transcendentals=0),
         name="legendre_rows",
@@ -435,9 +447,10 @@
     pairs = LMAX // (2 * n_dev)
     all_steps = step_blocks(n_dev) * n_dev
     cut = STREAMED * CHUNK
-    size = cut // PIECES * 8 * vregs
+    size = cut // PIECES * 4 * vregs
     spans = [pl.ds(p * size, size) for p in range(PIECES)]
-    states, coefs, weights = pl.ds(PIECES * size, 16 * vregs), pl.ds(0, all_steps - cut), pl.ds(all_steps - cut, all_steps)
+    states, coefs = pl.ds(PIECES * size, 16 * vregs), pl.ds(cut, all_steps - cut)
+    early, weights = pl.ds(0, cut), pl.ds(all_steps, all_steps)
     copies = fetch(
         [
             (u_hbm.at[states], u_ref.at[states]),
@@ -502,16 +515,23 @@
                 value = value + u[v] * now[s % 2][v][part]
             prod_ref[part, pl.ds((s // 8) * 8 * PITCH + s % 8, 8, stride=PITCH), :] = value
 
-    def products(chunk, prod_ref):
+    def products(chunk, prod_ref, odd):
         now = spectra_now(chunk)
-        start = pl.multiple_of(chunk * (CHUNK * 8 * vregs), CHUNK * 8 * vregs)
-        for s in range(CHUNK):
-            product(s, [u_ref[pl.ds(start + 8 * (s * vregs + v), 8), :] for v in range(vregs)], now, prod_ref)
+        start = pl.multiple_of(chunk * (CHUNK * 4 * vregs), CHUNK * 4 * vregs)
+        first = pl.multiple_of(chunk * CHUNK, CHUNK)
+        _, odd = turn_lanes(chunk, per_block, q, seed_low, odd, odd)
+        for s in range(0, CHUNK, 2):
+            even = [u_ref[pl.ds(start + 8 * (s // 2 * vregs + v), 8), :] for v in range(vregs)]
+            one = rows_ref[pl.ds(first + s, 1), :]
+            odd = [one * e - o for e, o in zip(even, odd)]
+            product(s, even, now, prod_ref)
+            product(s + 1, odd, now, prod_ref)
+        return odd
 
     def steps(chunk, prod_ref, state):
         now = spectra_now(chunk)
         even, odd = turn_lanes(chunk, per_block, q, seed_low, list(state[:vregs]), list(state[vregs:]))
-        first = pl.multiple_of((chunk - STREAMED) * CHUNK, CHUNK)
+        first = pl.multiple_of(chunk * CHUNK, CHUNK)
         for s in range(0, CHUNK, 2):
             fresh_even, fresh_odd = advance(rows_ref, first + s, even, odd, x2)
             product(s, even, now, prod_ref)
@@ -534,34 +554,34 @@
         reduce(2 * h, prod_a)
         return state
 
-    def two_streamed(h, carry):
-        products(2 * h, prod_a)
+    def two_streamed(h, odd):
+        odd = products(2 * h, prod_a, list(odd))
         reduce(jnp.maximum(2 * h - 1, 0), prod_b)
-        products(2 * h + 1, prod_b)
+        odd = products(2 * h + 1, prod_b, odd)
         reduce(2 * h, prod_a)
-        return carry
+        return tuple(odd)
 
     m_low = (d + n_dev * q).astype(F32)
     x2 = [x_ref[1, 8 * v : 8 * v + 8, :] for v in range(vregs)]
     seed_low = [jnp.exp(m_low * x_ref[2, 8 * v : 8 * v + 8, :]) for v in range(vregs)]
     for copy in copies:
         copy.wait()
-    moved = [(u_hbm.at[span], u_ref.at[span]) for span in spans] + [
-        (rows_hbm.at[weights], rows_ref.at[weights]),
-    ]
+    moved = [(rows_hbm.at[early], rows_ref.at[early])] + [(u_hbm.at[span], u_ref.at[span]) for span in spans]
+    moved.append((rows_hbm.at[weights], rows_ref.at[weights]))
     copies = [pltpu.make_async_copy(src, dst, sems.at[2 + i]) for i, (src, dst) in enumerate(moved)]
     for copy in copies:
         copy.start()
     state = [u_ref[PIECES * size + 8 * v : PIECES * size + 8 * v + 8, :] for v in range(2 * vregs)]
-    lax.fori_loop(STREAMED // 2, chunks // 2, two_inline, tuple(state))
+    lax.fori_loop(STREAMED // 2, chunks // 2, two_inline, tuple(state), unroll=True)
     reduce(chunks - 1, prod_b)
     piece = STREAMED // PIECES
+    odd = (jnp.zeros((8, LANES), F32),) * vregs
+    copies[0].wait()
     for p in range(PIECES):
-        copies[p].wait()
-        lax.fori_loop(p * piece // 2, (p + 1) * piece // 2, two_streamed, 0)
+        copies[1 + p].wait()
+        odd = lax.fori_loop(p * piece // 2, (p + 1) * piece // 2, two_streamed, odd)
     reduce(STREAMED - 1, prod_b)
-    for copy in copies[PIECES:]:
-        copy.wait()
+    copies[-1].wait()
 
     def packed(tau):
         re, im = sum_ref[0, pl.ds(tau, 8), :], sum_ref[1, pl.ds(tau, 8), :]
@@ -583,7 +603,7 @@
             flats = [jnp.where(low, load(base), load(base + 1)) for low in lows]
         values = [packed(tau) for tau in taus]
         values = [v + flats[j] for v, (_, j) in zip(values, places)]
-        values = [v * v * rows_ref[pl.ds(all_steps - cut + tau, 8), :] for v, tau in zip(values, taus)]
+        values = [v * v * rows_ref[pl.ds(all_steps + tau, 8), :] for v, tau in zip(values, taus)]
         low_parts = values
         if with_high:
             low_parts = [jnp.where(lows[j], v, 0.0) for v, (_, j) in zip(values, places)]
@@ -652,7 +672,7 @@
             pltpu.VMEM((2, step_blocks(n_dev) * n_dev, LANES), F32),
             pltpu.VMEM((n_dev, LANES), F32),
             pltpu.VMEM((n_dev, LANES), F32),
-            pltpu.SemaphoreType.DMA((3 + PIECES,)),
+            pltpu.SemaphoreType.DMA((4 + PIECES,)),
         ],
         compiler_params=pltpu.CompilerParams(vmem_limit_bytes=POWER_VMEM),
         cost_estimate=pl.CostEstimate(flops=u.size * 4, bytes_accessed=1000000, transcendentals=0),

time: 51.3 us -> 49.9 us (0.973)
  Pallas kernels: 22.9 us -> 21.4 us
    pallas_call x1, Pallas kernels: 11.8 us -> 10.5 us  [power_of_orders(): pl.pallas_call(functools.partial(power_kernel, n_dev, vregs), out_shape=j...]
    pallas_call x1, Pallas kernels: 3.01 us -> 2.39 us  [cycle_spectra(): pl.pallas_call(functools.partial(dft_kernel, n_dev, n_blk), out_shape=out...]
  transfers between devices with their start and end apart: 6 -> 6, of which waited for: 5 -> 5; matrix products, arithmetic and copies ran while one was open for 0% -> 0% of each run, Pallas kernels for 16% -> 17%
where the time goes in v4:
time: 49.9 us; the launch traced here: 49.6 us
  Pallas kernels  21.4 us (43%)
  starting transfers between devices  15.7 us (31%)
  waiting for transfers between devices  8.69 us (17%)
  between operations  2.53 us (5%)
  other arithmetic  1.23 us (2%)
    pallas_call x1, Pallas kernels, power_of_orders(): pl.pallas_call(functools.partial(power_kernel, n_dev, vregs), out_shape=j...  10.5 us
    ppermute x5, waiting for transfers between devices, on_device(): lax.ppermute(power, axis, [(i, i ^ bit) for i in range(size)])  8.69 us
    pallas_call x1, Pallas kernels, legendre_rows(): pl.pallas_call(functools.partial(recurrence_kernel, n_dev, vregs, float(2...  8.57 us
    ppermute x5, starting transfers between devices, on_device(): lax.ppermute(power, axis, [(i, i ^ bit) for i in range(size)])  8.42 us
    all_to_all x1, starting transfers between devices, on_device(): lax.all_to_all(sent.reshape(n_dev, 2 * cycles, 2 * pairs), ('blk', 'mblk'...  7.3 us
    pallas_call x1, Pallas kernels, cycle_spectra(): pl.pallas_call(functools.partial(dft_kernel, n_dev, n_blk), out_shape=out...  2.39 us
    reduce_sum x1, other arithmetic, on_device(): misfit = jnp.mean(rel_error * rel_error)  1.21 us
  transfers between devices with their start and end apart: 6, of which 5 were waited for; matrix products, arithmetic and copies ran while one was open for 0% of the time, Pallas kernels for 17%

profile of v4, /device:TPU:0, one launch (start us, length us, event | category | flops | bytes accessed | tf_op | source)
XLA Modules:
  0.0 49.6 jit_solution(7910172707426608778)
XLA Ops:
  0.6 2.4 %cycle_dft.1 = f32[256,128]{1,0:T(8,128)} custom-call(s32[16]{0:T(128)} %ids_hbm.1, s32[16]{0:T(128)} %mask_hbm.1, f32[16,1024]{1,0:T(8,128)} %pix_hbm.1, bf16[128,96]{1,0:T(8,128)(2,1)} %constant.31.clone.first_hbm, f32[4,32,256]{2,1,0:T(8,128)} %constant.32.clone.turn_hbm, bf16[2,512,256]{2,1,0:T(8,128)(2,1)} %constant.33.clone.second_hbm, ...), custom_call_target="tpu_custom_call" | custom-call | tf_op jit(solution)/shard_map/cycle_dft/pallas_call | solution.py:174
  3.0 7.3 %all-to-all-start = ((f32[32,8,128]{2,1,0:T(8,128)}), f32[32,8,128]{2,1,0:T(8,128)S(1)}, u32[]{:S(2)}, u32[]{:S(2)}) async-start(f32[32,8,128]{2,1,0:T(8,128)} %bitcast.6), calls=%async_computation | async-start | bytes 262144 | tf_op jit(solution)/shard_map/all_to_all | solution.py:694
  10.3 0.0 copy-start
  10.4 0.0 copy-start.1
  10.4 0.0 copy-start.2
  10.4 0.0 copy-start.3
  10.4 8.6 %legendre_rows.1 = (f32[8320,128]{1,0:T(8,128)}, f32[24608,128]{1,0:T(8,128)}) custom-call(f32[4160,128]{1,0:T(8,128)} %constant.27.clone.rise_hbm, f32[4224,128]{1,0:T(8,128)} %constant.28.clone.low_hbm, f32[4224,128]{1,0:T(8,128)} %constant.29.clone.high_hbm, f32[3,16,128]{2,1,0:T(8,128)} %constant.30.clone.x_hbm.x_ref), custom_call_target="tpu_custom_call" | custom-call | flops 68157440 | bytes 25000000 | tf_op jit(solution)/shard_map/legendre_rows/pallas_call | solution.py:366
  19.0 0.0 all-to-all-done
  19.0 0.0 copy-done
  19.0 0.0 copy-done.1
  19.0 0.0 copy-done.2
  19.0 0.0 copy-done.3
  19.0 0.0 copy-start.4
  19.0 10.5 %order_power.1 = f32[32,128]{1,0:T(8,128)S(1)} custom-call(f32[8320,128]{1,0:T(8,128)} %get-tuple-element.4.rows_hbm, f32[24608,128]{1,0:T(8,128)} %get-tuple-element.5.u_hbm, f32[256,128]{1,0:T(8,128)S(1)} %bitcast.5, bf16[144,256]{1,0:T(8,128)(2,1)S(1)} %copy-done.1, f32[3,16,128]{2,1,0:T(8,128)S(1)} %copy-done, f32[128,128]{1,0:T(8,128)S(1)} %copy-done.2, ...), custom_call_target="tpu_custom_call" | custom-call | flops 12599296 | bytes 1000000 | tf_op jit(solution)/shard_map/order_power/pallas_call | solution.py:662
  29.5 0.3 collective-permute-start
  29.8 0.9 %collective-permute-done = f32[32,128]{1,0:T(8,128)S(1)} collective-permute-done((f32[32,128]{1,0:T(8,128)S(1)}, f32[32,128]{1,0:T(8,128)S(1)}, u32[]{:S(2)}, u32[]{:S(2)}) %collective-permute-start) | collective-permute-done | bytes 16416 | tf_op jit(solution)/shard_map/ppermute | solution.py:701
  30.8 1.8 %collective-permute-start.1 = (f32[32,128]{1,0:T(8,128)S(1)}, f32[32,128]{1,0:T(8,128)S(1)}, u32[]{:S(2)}, u32[]{:S(2)}) collective-permute-start(f32[32,128]{1,0:T(8,128)S(1)} %add.15), channel_id=1, source_target_pairs={{0,2},{1,3},{2,0},{3,1},{4,6},{5,7},{6,4},{7,5},{8,10},{9,11},{10,... | collective-permute-start | bytes 49160 | tf_op jit(solution)/shard_map/ppermute | solution.py:701
  32.6 1.9 %collective-permute-done.1 = f32[32,128]{1,0:T(8,128)S(1)} collective-permute-done((f32[32,128]{1,0:T(8,128)S(1)}, f32[32,128]{1,0:T(8,128)S(1)}, u32[]{:S(2)}, u32[]{:S(2)}) %collective-permute-start.1) | collective-permute-done | bytes 16416 | tf_op jit(solution)/shard_map/ppermute | solution.py:701
  34.5 1.8 %collective-permute-start.2 = (f32[32,128]{1,0:T(8,128)S(1)}, f32[32,128]{1,0:T(8,128)S(1)}, u32[]{:S(2)}, u32[]{:S(2)}) collective-permute-start(f32[32,128]{1,0:T(8,128)S(1)} %add.16), channel_id=1, source_target_pairs={{0,4},{1,5},{2,6},{3,7},{4,0},{5,1},{6,2},{7,3},{8,12},{9,13},{10,... | collective-permute-start | bytes 49160 | tf_op jit(solution)/shard_map/ppermute | solution.py:701
  36.3 1.9 %collective-permute-done.2 = f32[32,128]{1,0:T(8,128)S(1)} collective-permute-done((f32[32,128]{1,0:T(8,128)S(1)}, f32[32,128]{1,0:T(8,128)S(1)}, u32[]{:S(2)}, u32[]{:S(2)}) %collective-permute-start.2) | collective-permute-done | bytes 16416 | tf_op jit(solution)/shard_map/ppermute | solution.py:701
  38.3 2.7 %collective-permute-start.3 = (f32[32,128]{1,0:T(8,128)S(1)}, f32[32,128]{1,0:T(8,128)S(1)}, u32[]{:S(2)}, u32[]{:S(2)}) collective-permute-start(f32[32,128]{1,0:T(8,128)S(1)} %add.17), channel_id=1, source_target_pairs={{0,8},{1,9},{2,10},{3,11},{4,12},{5,13},{6,14},{7,15},{8,0},{9,1},... | collective-permute-start | bytes 49160 | tf_op jit(solution)/shard_map/ppermute | solution.py:701
  41.0 1.9 %collective-permute-done.3 = f32[32,128]{1,0:T(8,128)S(1)} collective-permute-done((f32[32,128]{1,0:T(8,128)S(1)}, f32[32,128]{1,0:T(8,128)S(1)}, u32[]{:S(2)}, u32[]{:S(2)}) %collective-permute-start.3) | collective-permute-done | bytes 16416 | tf_op jit(solution)/shard_map/ppermute | solution.py:701
  42.9 1.8 %collective-permute-start.4 = (f32[32,128]{1,0:T(8,128)S(1)}, f32[32,128]{1,0:T(8,128)S(1)}, u32[]{:S(2)}, u32[]{:S(2)}) collective-permute-start(f32[32,128]{1,0:T(8,128)S(1)} %add.18), channel_id=1, source_target_pairs={{0,16},{16,0},{1,17},{17,1},{2,18},{18,2},{3,19},{19,3},{4,20},{20... | collective-permute-start | bytes 49160 | tf_op jit(solution)/shard_map/ppermute | solution.py:701
  44.7 2.0 %collective-permute-done.4 = f32[32,128]{1,0:T(8,128)S(1)} collective-permute-done((f32[32,128]{1,0:T(8,128)S(1)}, f32[32,128]{1,0:T(8,128)S(1)}, u32[]{:S(2)}, u32[]{:S(2)}) %collective-permute-start.4) | collective-permute-done | bytes 16416 | tf_op jit(solution)/shard_map/ppermute | solution.py:701
  46.6 0.0 copy-done.4
  46.6 1.2 %fusion.1 = (f32[]{:T(128)}, f32[4096]{0:T(1024)}) fusion(f32[4096]{0:T(1024)S(1)} %copy-done.4, f32[32,128]{1,0:T(8,128)S(1)} %add.18, f32[32,128]{1,0:T(8,128)S(1)} %collective-permute-done.4), kind=kLoop, calls=%fused_computation.3 | loop fusion | flops 20479 | bytes 65540 | tf_op jit(solution)/shard_map/reduce_sum | solution.py:705
  (4 shorter events, 0.0 us)
Async XLA Ops:
  3.0 15.9 %all-to-all-start = ((f32[32,8,128]{2,1,0:T(8,128)}), f32[32,8,128]{2,1,0:T(8,128)S(1)}, u32[]{:S(2)}, u32[]{:S(2)}) async-start(f32[32,8,128]{2,1,0:T(8,128)} %bitcast.6), calls=%async_computation | async-start | bytes 262144 | tf_op jit(solution)/shard_map/all_to_all | solution.py:694
  10.3 8.6 %copy-start = (f32[3,16,128]{2,1,0:T(8,128)S(1)}, f32[3,16,128]{2,1,0:T(8,128)}, u32[]{:S(2)}) copy-start(f32[3,16,128]{2,1,0:T(8,128)} %constant.30.clone.x_hbm.x_ref) | copy-start | bytes 73732
  10.4 8.6 %copy-start.1 = (bf16[144,256]{1,0:T(8,128)(2,1)S(1)}, bf16[144,256]{1,0:T(8,128)(2,1)}, u32[]{:S(2)}) copy-start(bf16[144,256]{1,0:T(8,128)(2,1)} %constant.35.clone.pick_ref) | copy-start | bytes 221188
  10.4 8.6 %copy-start.2 = (f32[128,128]{1,0:T(8,128)S(1)}, f32[128,128]{1,0:T(8,128)}, u32[]{:S(2)}) copy-start(f32[128,128]{1,0:T(8,128)} %constant.36.clone.spread_ref) | copy-start | bytes 196612
  10.4 8.6 %copy-start.3 = (bf16[32,128]{1,0:T(8,128)(2,1)S(1)}, bf16[32,128]{1,0:T(8,128)(2,1)}, u32[]{:S(2)}) copy-start(bf16[32,128]{1,0:T(8,128)(2,1)} %constant.37.clone.gather_ref) | copy-start | bytes 24580
  19.0 27.6 %copy-start.4 = (f32[4096]{0:T(1024)S(1)}, f32[4096]{0:T(1024)}, u32[]{:S(2)}) copy-start(f32[4096]{0:T(1024)} %param.19) | copy-start | bytes 49156
  29.5 1.2 %collective-permute-start = (f32[32,128]{1,0:T(8,128)S(1)}, f32[32,128]{1,0:T(8,128)S(1)}, u32[]{:S(2)}, u32[]{:S(2)}) collective-permute-start(f32[32,128]{1,0:T(8,128)S(1)} %order_power.1), channel_id=1, source_target_pairs={{0,1},{1,0},{2,3},{3,2},{4,5},{5,4},{6,7},{7,6},{8,9},{9,8},{10,11... | collective-permute-start | bytes 49160 | tf_op jit(solution)/shard_map/ppermute | solution.py:701
  30.8 3.7 %collective-permute-start.1 = (f32[32,128]{1,0:T(8,128)S(1)}, f32[32,128]{1,0:T(8,128)S(1)}, u32[]{:S(2)}, u32[]{:S(2)}) collective-permute-start(f32[32,128]{1,0:T(8,128)S(1)} %add.15), channel_id=1, source_target_pairs={{0,2},{1,3},{2,0},{3,1},{4,6},{5,7},{6,4},{7,5},{8,10},{9,11},{10,... | collective-permute-start | bytes 49160 | tf_op jit(solution)/shard_map/ppermute | solution.py:701
  34.5 3.7 %collective-permute-start.2 = (f32[32,128]{1,0:T(8,128)S(1)}, f32[32,128]{1,0:T(8,128)S(1)}, u32[]{:S(2)}, u32[]{:S(2)}) collective-permute-start(f32[32,128]{1,0:T(8,128)S(1)} %add.16), channel_id=1, source_target_pairs={{0,4},{1,5},{2,6},{3,7},{4,0},{5,1},{6,2},{7,3},{8,12},{9,13},{10,... | collective-permute-start | bytes 49160 | tf_op jit(solution)/shard_map/ppermute | solution.py:701
  38.3 4.6 %collective-permute-start.3 = (f32[32,128]{1,0:T(8,128)S(1)}, f32[32,128]{1,0:T(8,128)S(1)}, u32[]{:S(2)}, u32[]{:S(2)}) collective-permute-start(f32[32,128]{1,0:T(8,128)S(1)} %add.17), channel_id=1, source_target_pairs={{0,8},{1,9},{2,10},{3,11},{4,12},{5,13},{6,14},{7,15},{8,0},{9,1},... | collective-permute-start | bytes 49160 | tf_op jit(solution)/shard_map/ppermute | solution.py:701
  42.9 3.7 %collective-permute-start.4 = (f32[32,128]{1,0:T(8,128)S(1)}, f32[32,128]{1,0:T(8,128)S(1)}, u32[]{:S(2)}, u32[]{:S(2)}) collective-permute-start(f32[32,128]{1,0:T(8,128)S(1)} %add.18), channel_id=1, source_target_pairs={{0,16},{16,0},{1,17},{17,1},{2,18},{18,2},{3,19},{19,3},{4,20},{20... | collective-permute-start | bytes 49160 | tf_op jit(solution)/shard_map/ppermute | solution.py:701

commit v5 on v4

--- a/solution.py
+++ b/solution.py
@@ -253,6 +253,7 @@
     x_ref,
     rows_ref,
     u_ref,
+    even_ref,
     sems,
 ):
     pairs = LMAX // (2 * n_dev)
@@ -347,10 +348,15 @@
                 u_ref[PIECES * size + 8 * v : PIECES * size + 8 * v + 8, :] = state[v]
         span = pl.ds(p * size, size + extra)
         send(u_ref.at[span], u_hbm.at[span], 10 + p)
+    cut = STREAMED * CHUNK
+    for i in range(cut // 16):
+        even_ref[8 * i : 8 * i + 8, :] = rows_ref[pl.ds(16 * i, 8, stride=2), :]
+    send(even_ref, rows_hbm.at[pl.ds(0, cut // 2)], 10 + PIECES)
     for copy in copies[7:]:
         copy.wait()
     coefficients(STREAMED, chunks)
-    send(rows_ref, rows_hbm, 10 + PIECES)
+    rest = 2 * total - cut
+    send(rows_ref.at[pl.ds(cut, rest)], rows_hbm.at[pl.ds(cut // 2, rest)], 11 + PIECES)
     for copy in out:
         copy.wait()
 
@@ -365,11 +371,11 @@
     u = jax.ShapeDtypeStruct((cut * 4 * vregs + 16 * vregs, LANES), F32)
     return pl.pallas_call(
         functools.partial(recurrence_kernel, n_dev, vregs, float(2 * lats * CYCLE_PIX)),
-        out_shape=(rows, u),
+        out_shape=(jax.ShapeDtypeStruct((2 * total - cut // 2, LANES), F32), u),
         in_specs=[ANY] * 4,
         out_specs=(ANY, ANY),
         scratch_shapes=[pltpu.VMEM(t.shape, t.dtype) for t in [*tables, rows, u]]
-        + [pltpu.SemaphoreType.DMA((11 + PIECES,))],
+        + [pltpu.VMEM((cut // 2, LANES), F32), pltpu.SemaphoreType.DMA((12 + PIECES,))],
         compiler_params=pltpu.CompilerParams(vmem_limit_bytes=VMEM_LIMIT),
         cost_estimate=pl.CostEstimate(flops=total * 8 * LANES * vregs * 8, bytes_accessed=25000000, transcendentals=0),
         name="legendre_rows",
@@ -449,12 +455,13 @@
     cut = STREAMED * CHUNK
     size = cut // PIECES * 4 * vregs
     spans = [pl.ds(p * size, size) for p in range(PIECES)]
-    states, coefs = pl.ds(PIECES * size, 16 * vregs), pl.ds(cut, all_steps - cut)
-    early, weights = pl.ds(0, cut), pl.ds(all_steps, all_steps)
+    states, soon = pl.ds(PIECES * size, 16 * vregs), pl.ds(cut // 2, 8 * CHUNK)
+    later = pl.ds(cut // 2 + 8 * CHUNK, all_steps - cut - 8 * CHUNK)
+    early, weights = pl.ds(0, cut // 2), pl.ds(all_steps - cut // 2, all_steps)
     copies = fetch(
         [
             (u_hbm.at[states], u_ref.at[states]),
-            (rows_hbm.at[coefs], rows_ref.at[coefs]),
+            (rows_hbm.at[soon], rows_ref.at[soon]),
         ],
         sems,
     )
@@ -518,11 +525,11 @@
     def products(chunk, prod_ref, odd):
         now = spectra_now(chunk)
         start = pl.multiple_of(chunk * (CHUNK * 4 * vregs), CHUNK * 4 * vregs)
-        first = pl.multiple_of(chunk * CHUNK, CHUNK)
+        first = pl.multiple_of(chunk * (CHUNK // 2), CHUNK // 2)
         _, odd = turn_lanes(chunk, per_block, q, seed_low, odd, odd)
         for s in range(0, CHUNK, 2):
             even = [u_ref[pl.ds(start + 8 * (s // 2 * vregs + v), 8), :] for v in range(vregs)]
-            one = rows_ref[pl.ds(first + s, 1), :]
+            one = rows_ref[pl.ds(first + s // 2, 1), :]
             odd = [one * e - o for e, o in zip(even, odd)]
             product(s, even, now, prod_ref)
             product(s + 1, odd, now, prod_ref)
@@ -531,7 +538,7 @@
     def steps(chunk, prod_ref, state):
         now = spectra_now(chunk)
         even, odd = turn_lanes(chunk, per_block, q, seed_low, list(state[:vregs]), list(state[vregs:]))
-        first = pl.multiple_of(chunk * CHUNK, CHUNK)
+        first = pl.multiple_of(chunk * CHUNK - cut // 2, CHUNK // 2)
         for s in range(0, CHUNK, 2):
             fresh_even, fresh_odd = advance(rows_ref, first + s, even, odd, x2)
             product(s, even, now, prod_ref)
@@ -566,19 +573,21 @@
     seed_low = [jnp.exp(m_low * x_ref[2, 8 * v : 8 * v + 8, :]) for v in range(vregs)]
     for copy in copies:
         copy.wait()
-    moved = [(rows_hbm.at[early], rows_ref.at[early])] + [(u_hbm.at[span], u_ref.at[span]) for span in spans]
+    moved = [(rows_hbm.at[span], rows_ref.at[span]) for span in (later, early)] + [(u_hbm.at[span], u_ref.at[span]) for span in spans]
     moved.append((rows_hbm.at[weights], rows_ref.at[weights]))
     copies = [pltpu.make_async_copy(src, dst, sems.at[2 + i]) for i, (src, dst) in enumerate(moved)]
     for copy in copies:
         copy.start()
     state = [u_ref[PIECES * size + 8 * v : PIECES * size + 8 * v + 8, :] for v in range(2 * vregs)]
-    lax.fori_loop(STREAMED // 2, chunks // 2, two_inline, tuple(state), unroll=True)
+    state = lax.fori_loop(STREAMED // 2, STREAMED // 2 + 4, two_inline, tuple(state), unroll=True)
+    copies[0].wait()
+    lax.fori_loop(STREAMED // 2 + 4, chunks // 2, two_inline, tuple(state), unroll=True)
     reduce(chunks - 1, prod_b)
     piece = STREAMED // PIECES
     odd = (jnp.zeros((8, LANES), F32),) * vregs
-    copies[0].wait()
+    copies[1].wait()
     for p in range(PIECES):
-        copies[1 + p].wait()
+        copies[2 + p].wait()
         odd = lax.fori_loop(p * piece // 2, (p + 1) * piece // 2, two_streamed, odd)
     reduce(STREAMED - 1, prod_b)
     copies[-1].wait()
@@ -603,7 +612,7 @@
             flats = [jnp.where(low, load(base), load(base + 1)) for low in lows]
         values = [packed(tau) for tau in taus]
         values = [v + flats[j] for v, (_, j) in zip(values, places)]
-        values = [v * v * rows_ref[pl.ds(all_steps + tau, 8), :] for v, tau in zip(values, taus)]
+        values = [v * v * rows_ref[pl.ds(all_steps - cut // 2 + tau, 8), :] for v, tau in zip(values, taus)]
         low_parts = values
         if with_high:
             low_parts = [jnp.where(lows[j], v, 0.0) for v, (_, j) in zip(values, places)]
@@ -624,7 +633,7 @@
                     total = total + high_parts[j * tiles + i]
                 acch_ref[8 * i : 8 * i + 8, :] = total
 
-    many = 512 // n_dev
+    many = 1024 // n_dev
     half = pairs // many
 
     def both_halves(g, carry):
@@ -672,12 +681,33 @@
             pltpu.VMEM((2, step_blocks(n_dev) * n_dev, LANES), F32),
             pltpu.VMEM((n_dev, LANES), F32),
             pltpu.VMEM((n_dev, LANES), F32),
-            pltpu.SemaphoreType.DMA((4 + PIECES,)),
+            pltpu.SemaphoreType.DMA((5 + PIECES,)),
         ],
         compiler_params=pltpu.CompilerParams(vmem_limit_bytes=POWER_VMEM),
         cost_estimate=pl.CostEstimate(flops=u.size * 4, bytes_accessed=1000000, transcendentals=0),
         name="order_power",
     )(rows, u, got, *tables)
+
+
+def finish_kernel(own_ref, other_ref, model_ref, cl_ref, misfit_ref):
+    cl = own_ref[...] + other_ref[...]
+    model = model_ref[...]
+    cl_ref[...] = cl
+    error = (cl - model) / model
+    squares = jnp.sum(error * error, axis=0, keepdims=True)
+    misfit_ref[...] = jnp.sum(squares, axis=1, keepdims=True) * (1.0 / LMAX)
+
+
+def finish(own, other, model_cl):
+    cl, misfit = pl.pallas_call(
+        finish_kernel,
+        out_shape=(jax.ShapeDtypeStruct(own.shape, F32), jax.ShapeDtypeStruct((1, 1), F32)),
+        in_specs=[VMEM] * 3,
+        out_specs=(VMEM, VMEM),
+        compiler_params=pltpu.CompilerParams(vmem_limit_bytes=2 * 1024 * 1024),
+        name="finish",
+    )(own, other, model_cl.reshape(own.shape))
+    return cl.reshape(LMAX), misfit.reshape(())
 
 
 def on_device(pixels, block_ids, block_mask, model_cl):
@@ -695,15 +725,14 @@
     got = got.reshape(n_dev * 2 * cycles, 2 * pairs)
     power = power_of_orders(rows, u, got, n_dev, n_blk, lats, slots)
 
+    other = jnp.zeros_like(power)
     for axis, size in (("mblk", n_mblk), ("blk", n_blk)):
         bit = 1
         while bit < size:
-            power = power + lax.ppermute(power, axis, [(i, i ^ bit) for i in range(size)])
+            power = power + other
+            other = lax.ppermute(power, axis, [(i, i ^ bit) for i in range(size)])
             bit *= 2
-    pseudo_cl = power.reshape(LMAX)
-    rel_error = (pseudo_cl - model_cl) / model_cl
-    misfit = jnp.mean(rel_error * rel_error)
-    return (pseudo_cl, misfit)
+    return finish(power, other, model_cl)
 
 
 def solution(mesh):

time: 49.9 us -> 47.3 us (0.948)
  between operations: 2.53 us -> 0.75 us
  other arithmetic: 1.23 us -> 0.02 us
    reduce_sum x1 -> x0, other arithmetic: 1.21 us -> none  [on_device(): misfit = jnp.mean(rel_error * rel_error)]
    pallas_call x0 -> x1, Pallas kernels: none -> 0.61 us  [finish(): pl.pallas_call(finish_kernel, out_shape=(jax.ShapeDtypeStruct(own.shape,...]
  transfers between devices with their start and end apart: 6 -> 6, of which waited for: 5 -> 5; matrix products, arithmetic and copies ran while one was open for 0% -> 0% of each run, Pallas kernels for 17% -> 18%
where the time goes in v5:
time: 47.3 us; the launch traced here: 47.1 us
  Pallas kernels  21.8 us (46%)
  starting transfers between devices  15.7 us (33%)
  waiting for transfers between devices  8.69 us (18%)
  between operations  0.75 us (2%)
    pallas_call x1, Pallas kernels, power_of_orders(): pl.pallas_call(functools.partial(power_kernel, n_dev, vregs), out_shape=j...  10.5 us
    ppermute x5, waiting for transfers between devices, on_device(): other = lax.ppermute(power, axis, [(i, i ^ bit) for i in range(size)])  8.69 us
    ppermute x5, starting transfers between devices, on_device(): other = lax.ppermute(power, axis, [(i, i ^ bit) for i in range(size)])  8.42 us
    pallas_call x1, Pallas kernels, legendre_rows(): pl.pallas_call(functools.partial(recurrence_kernel, n_dev, vregs, float(2...  8.36 us
    all_to_all x1, starting transfers between devices, on_device(): lax.all_to_all(sent.reshape(n_dev, 2 * cycles, 2 * pairs), ('blk', 'mblk'...  7.3 us
    pallas_call x1, Pallas kernels, cycle_spectra(): pl.pallas_call(functools.partial(dft_kernel, n_dev, n_blk), out_shape=out...  2.39 us
  transfers between devices with their start and end apart: 6, of which 5 were waited for; matrix products, arithmetic and copies ran while one was open for 0% of the time, Pallas kernels for 18%

profile of v5, /device:TPU:0, one launch (start us, length us, event | category | flops | bytes accessed | tf_op | source)
XLA Modules:
  0.0 47.1 jit_solution(12805498671959580637)
XLA Ops:
  0.6 2.4 %cycle_dft.1 = f32[256,128]{1,0:T(8,128)} custom-call(s32[16]{0:T(128)} %ids_hbm.1, s32[16]{0:T(128)} %mask_hbm.1, f32[16,1024]{1,0:T(8,128)} %pix_hbm.1, bf16[128,96]{1,0:T(8,128)(2,1)} %constant.26.clone.first_hbm, f32[4,32,256]{2,1,0:T(8,128)} %constant.27.clone.turn_hbm, bf16[2,512,256]{2,1,0:T(8,128)(2,1)} %constant.28.clone.second_hbm, ...), custom_call_target="tpu_custom_call" | custom-call | tf_op jit(solution)/shard_map/cycle_dft/pallas_call | solution.py:174
  3.0 7.3 %all-to-all-start = ((f32[32,8,128]{2,1,0:T(8,128)}), f32[32,8,128]{2,1,0:T(8,128)S(1)}, u32[]{:S(2)}, u32[]{:S(2)}) async-start(f32[32,8,128]{2,1,0:T(8,128)} %bitcast.7), calls=%async_computation | async-start | bytes 262144 | tf_op jit(solution)/shard_map/all_to_all | solution.py:724
  10.3 0.0 copy-start
  10.4 0.0 copy-start.1
  10.4 0.0 copy-start.2
  10.4 0.0 copy-start.4
  10.4 8.4 %legendre_rows.1 = (f32[6784,128]{1,0:T(8,128)}, f32[24608,128]{1,0:T(8,128)}) custom-call(f32[4160,128]{1,0:T(8,128)} %constant.22.clone.rise_hbm, f32[4224,128]{1,0:T(8,128)} %constant.23.clone.low_hbm, f32[4224,128]{1,0:T(8,128)} %constant.24.clone.high_hbm, f32[3,16,128]{2,1,0:T(8,128)} %constant.25.clone.x_hbm.x_ref), custom_call_target="tpu_custom_call" | custom-call | flops 68157440 | bytes 25000000 | tf_op jit(solution)/shard_map/legendre_rows/pallas_call | solution.py:372
  18.8 0.0 all-to-all-done
  18.8 0.0 copy-done
  18.8 0.0 copy-done.1
  18.8 0.0 copy-done.2
  18.8 0.0 copy-done.4
  18.8 0.0 copy-start.3
  18.8 10.5 %order_power.1 = f32[32,128]{1,0:T(8,128)S(1)} custom-call(f32[6784,128]{1,0:T(8,128)} %get-tuple-element.6.rows_hbm, f32[24608,128]{1,0:T(8,128)} %get-tuple-element.7.u_hbm, f32[256,128]{1,0:T(8,128)S(1)} %bitcast.5, bf16[144,256]{1,0:T(8,128)(2,1)S(1)} %copy-done.1, f32[3,16,128]{2,1,0:T(8,128)S(1)} %copy-done, f32[128,128]{1,0:T(8,128)S(1)} %copy-done.2, ...), custom_call_target="tpu_custom_call" | custom-call | flops 12599296 | bytes 1000000 | tf_op jit(solution)/shard_map/order_power/pallas_call | solution.py:671
  29.3 0.3 collective-permute-start
  29.6 0.9 %collective-permute-done = f32[32,128]{1,0:T(8,128)S(1)} collective-permute-done((f32[32,128]{1,0:T(8,128)S(1)}, f32[32,128]{1,0:T(8,128)S(1)}, u32[]{:S(2)}, u32[]{:S(2)}) %collective-permute-start) | collective-permute-done | bytes 16416 | tf_op jit(solution)/shard_map/ppermute | solution.py:733
  30.6 1.8 %collective-permute-start.1 = (f32[32,128]{1,0:T(8,128)S(1)}, f32[32,128]{1,0:T(8,128)S(1)}, u32[]{:S(2)}, u32[]{:S(2)}) collective-permute-start(f32[32,128]{1,0:T(8,128)S(1)} %add.12), channel_id=1, source_target_pairs={{0,2},{1,3},{2,0},{3,1},{4,6},{5,7},{6,4},{7,5},{8,10},{9,11},{10,... | collective-permute-start | bytes 49160 | tf_op jit(solution)/shard_map/ppermute | solution.py:733
  32.4 1.9 %collective-permute-done.1 = f32[32,128]{1,0:T(8,128)S(1)} collective-permute-done((f32[32,128]{1,0:T(8,128)S(1)}, f32[32,128]{1,0:T(8,128)S(1)}, u32[]{:S(2)}, u32[]{:S(2)}) %collective-permute-start.1) | collective-permute-done | bytes 16416 | tf_op jit(solution)/shard_map/ppermute | solution.py:733
  34.3 1.8 %collective-permute-start.2 = (f32[32,128]{1,0:T(8,128)S(1)}, f32[32,128]{1,0:T(8,128)S(1)}, u32[]{:S(2)}, u32[]{:S(2)}) collective-permute-start(f32[32,128]{1,0:T(8,128)S(1)} %add.13), channel_id=1, source_target_pairs={{0,4},{1,5},{2,6},{3,7},{4,0},{5,1},{6,2},{7,3},{8,12},{9,13},{10,... | collective-permute-start | bytes 49160 | tf_op jit(solution)/shard_map/ppermute | solution.py:733
  36.1 1.9 %collective-permute-done.2 = f32[32,128]{1,0:T(8,128)S(1)} collective-permute-done((f32[32,128]{1,0:T(8,128)S(1)}, f32[32,128]{1,0:T(8,128)S(1)}, u32[]{:S(2)}, u32[]{:S(2)}) %collective-permute-start.2) | collective-permute-done | bytes 16416 | tf_op jit(solution)/shard_map/ppermute | solution.py:733
  38.1 2.7 %collective-permute-start.3 = (f32[32,128]{1,0:T(8,128)S(1)}, f32[32,128]{1,0:T(8,128)S(1)}, u32[]{:S(2)}, u32[]{:S(2)}) collective-permute-start(f32[32,128]{1,0:T(8,128)S(1)} %add.14), channel_id=1, source_target_pairs={{0,8},{1,9},{2,10},{3,11},{4,12},{5,13},{6,14},{7,15},{8,0},{9,1},... | collective-permute-start | bytes 49160 | tf_op jit(solution)/shard_map/ppermute | solution.py:733
  40.8 1.9 %collective-permute-done.3 = f32[32,128]{1,0:T(8,128)S(1)} collective-permute-done((f32[32,128]{1,0:T(8,128)S(1)}, f32[32,128]{1,0:T(8,128)S(1)}, u32[]{:S(2)}, u32[]{:S(2)}) %collective-permute-start.3) | collective-permute-done | bytes 16416 | tf_op jit(solution)/shard_map/ppermute | solution.py:733
  42.7 1.8 %collective-permute-start.4 = (f32[32,128]{1,0:T(8,128)S(1)}, f32[32,128]{1,0:T(8,128)S(1)}, u32[]{:S(2)}, u32[]{:S(2)}) collective-permute-start(f32[32,128]{1,0:T(8,128)S(1)} %add.15.own_ref), channel_id=1, source_target_pairs={{0,16},{16,0},{1,17},{17,1},{2,18},{18,2},{3,19},{19,3},{4,20},{20... | collective-permute-start | bytes 49160 | tf_op jit(solution)/shard_map/ppermute | solution.py:733
  44.5 2.0 %collective-permute-done.4.other_ref = f32[32,128]{1,0:T(8,128)S(1)} collective-permute-done((f32[32,128]{1,0:T(8,128)S(1)}, f32[32,128]{1,0:T(8,128)S(1)}, u32[]{:S(2)}, u32[]{:S(2)}) %collective-permute-start.4) | collective-permute-done | bytes 16416 | tf_op jit(solution)/shard_map/ppermute | solution.py:733
  46.4 0.0 copy-done.3
  46.4 0.6 %finish.1 = (f32[32,128]{1,0:T(8,128)}, f32[1,1]{1,0:T(1,128)}) custom-call(f32[32,128]{1,0:T(8,128)S(1)} %add.15.own_ref, f32[32,128]{1,0:T(8,128)S(1)} %collective-permute-done.4.other_ref, f32[32,128]{1,0:T(8,128)S(1)} %bitcast.6), custom_call_target="tpu_custom_call" | custom-call | tf_op jit(solution)/shard_map/finish/pallas_call | solution.py:702
  (4 shorter events, 0.0 us)
Async XLA Ops:
  3.0 15.7 %all-to-all-start = ((f32[32,8,128]{2,1,0:T(8,128)}), f32[32,8,128]{2,1,0:T(8,128)S(1)}, u32[]{:S(2)}, u32[]{:S(2)}) async-start(f32[32,8,128]{2,1,0:T(8,128)} %bitcast.7), calls=%async_computation | async-start | bytes 262144 | tf_op jit(solution)/shard_map/all_to_all | solution.py:724
  10.3 8.4 %copy-start = (f32[3,16,128]{2,1,0:T(8,128)S(1)}, f32[3,16,128]{2,1,0:T(8,128)}, u32[]{:S(2)}) copy-start(f32[3,16,128]{2,1,0:T(8,128)} %constant.25.clone.x_hbm.x_ref) | copy-start | bytes 73732
  10.4 8.4 %copy-start.1 = (bf16[144,256]{1,0:T(8,128)(2,1)S(1)}, bf16[144,256]{1,0:T(8,128)(2,1)}, u32[]{:S(2)}) copy-start(bf16[144,256]{1,0:T(8,128)(2,1)} %constant.30.clone.pick_ref) | copy-start | bytes 221188
  10.4 8.4 %copy-start.2 = (f32[128,128]{1,0:T(8,128)S(1)}, f32[128,128]{1,0:T(8,128)}, u32[]{:S(2)}) copy-start(f32[128,128]{1,0:T(8,128)} %constant.31.clone.spread_ref) | copy-start | bytes 196612
  10.4 8.4 %copy-start.4 = (bf16[32,128]{1,0:T(8,128)(2,1)S(1)}, bf16[32,128]{1,0:T(8,128)(2,1)}, u32[]{:S(2)}) copy-start(bf16[32,128]{1,0:T(8,128)(2,1)} %constant.32.clone.gather_ref) | copy-start | bytes 24580
  18.8 27.6 %copy-start.3 = (f32[4096]{0:T(1024)S(1)}, f32[4096]{0:T(1024)}, u32[]{:S(2)}) copy-start(f32[4096]{0:T(1024)} %param.19) | copy-start | bytes 49156
  29.3 1.2 %collective-permute-start = (f32[32,128]{1,0:T(8,128)S(1)}, f32[32,128]{1,0:T(8,128)S(1)}, u32[]{:S(2)}, u32[]{:S(2)}) collective-permute-start(f32[32,128]{1,0:T(8,128)S(1)} %order_power.1), channel_id=1, source_target_pairs={{0,1},{1,0},{2,3},{3,2},{4,5},{5,4},{6,7},{7,6},{8,9},{9,8},{10,11... | collective-permute-start | bytes 49160 | tf_op jit(solution)/shard_map/ppermute | solution.py:733
  30.6 3.7 %collective-permute-start.1 = (f32[32,128]{1,0:T(8,128)S(1)}, f32[32,128]{1,0:T(8,128)S(1)}, u32[]{:S(2)}, u32[]{:S(2)}) collective-permute-start(f32[32,128]{1,0:T(8,128)S(1)} %add.12), channel_id=1, source_target_pairs={{0,2},{1,3},{2,0},{3,1},{4,6},{5,7},{6,4},{7,5},{8,10},{9,11},{10,... | collective-permute-start | bytes 49160 | tf_op jit(solution)/shard_map/ppermute | solution.py:733
  34.3 3.7 %collective-permute-start.2 = (f32[32,128]{1,0:T(8,128)S(1)}, f32[32,128]{1,0:T(8,128)S(1)}, u32[]{:S(2)}, u32[]{:S(2)}) collective-permute-start(f32[32,128]{1,0:T(8,128)S(1)} %add.13), channel_id=1, source_target_pairs={{0,4},{1,5},{2,6},{3,7},{4,0},{5,1},{6,2},{7,3},{8,12},{9,13},{10,... | collective-permute-start | bytes 49160 | tf_op jit(solution)/shard_map/ppermute | solution.py:733
  38.1 4.6 %collective-permute-start.3 = (f32[32,128]{1,0:T(8,128)S(1)}, f32[32,128]{1,0:T(8,128)S(1)}, u32[]{:S(2)}, u32[]{:S(2)}) collective-permute-start(f32[32,128]{1,0:T(8,128)S(1)} %add.14), channel_id=1, source_target_pairs={{0,8},{1,9},{2,10},{3,11},{4,12},{5,13},{6,14},{7,15},{8,0},{9,1},... | collective-permute-start | bytes 49160 | tf_op jit(solution)/shard_map/ppermute | solution.py:733
  42.7 3.7 %collective-permute-start.4 = (f32[32,128]{1,0:T(8,128)S(1)}, f32[32,128]{1,0:T(8,128)S(1)}, u32[]{:S(2)}, u32[]{:S(2)}) collective-permute-start(f32[32,128]{1,0:T(8,128)S(1)} %add.15.own_ref), channel_id=1, source_target_pairs={{0,16},{16,0},{1,17},{17,1},{2,18},{18,2},{3,19},{19,3},{4,20},{20... | collective-permute-start | bytes 49160 | tf_op jit(solution)/shard_map/ppermute | solution.py:733

commit v6 on v5

--- a/solution.py
+++ b/solution.py
@@ -689,8 +689,23 @@
     )(rows, u, got, *tables)
 
 
-def finish_kernel(own_ref, other_ref, model_ref, cl_ref, misfit_ref):
-    cl = own_ref[...] + other_ref[...]
+def tree_sum(parts):
+    while len(parts) > 1:
+        parts = [a + b for a, b in zip(parts[::2], parts[1::2])]
+    return parts[0]
+
+
+def exchange(value, bits, n_dev):
+    parts = [value]
+    for chosen in range(1, 1 << len(bits)):
+        flip = sum(bit for i, bit in enumerate(bits) if chosen >> i & 1)
+        parts.append(lax.ppermute(value, ("blk", "mblk"), [(i, i ^ flip) for i in range(n_dev)]))
+    return parts
+
+
+def finish_kernel(*refs):
+    *part_refs, model_ref, cl_ref, misfit_ref = refs
+    cl = tree_sum([ref[...] for ref in part_refs])
     model = model_ref[...]
     cl_ref[...] = cl
     error = (cl - model) / model
@@ -698,15 +713,16 @@
     misfit_ref[...] = jnp.sum(squares, axis=1, keepdims=True) * (1.0 / LMAX)
 
 
-def finish(own, other, model_cl):
+def finish(parts, model_cl):
+    shape = parts[0].shape
     cl, misfit = pl.pallas_call(
         finish_kernel,
-        out_shape=(jax.ShapeDtypeStruct(own.shape, F32), jax.ShapeDtypeStruct((1, 1), F32)),
-        in_specs=[VMEM] * 3,
+        out_shape=(jax.ShapeDtypeStruct(shape, F32), jax.ShapeDtypeStruct((1, 1), F32)),
+        in_specs=[VMEM] * (len(parts) + 1),
         out_specs=(VMEM, VMEM),
         compiler_params=pltpu.CompilerParams(vmem_limit_bytes=2 * 1024 * 1024),
         name="finish",
-    )(own, other, model_cl.reshape(own.shape))
+    )(*parts, model_cl.reshape(shape))
     return cl.reshape(LMAX), misfit.reshape(())
 
 
@@ -725,14 +741,17 @@
     got = got.reshape(n_dev * 2 * cycles, 2 * pairs)
     power = power_of_orders(rows, u, got, n_dev, n_blk, lats, slots)
 
-    other = jnp.zeros_like(power)
-    for axis, size in (("mblk", n_mblk), ("blk", n_blk)):
-        bit = 1
-        while bit < size:
-            power = power + other
-            other = lax.ppermute(power, axis, [(i, i ^ bit) for i in range(size)])
-            bit *= 2
-    return finish(power, other, model_cl)
+    inner = [1 << i for i in range(n_mblk.bit_length() - 1)]
+    outer = [n_mblk << i for i in range(n_blk.bit_length() - 1)]
+    rounds = [inner[-1:], inner[-2:-1] + outer]
+    inner = inner[:-2]
+    while inner:
+        rounds.append(inner[-2:])
+        inner = inner[:-2]
+    parts = [power]
+    for bits in rounds:
+        parts = exchange(tree_sum(parts), bits, n_dev)
+    return finish(parts, model_cl)
 
 
 def solution(mesh):

time: 47.3 us -> 45.8 us (0.968)
  waiting for transfers between devices: 8.69 us -> 7.44 us
    ppermute x5 -> x7, waiting for transfers between devices: 8.69 us -> 7.44 us  [exchange(): lax.ppermute(value, ('blk', 'mblk'), [(i, i ^ flip) for i in range(n_dev)])]
    ppermute x5 -> x7, starting transfers between devices: 8.42 us -> 8.16 us  [exchange(): lax.ppermute(value, ('blk', 'mblk'), [(i, i ^ flip) for i in range(n_dev)])]
  transfers between devices with their start and end apart: 6 -> 8, of which waited for: 5 -> 6; matrix products, arithmetic and copies ran while one was open for 0% -> 0% of each run, Pallas kernels for 18% -> 18%
where the time goes in v6:
time: 45.8 us; the launch traced here: 45.6 us
  Pallas kernels  21.9 us (48%)
  starting transfers between devices  15.5 us (34%)
  waiting for transfers between devices  7.44 us (16%)
  between operations  0.76 us (2%)
    pallas_call x1, Pallas kernels, power_of_orders(): pl.pallas_call(functools.partial(power_kernel, n_dev, vregs), out_shape=j...  10.5 us
    pallas_call x1, Pallas kernels, legendre_rows(): pl.pallas_call(functools.partial(recurrence_kernel, n_dev, vregs, float(2...  8.37 us
    ppermute x7, starting transfers between devices, exchange(): lax.ppermute(value, ('blk', 'mblk'), [(i, i ^ flip) for i in range(n_dev)])  8.16 us
    ppermute x7, waiting for transfers between devices, exchange(): lax.ppermute(value, ('blk', 'mblk'), [(i, i ^ flip) for i in range(n_dev)])  7.44 us
    all_to_all x1, starting transfers between devices, on_device(): lax.all_to_all(sent.reshape(n_dev, 2 * cycles, 2 * pairs), ('blk', 'mblk'...  7.3 us
    pallas_call x1, Pallas kernels, cycle_spectra(): pl.pallas_call(functools.partial(dft_kernel, n_dev, n_blk), out_shape=out...  2.4 us
  transfers between devices with their start and end apart: 8, of which 6 were waited for; matrix products, arithmetic and copies ran while one was open for 0% of the time, Pallas kernels for 18%

profile of v6, /device:TPU:0, one launch (start us, length us, event | category | flops | bytes accessed | tf_op | source)
XLA Modules:
  0.0 45.6 jit_solution(15835557400955377554)
XLA Ops:
  0.6 2.4 %cycle_dft.1 = f32[256,128]{1,0:T(8,128)} custom-call(s32[16]{0:T(128)} %ids_hbm.1, s32[16]{0:T(128)} %mask_hbm.1, f32[16,1024]{1,0:T(8,128)} %pix_hbm.1, bf16[128,96]{1,0:T(8,128)(2,1)} %constant.26.clone.first_hbm, f32[4,32,256]{2,1,0:T(8,128)} %constant.27.clone.turn_hbm, bf16[2,512,256]{2,1,0:T(8,128)(2,1)} %constant.28.clone.second_hbm, ...), custom_call_target="tpu_custom_call" | custom-call | tf_op jit(solution)/shard_map/cycle_dft/pallas_call | solution.py:174
  3.0 7.3 %all-to-all-start = ((f32[32,8,128]{2,1,0:T(8,128)}), f32[32,8,128]{2,1,0:T(8,128)S(1)}, u32[]{:S(2)}, u32[]{:S(2)}) async-start(f32[32,8,128]{2,1,0:T(8,128)} %bitcast.7), calls=%async_computation | async-start | bytes 262144 | tf_op jit(solution)/shard_map/all_to_all | solution.py:740
  10.4 0.0 copy-start
  10.4 0.0 copy-start.1
  10.4 0.0 copy-start.2
  10.4 0.0 copy-start.4
  10.4 8.4 %legendre_rows.1 = (f32[6784,128]{1,0:T(8,128)}, f32[24608,128]{1,0:T(8,128)}) custom-call(f32[4160,128]{1,0:T(8,128)} %constant.22.clone.rise_hbm, f32[4224,128]{1,0:T(8,128)} %constant.23.clone.low_hbm, f32[4224,128]{1,0:T(8,128)} %constant.24.clone.high_hbm, f32[3,16,128]{2,1,0:T(8,128)} %constant.25.clone.x_hbm.x_ref), custom_call_target="tpu_custom_call" | custom-call | flops 68157440 | bytes 25000000 | tf_op jit(solution)/shard_map/legendre_rows/pallas_call | solution.py:372
  18.8 0.0 all-to-all-done
  18.8 0.0 copy-done
  18.8 0.0 copy-done.1
  18.8 0.0 copy-done.2
  18.8 0.0 copy-done.4
  18.8 0.0 copy-start.3
  18.8 10.5 %order_power.1 = f32[32,128]{1,0:T(8,128)S(1)} custom-call(f32[6784,128]{1,0:T(8,128)} %get-tuple-element.6.rows_hbm, f32[24608,128]{1,0:T(8,128)} %get-tuple-element.7.u_hbm, f32[256,128]{1,0:T(8,128)S(1)} %bitcast.5, bf16[144,256]{1,0:T(8,128)(2,1)S(1)} %copy-done.1, f32[3,16,128]{2,1,0:T(8,128)S(1)} %copy-done, f32[128,128]{1,0:T(8,128)S(1)} %copy-done.2, ...), custom_call_target="tpu_custom_call" | custom-call | flops 12599296 | bytes 1000000 | tf_op jit(solution)/shard_map/order_power/pallas_call | solution.py:671
  29.3 2.8 %collective-permute-start = (f32[32,128]{1,0:T(8,128)S(1)}, f32[32,128]{1,0:T(8,128)S(1)}, u32[]{:S(2)}, u32[]{:S(2)}) collective-permute-start(f32[32,128]{1,0:T(8,128)S(1)} %order_power.1), channel_id=1, source_target_pairs={{0,8},{1,9},{2,10},{3,11},{4,12},{5,13},{6,14},{7,15},{8,0},{9,1},... | collective-permute-start | bytes 49160 | tf_op jit(solution)/shard_map/ppermute | solution.py:702
  32.1 1.9 %collective-permute-done = f32[32,128]{1,0:T(8,128)S(1)} collective-permute-done((f32[32,128]{1,0:T(8,128)S(1)}, f32[32,128]{1,0:T(8,128)S(1)}, u32[]{:S(2)}, u32[]{:S(2)}) %collective-permute-start) | collective-permute-done | bytes 16416 | tf_op jit(solution)/shard_map/ppermute | solution.py:702
  34.0 2.7 %collective-permute-start.3 = (f32[32,128]{1,0:T(8,128)S(1)}, f32[32,128]{1,0:T(8,128)S(1)}, u32[]{:S(2)}, u32[]{:S(2)}) collective-permute-start(f32[32,128]{1,0:T(8,128)S(1)} %add.12), channel_id=1, source_target_pairs={{0,20},{1,21},{2,22},{3,23},{4,16},{5,17},{6,18},{7,19},{8,28},{9,... | collective-permute-start | bytes 49160 | tf_op jit(solution)/shard_map/ppermute | solution.py:702
  36.8 0.6 %collective-permute-start.2 = (f32[32,128]{1,0:T(8,128)S(1)}, f32[32,128]{1,0:T(8,128)S(1)}, u32[]{:S(2)}, u32[]{:S(2)}) collective-permute-start(f32[32,128]{1,0:T(8,128)S(1)} %add.12), channel_id=1, source_target_pairs={{0,16},{1,17},{2,18},{3,19},{4,20},{5,21},{6,22},{7,23},{8,24},{9,... | collective-permute-start | bytes 49160 | tf_op jit(solution)/shard_map/ppermute | solution.py:702
  37.3 0.2 collective-permute-start.1
  37.5 1.1 %collective-permute-done.3 = f32[32,128]{1,0:T(8,128)S(1)} collective-permute-done((f32[32,128]{1,0:T(8,128)S(1)}, f32[32,128]{1,0:T(8,128)S(1)}, u32[]{:S(2)}, u32[]{:S(2)}) %collective-permute-start.3) | collective-permute-done | bytes 16416 | tf_op jit(solution)/shard_map/ppermute | solution.py:702
  38.7 1.8 %collective-permute-done.2 = f32[32,128]{1,0:T(8,128)S(1)} collective-permute-done((f32[32,128]{1,0:T(8,128)S(1)}, f32[32,128]{1,0:T(8,128)S(1)}, u32[]{:S(2)}, u32[]{:S(2)}) %collective-permute-start.2) | collective-permute-done | bytes 16416 | tf_op jit(solution)/shard_map/ppermute | solution.py:702
  40.5 0.6 %collective-permute-done.1 = f32[32,128]{1,0:T(8,128)S(1)} collective-permute-done((f32[32,128]{1,0:T(8,128)S(1)}, f32[32,128]{1,0:T(8,128)S(1)}, u32[]{:S(2)}, u32[]{:S(2)}) %collective-permute-start.1) | collective-permute-done | bytes 16416 | tf_op jit(solution)/shard_map/ppermute | solution.py:702
  41.1 0.1 collective-permute-start.6
  41.2 1.5 %collective-permute-start.5 = (f32[32,128]{1,0:T(8,128)S(1)}, f32[32,128]{1,0:T(8,128)S(1)}, u32[]{:S(2)}, u32[]{:S(2)}) collective-permute-start(f32[32,128]{1,0:T(8,128)S(1)} %add_add_fusion.refs_0_), channel_id=1, source_target_pairs={{0,2},{1,3},{2,0},{3,1},{4,6},{5,7},{6,4},{7,5},{8,10},{9,11},{10,... | collective-permute-start | bytes 49160 | tf_op jit(solution)/shard_map/ppermute | solution.py:702
  42.7 0.3 collective-permute-start.4
  43.0 1.4 %collective-permute-done.6.refs_3_ = f32[32,128]{1,0:T(8,128)S(1)} collective-permute-done((f32[32,128]{1,0:T(8,128)S(1)}, f32[32,128]{1,0:T(8,128)S(1)}, u32[]{:S(2)}, u32[]{:S(2)}) %collective-permute-start.6) | collective-permute-done | bytes 16416 | tf_op jit(solution)/shard_map/ppermute | solution.py:702
  44.5 0.5 %collective-permute-done.5.refs_2_ = f32[32,128]{1,0:T(8,128)S(1)} collective-permute-done((f32[32,128]{1,0:T(8,128)S(1)}, f32[32,128]{1,0:T(8,128)S(1)}, u32[]{:S(2)}, u32[]{:S(2)}) %collective-permute-start.5) | collective-permute-done | bytes 16416 | tf_op jit(solution)/shard_map/ppermute | solution.py:702
  45.0 0.0 collective-permute-done.4.refs_1_
  45.0 0.0 copy-done.3
  45.0 0.6 %finish.1 = (f32[32,128]{1,0:T(8,128)}, f32[1,1]{1,0:T(1,128)}) custom-call(f32[32,128]{1,0:T(8,128)S(1)} %add_add_fusion.refs_0_, f32[32,128]{1,0:T(8,128)S(1)} %collective-permute-done.4.refs_1_, f32[32,128]{1,0:T(8,128)S(1)} %collective-permute-done.5.refs_2_, f32[32,128]{1,0:T(8,128)S(1)} %collective-permute-done.6.refs_3_, f32[32,128]{1,0:T(8,128)S(1)} %bitcast.6), custom_call_target="tpu_custom_call" | custom-call | tf_op jit(solution)/shard_map/finish/pallas_call | solution.py:718
  (2 shorter events, 0.0 us)
Async XLA Ops:
  3.0 15.7 %all-to-all-start = ((f32[32,8,128]{2,1,0:T(8,128)}), f32[32,8,128]{2,1,0:T(8,128)S(1)}, u32[]{:S(2)}, u32[]{:S(2)}) async-start(f32[32,8,128]{2,1,0:T(8,128)} %bitcast.7), calls=%async_computation | async-start | bytes 262144 | tf_op jit(solution)/shard_map/all_to_all | solution.py:740
  10.4 8.4 %copy-start = (f32[3,16,128]{2,1,0:T(8,128)S(1)}, f32[3,16,128]{2,1,0:T(8,128)}, u32[]{:S(2)}) copy-start(f32[3,16,128]{2,1,0:T(8,128)} %constant.25.clone.x_hbm.x_ref) | copy-start | bytes 73732
  10.4 8.4 %copy-start.1 = (bf16[144,256]{1,0:T(8,128)(2,1)S(1)}, bf16[144,256]{1,0:T(8,128)(2,1)}, u32[]{:S(2)}) copy-start(bf16[144,256]{1,0:T(8,128)(2,1)} %constant.30.clone.pick_ref) | copy-start | bytes 221188
  10.4 8.4 %copy-start.2 = (f32[128,128]{1,0:T(8,128)S(1)}, f32[128,128]{1,0:T(8,128)}, u32[]{:S(2)}) copy-start(f32[128,128]{1,0:T(8,128)} %constant.31.clone.spread_ref) | copy-start | bytes 196612
  10.4 8.4 %copy-start.4 = (bf16[32,128]{1,0:T(8,128)(2,1)S(1)}, bf16[32,128]{1,0:T(8,128)(2,1)}, u32[]{:S(2)}) copy-start(bf16[32,128]{1,0:T(8,128)(2,1)} %constant.32.clone.gather_ref) | copy-start | bytes 24580
  18.8 26.1 %copy-start.3 = (f32[4096]{0:T(1024)S(1)}, f32[4096]{0:T(1024)}, u32[]{:S(2)}) copy-start(f32[4096]{0:T(1024)} %param.19) | copy-start | bytes 49156
  29.3 4.7 %collective-permute-start = (f32[32,128]{1,0:T(8,128)S(1)}, f32[32,128]{1,0:T(8,128)S(1)}, u32[]{:S(2)}, u32[]{:S(2)}) collective-permute-start(f32[32,128]{1,0:T(8,128)S(1)} %order_power.1), channel_id=1, source_target_pairs={{0,8},{1,9},{2,10},{3,11},{4,12},{5,13},{6,14},{7,15},{8,0},{9,1},... | collective-permute-start | bytes 49160 | tf_op jit(solution)/shard_map/ppermute | solution.py:702
  34.0 4.6 %collective-permute-start.3 = (f32[32,128]{1,0:T(8,128)S(1)}, f32[32,128]{1,0:T(8,128)S(1)}, u32[]{:S(2)}, u32[]{:S(2)}) collective-permute-start(f32[32,128]{1,0:T(8,128)S(1)} %add.12), channel_id=1, source_target_pairs={{0,20},{1,21},{2,22},{3,23},{4,16},{5,17},{6,18},{7,19},{8,28},{9,... | collective-permute-start | bytes 49160 | tf_op jit(solution)/shard_map/ppermute | solution.py:702
  36.8 3.7 %collective-permute-start.2 = (f32[32,128]{1,0:T(8,128)S(1)}, f32[32,128]{1,0:T(8,128)S(1)}, u32[]{:S(2)}, u32[]{:S(2)}) collective-permute-start(f32[32,128]{1,0:T(8,128)S(1)} %add.12), channel_id=1, source_target_pairs={{0,16},{1,17},{2,18},{3,19},{4,20},{5,21},{6,22},{7,23},{8,24},{9,... | collective-permute-start | bytes 49160 | tf_op jit(solution)/shard_map/ppermute | solution.py:702
  37.3 3.7 %collective-permute-start.1 = (f32[32,128]{1,0:T(8,128)S(1)}, f32[32,128]{1,0:T(8,128)S(1)}, u32[]{:S(2)}, u32[]{:S(2)}) collective-permute-start(f32[32,128]{1,0:T(8,128)S(1)} %add.12), channel_id=1, source_target_pairs={{0,4},{1,5},{2,6},{3,7},{4,0},{5,1},{6,2},{7,3},{8,12},{9,13},{10,... | collective-permute-start | bytes 49160 | tf_op jit(solution)/shard_map/ppermute | solution.py:702
  41.1 3.4 %collective-permute-start.6 = (f32[32,128]{1,0:T(8,128)S(1)}, f32[32,128]{1,0:T(8,128)S(1)}, u32[]{:S(2)}, u32[]{:S(2)}) collective-permute-start(f32[32,128]{1,0:T(8,128)S(1)} %add_add_fusion.refs_0_), channel_id=1, source_target_pairs={{0,3},{1,2},{2,1},{3,0},{4,7},{5,6},{6,5},{7,4},{8,11},{9,10},{10,... | collective-permute-start | bytes 49160 | tf_op jit(solution)/shard_map/ppermute | solution.py:702
  41.2 3.8 %collective-permute-start.5 = (f32[32,128]{1,0:T(8,128)S(1)}, f32[32,128]{1,0:T(8,128)S(1)}, u32[]{:S(2)}, u32[]{:S(2)}) collective-permute-start(f32[32,128]{1,0:T(8,128)S(1)} %add_add_fusion.refs_0_), channel_id=1, source_target_pairs={{0,2},{1,3},{2,0},{3,1},{4,6},{5,7},{6,4},{7,5},{8,10},{9,11},{10,... | collective-permute-start | bytes 49160 | tf_op jit(solution)/shard_map/ppermute | solution.py:702
  42.7 2.3 %collective-permute-start.4 = (f32[32,128]{1,0:T(8,128)S(1)}, f32[32,128]{1,0:T(8,128)S(1)}, u32[]{:S(2)}, u32[]{:S(2)}) collective-permute-start(f32[32,128]{1,0:T(8,128)S(1)} %add_add_fusion.refs_0_), channel_id=1, source_target_pairs={{0,1},{1,0},{2,3},{3,2},{4,5},{5,4},{6,7},{7,6},{8,9},{9,8},{10,11... | collective-permute-start | bytes 49160 | tf_op jit(solution)/shard_map/ppermute | solution.py:702
